TPU v7x, 128 devices: a whole 4x4x4 slice. The times are simulated.
128 devices in a mesh: tm: 16 (over y_lo, x, core), height: 8 (over z, y_hi).
Axes of the slice: x: 4, y: 4 (y_hi: 2, y_lo: 2; y = y_hi * 2 + y_lo), z: 4, core: 2. Of those that a mesh axis runs over, the one named last changes fastest.
Arguments:
- query_band: bfloat16 [48, 24, 24, 2048], P('tm', 'height'), may hold values from -4.5 to 4.5
- key_band: bfloat16 [48, 24, 24, 2048], P('tm', 'height'), may hold values from -11 to 11
- value_band: bfloat16 [48, 24, 24, 2048], P('tm', 'height'), may hold values from -6 to 6
Outputs:
- attended: bfloat16 [48, 24, 24, 2048], P('tm', 'height')
All inputs are finite; a program needn't handle non-finite values.
Results may differ from a plain program's by a relative error of at most 0.0033.
Values may be sent and summed in bfloat16 or wider, within the bound.
No kernel may reach another device: no remote copies, remote signals or barrier semaphores. Data moves between devices by JAX's collectives and lax.ppermute only.
A program may use at most 128 MiB of HBM per device.

v0:
```python
import jax
import jax.numpy as jnp
from jax import lax
from jax.sharding import PartitionSpec as P

HEAD_DIM = 128
TILE_T = 6
TILE_H = 8
TILE_W = 8


def from_behind(value, axis, steps):
    count = lax.axis_size(axis)
    leading, last = (max(0, -steps), min(count, count - steps))
    return lax.ppermute(value, axis, [(source, source + steps) for source in range(leading, last)])


def attend_plane(queries, window, time_ok):
    part_frames, rows_all, cols_all, local_features = queries.shape
    local_heads = local_features // HEAD_DIM
    window_frames = window.shape[1]
    key_count = window_frames * rows_all * cols_all
    head_window = jnp.transpose(window.reshape(2, key_count, local_heads, HEAD_DIM), (0, 2, 1, 3))
    key_rows = head_window[0]
    value_rows = head_window[1]
    head_queries = jnp.transpose(
        queries.reshape(part_frames, rows_all, cols_all, local_heads, HEAD_DIM), (3, 0, 1, 2, 4)
    )
    frame_tile = jnp.arange(window_frames, dtype=jnp.int32) // TILE_T
    row_tile = jnp.arange(rows_all, dtype=jnp.int32) // TILE_H
    col_tile = jnp.arange(cols_all, dtype=jnp.int32) // TILE_W
    grid_shape = (window_frames, rows_all, cols_all)
    key_time = jnp.broadcast_to(time_ok[frame_tile][:, None, None], grid_shape).reshape(-1)
    key_row = jnp.broadcast_to(row_tile[None, :, None], grid_shape).reshape(-1)
    key_col = jnp.broadcast_to(col_tile[None, None, :], grid_shape).reshape(-1)
    row_count = rows_all // TILE_H
    col_count = cols_all // TILE_W
    zero_index = jnp.zeros((), jnp.int32)
    query_count = part_frames * TILE_H * TILE_W

    def one_tile(tile_id):
        row_index = tile_id // col_count
        col_index = tile_id % col_count
        query_block = lax.dynamic_slice(
            head_queries,
            (zero_index, zero_index, row_index * TILE_H, col_index * TILE_W, zero_index),
            (local_heads, part_frames, TILE_H, TILE_W, HEAD_DIM),
        ).reshape(local_heads, query_count, HEAD_DIM)
        usable = (
            key_time & (jnp.abs(key_row - row_index) <= 1) & (jnp.abs(key_col - col_index) <= 1)
        )
        scores = jnp.einsum(
            "hqd,hkd->hqk", query_block, key_rows, preferred_element_type=jnp.float32
        ) * HEAD_DIM ** (-0.5)
        scores = jnp.where(usable[None, None, :], scores, jnp.float32(-1e30))
        largest = jnp.max(scores, axis=2, keepdims=True)
        weights = lax.optimization_barrier(jnp.exp(scores - largest).astype(jnp.bfloat16))
        weight_sum = jnp.sum(weights.astype(jnp.float32), axis=2, keepdims=True)
        summed = jnp.einsum("hqk,hkd->hqd", weights, value_rows, preferred_element_type=jnp.float32)
        return (summed / weight_sum).astype(jnp.bfloat16)

    tile_outputs = lax.map(one_tile, jnp.arange(row_count * col_count, dtype=jnp.int32))
    tile_outputs = tile_outputs.reshape(
        row_count, col_count, local_heads, part_frames, TILE_H, TILE_W, HEAD_DIM
    )
    return jnp.transpose(tile_outputs, (3, 0, 4, 1, 5, 2, 6)).reshape(
        part_frames, rows_all, cols_all, local_features
    )


def body(query_band, key_band, value_band):
    parity = lax.axis_index("tm") % 2
    relaid = (
        lax.all_to_all(query_band, "height", split_axis=3, concat_axis=1, tiled=True),
        lax.all_to_all(key_band, "height", split_axis=3, concat_axis=1, tiled=True),
        lax.all_to_all(value_band, "height", split_axis=3, concat_axis=1, tiled=True),
    )
    queries = relaid[0]
    pair_local = jnp.stack([relaid[1], relaid[2]])
    part_frames = pair_local.shape[1]
    pieces = []
    for step_by in (3, 2, 1, 0, -1, -2, -3):
        if step_by == 0:
            pieces.append(pair_local)
        else:
            pieces.append(from_behind(pair_local, "tm", step_by))
    spread = jnp.concatenate(pieces, axis=1)
    window = lax.dynamic_slice_in_dim(spread, (1 - parity) * part_frames, 3 * TILE_T, 1)
    time_index = lax.axis_index("tm") // 2
    time_tiles = lax.axis_size("tm") // 2
    offsets = jnp.arange(3, dtype=jnp.int32) - 1
    time_ok = (time_index + offsets >= 0) & (time_index + offsets < time_tiles)
    attended_heads = attend_plane(queries, window, time_ok)
    return lax.all_to_all(attended_heads, "height", split_axis=1, concat_axis=3, tiled=True)


def solution(mesh):
    return jax.shard_map(
        body,
        mesh=mesh,
        in_specs=(
            P("tm", "height", None, None),
            P("tm", "height", None, None),
            P("tm", "height", None, None),
        ),
        out_specs=P("tm", "height", None, None),
        check_vma=False,
    )
```

profile of v0, /device:TPU:14, one launch (start us, length us, event | category | flops | bytes accessed | tf_op | source)
XLA Modules:
  0.0 468.4 jit_solution(16043558170980023195)
XLA Ops:
  0.0 9.4 %copy.21 = bf16[3,3,24,2048]{2,1,0,3:T(4,128)(2,1)} copy(bf16[3,3,24,2048]{3,2,1,0:T(8,128)(2,1)} %param.7) | data formatting | bytes 1769472 | tf_op args[2]
  9.4 9.4 %reshape.173 = bf16[8,2,27648]{2,1,0:T(2,128)(2,1)} reshape(bf16[2048,3,3,24]{3,2,1,0:T(4,128)(2,1)} %bitcast.76) | data formatting | bytes 1769472
  18.8 7.0 %all-to-all-start.2 = ((bf16[8,2,27648]{2,1,0:T(2,128)(2,1)}), bf16[8,2,27648]{2,1,0:T(2,128)(2,1)S(1)}, u32[]{:S(2)}, u32[]{:S(2)}) async-start(bf16[8,2,27648]{2,1,0:T(2,128)(2,1)} %reshape.173), calls=%async_computation.2 | async-start | bytes 1769472 | tf_op jit(solution)/shard_map/all_to_all | solution.py:76
  25.9 7.0 %copy.18 = bf16[3,3,24,2048]{2,1,0,3:T(4,128)(2,1)} copy(bf16[3,3,24,2048]{3,2,1,0:T(8,128)(2,1)S(1)} %copy-done) | data formatting | bytes 1769472 | tf_op args[1]
  32.9 9.4 %reshape.175 = bf16[8,2,27648]{2,1,0:T(2,128)(2,1)} reshape(bf16[2048,3,3,24]{3,2,1,0:T(4,128)(2,1)} %bitcast.77) | data formatting | bytes 1769472
  42.3 7.2 %all-to-all-start.1 = ((bf16[8,2,27648]{2,1,0:T(2,128)(2,1)}), bf16[8,2,27648]{2,1,0:T(2,128)(2,1)S(1)}, u32[]{:S(2)}, u32[]{:S(2)}) async-start(bf16[8,2,27648]{2,1,0:T(2,128)(2,1)} %reshape.175), calls=%async_computation.1 | async-start | bytes 1769472 | tf_op jit(solution)/shard_map/all_to_all | solution.py:75
  49.5 7.9 %reshape.174 = bf16[2048,3,3,24]{3,2,1,0:T(4,128)(2,1)} reshape(bf16[8,2,27648]{2,1,0:T(2,128)(2,1)S(1)} %all-to-all-done.2) | data formatting | bytes 1769472
  57.4 7.6 %copy.34 = bf16[3,3,24,8,256]{4,2,1,3,0:T(8,128)(2,1)S(1)} copy(bf16[3,3,24,8,256]{2,1,0,4,3:T(4,128)(2,1)} %bitcast.73) | data formatting | bytes 1769472 | tf_op jit(solution)/shard_map/all_to_all | solution.py:76
  65.1 7.9 %reshape.176 = bf16[2048,3,3,24]{3,2,1,0:T(4,128)(2,1)} reshape(bf16[8,2,27648]{2,1,0:T(2,128)(2,1)S(1)} %all-to-all-done.1) | data formatting | bytes 1769472
  72.9 7.6 %copy.32 = bf16[3,3,24,8,256]{4,2,1,3,0:T(8,128)(2,1)S(1)} copy(bf16[3,3,24,8,256]{2,1,0,4,3:T(4,128)(2,1)} %bitcast.74) | data formatting | bytes 1769472 | tf_op jit(solution)/shard_map/all_to_all | solution.py:75
  90.1 5.9 %collective-permute-start.4 = (bf16[2,3,24,24,256]{4,3,2,1,0:T(8,128)(2,1)}, bf16[2,3,24,24,256]{4,3,2,1,0:T(8,128)(2,1)}, u32[]{:S(2)}, u32[]{:S(2)}) collective-permute-start(bf16[2,3,24,24,256]{4,3,2,1,0:T(8,128)(2,1)} %pad_maximum_fusion), channel_id=1, source_target_pairs={{16,0},{24,8},{32,16},{40,24},{48,32},{56,40},{64,48},{72,56},{80,... | collective-permute-start | bytes 5308424 | tf_op jit(solution)/shard_map/ppermute | solution.py:15
  96.0 22.7 %collective-permute-done = bf16[2,3,24,24,256]{4,3,2,1,0:T(8,128)(2,1)} collective-permute-done((bf16[2,3,24,24,256]{4,3,2,1,0:T(8,128)(2,1)}, bf16[2,3,24,24,256]{4,3,2,1,0:T(8,128)(2,1)}, u32[]{:S(2)}, u32[]{:S(2)}) %collective-permute-start) | collective-permute-done | bytes 1769504 | tf_op jit(solution)/shard_map/ppermute | solution.py:15
  118.7 7.2 %collective-permute-start.5 = (bf16[2,3,24,24,256]{4,3,2,1,0:T(8,128)(2,1)}, bf16[2,3,24,24,256]{4,3,2,1,0:T(8,128)(2,1)}, u32[]{:S(2)}, u32[]{:S(2)}) collective-permute-start(bf16[2,3,24,24,256]{4,3,2,1,0:T(8,128)(2,1)} %pad_maximum_fusion), channel_id=1, source_target_pairs={{24,0},{32,8},{40,16},{48,24},{56,32},{64,40},{72,48},{80,56},{88,... | collective-permute-start | bytes 5308424 | tf_op jit(solution)/shard_map/ppermute | solution.py:15
  125.8 7.0 %copy.16 = bf16[3,3,24,2048]{2,1,0,3:T(4,128)(2,1)} copy(bf16[3,3,24,2048]{3,2,1,0:T(8,128)(2,1)S(1)} %copy-done.1) | data formatting | bytes 1769472 | tf_op args[0]
  132.9 9.4 %reshape.171 = bf16[8,2,27648]{2,1,0:T(2,128)(2,1)} reshape(bf16[2048,3,3,24]{3,2,1,0:T(4,128)(2,1)} %bitcast.78) | data formatting | bytes 1769472
  142.3 7.0 %all-to-all-start = ((bf16[8,2,27648]{2,1,0:T(2,128)(2,1)}), bf16[8,2,27648]{2,1,0:T(2,128)(2,1)S(1)}, u32[]{:S(2)}, u32[]{:S(2)}) async-start(bf16[8,2,27648]{2,1,0:T(2,128)(2,1)} %reshape.171), calls=%async_computation | async-start | bytes 1769472 | tf_op jit(solution)/shard_map/all_to_all | solution.py:74
  152.0 65.8 %all-to-all-done = bf16[8,2,27648]{2,1,0:T(2,128)(2,1)S(1)} async-done(((bf16[8,2,27648]{2,1,0:T(2,128)(2,1)}), bf16[8,2,27648]{2,1,0:T(2,128)(2,1)S(1)}, u32[]{:S(2)}, u32[]{:S(2)}) %all-to-all-start) | async-done | bytes 884768 | tf_op jit(solution)/shard_map/all_to_all | solution.py:74
  217.7 7.8 %reshape.172 = bf16[2048,3,3,24]{3,2,1,0:T(4,128)(2,1)} reshape(bf16[8,2,27648]{2,1,0:T(2,128)(2,1)S(1)} %all-to-all-done) | data formatting | bytes 1769472
  225.6 7.6 %copy.17 = bf16[3,3,24,8,256]{4,2,1,3,0:T(8,128)(2,1)S(1)} copy(bf16[3,3,24,8,256]{2,1,0,4,3:T(4,128)(2,1)} %bitcast.75) | data formatting | bytes 1769472 | tf_op jit(solution)/shard_map/all_to_all | solution.py:74
  248.7 20.5 %reshape.130 = bf16[2,10368,2,128]{3,2,1,0:T(2,128)(2,1)} reshape(bf16[2,18,24,24,256]{4,3,2,1,0:T(8,128)(2,1)} %constant_dynamic-slice_fusion.1) | data formatting | bytes 21233664 | tf_op jit(solution)/shard_map/reshape | solution.py:23
  269.2 8.8 %slice_bitcast_fusion = (bf16[2,10368,128]{2,0,1:T(2,128)(2,1)S(1)}, bf16[2,10368,128]{2,0,1:T(2,128)(2,1)S(1)}) fusion(bf16[2,2,10368,128]{3,1,2,0:T(2,128)(2,1)} %bitcast.72), kind=kLoop, calls=%fused_computation.16 | loop fusion | bytes 21233664 | tf_op jit(solution)/shard_map/squeeze | solution.py:25
  286.9 160.2 %while.14 = (s32[]{:T(128)}, bf16[9,2,192,128]{3,2,1,0:T(8,128)(2,1)}, s32[9]{0:T(128)S(1)}, bf16[2,3,24,24,128]{4,0,3,2,1:T(2,128)(2,1)}, bf16[2,10368,128]{2,1...) while((s32[]{:T(128)}, ...), condition=%wide.region_3.4_spmd.clone.clone, body=%wide.region_0.3_spmd.clone.clone.sunk | while | flops 2066481408 | bytes 67346256 | solution.py:62
  299.2 5.4 %fusion.31 = bf16[9,2,192,128]{3,2,1,0:T(8,128)(2,1)} fusion(bf16[9,2,192,128]{3,2,1,0:T(8,128)(2,1)} %get-tuple-element.286, s32[]{:T(128)} %get-tuple-element.285, bf16[2,192,10368]{2,1,0:T(8,128)(2,1)S(1)} %exponential_convert_fusion.2, bf16[2,10368,128]{2,1,0:T(8,128)(2,1)} %get-tuple-element.306, f32[2,192]{1,0:T(2,128)S(1)} %convert_reduce_fusion.2), kind=kOutput, calls=%fused_computation.10.clone.1 | convolution fusion | flops 1019314176 | bytes 13371392 | tf_op jit(solution)/shard_map/while/body/eval_jaxpr/hqk,hkd->hqd/dot_general | solution.py:59
  448.4 18.5 %all_to_all.63 = bf16[3,24,24,256]{3,2,0,1:T(8,128)(2,1)S(1)} all-to-all(bf16[3,24,24,256]{3,2,0,1:T(8,128)(2,1)S(1)} %copy.28), channel_id=1, replica_groups=mesh['tm'=16,'height'=8] {'height'}, dimensions={1} | all-to-all | bytes 1769472 | tf_op jit(solution)/shard_map/all_to_all | solution.py:94
  (162 shorter events, 175.8 us)
Async XLA Ops:
  0.0 25.9 %copy-start = (bf16[3,3,24,2048]{3,2,1,0:T(8,128)(2,1)S(1)}, bf16[3,3,24,2048]{3,2,1,0:T(8,128)(2,1)}, u32[]{:S(2)}) copy-start(bf16[3,3,24,2048]{3,2,1,0:T(8,128)(2,1)} %param.6) | copy-start | bytes 2654212
  18.8 23.5 %all-to-all-start.2 = ((bf16[8,2,27648]{2,1,0:T(2,128)(2,1)}), bf16[8,2,27648]{2,1,0:T(2,128)(2,1)S(1)}, u32[]{:S(2)}, u32[]{:S(2)}) async-start(bf16[8,2,27648]{2,1,0:T(2,128)(2,1)} %reshape.173), calls=%async_computation.2 | async-start | bytes 1769472 | tf_op jit(solution)/shard_map/all_to_all | solution.py:76
  42.3 22.7 %all-to-all-start.1 = ((bf16[8,2,27648]{2,1,0:T(2,128)(2,1)}), bf16[8,2,27648]{2,1,0:T(2,128)(2,1)S(1)}, u32[]{:S(2)}, u32[]{:S(2)}) async-start(bf16[8,2,27648]{2,1,0:T(2,128)(2,1)} %reshape.175), calls=%async_computation.1 | async-start | bytes 1769472 | tf_op jit(solution)/shard_map/all_to_all | solution.py:75
  65.0 60.8 %copy-start.1 = (bf16[3,3,24,2048]{3,2,1,0:T(8,128)(2,1)S(1)}, bf16[3,3,24,2048]{3,2,1,0:T(8,128)(2,1)}, u32[]{:S(2)}) copy-start(bf16[3,3,24,2048]{3,2,1,0:T(8,128)(2,1)} %param.5) | copy-start | bytes 2654212
  81.9 36.7 %collective-permute-start = (bf16[2,3,24,24,256]{4,3,2,1,0:T(8,128)(2,1)}, bf16[2,3,24,24,256]{4,3,2,1,0:T(8,128)(2,1)}, u32[]{:S(2)}, u32[]{:S(2)}) collective-permute-start(bf16[2,3,24,24,256]{4,3,2,1,0:T(8,128)(2,1)} %pad_maximum_fusion), channel_id=1, source_target_pairs={{0,24},{8,32},{16,40},{24,48},{32,56},{40,64},{48,72},{56,80},{64,... | collective-permute-start | bytes 5308424 | tf_op jit(solution)/shard_map/ppermute | solution.py:15
  83.2 152.7 %collective-permute-start.1 = (bf16[2,3,24,24,256]{4,3,2,1,0:T(8,128)(2,1)}, bf16[2,3,24,24,256]{4,3,2,1,0:T(8,128)(2,1)}, u32[]{:S(2)}, u32[]{:S(2)}) collective-permute-start(bf16[2,3,24,24,256]{4,3,2,1,0:T(8,128)(2,1)} %pad_maximum_fusion), channel_id=1, source_target_pairs={{0,16},{8,24},{16,32},{24,40},{32,48},{40,56},{48,64},{56,72},{64,... | collective-permute-start | bytes 5308424 | tf_op jit(solution)/shard_map/ppermute | solution.py:15
  84.5 153.0 %collective-permute-start.2 = (bf16[2,3,24,24,256]{4,3,2,1,0:T(8,128)(2,1)}, bf16[2,3,24,24,256]{4,3,2,1,0:T(8,128)(2,1)}, u32[]{:S(2)}, u32[]{:S(2)}) collective-permute-start(bf16[2,3,24,24,256]{4,3,2,1,0:T(8,128)(2,1)} %pad_maximum_fusion), channel_id=1, source_target_pairs={{0,8},{8,16},{16,24},{24,32},{32,40},{40,48},{48,56},{56,64},{64,7... | collective-permute-start | bytes 5308424 | tf_op jit(solution)/shard_map/ppermute | solution.py:15
  86.5 152.8 %collective-permute-start.3 = (bf16[2,3,24,24,256]{4,3,2,1,0:T(8,128)(2,1)}, bf16[2,3,24,24,256]{4,3,2,1,0:T(8,128)(2,1)}, u32[]{:S(2)}, u32[]{:S(2)}) collective-permute-start(bf16[2,3,24,24,256]{4,3,2,1,0:T(8,128)(2,1)} %pad_maximum_fusion), channel_id=1, source_target_pairs={{8,0},{16,8},{24,16},{32,24},{40,32},{48,40},{56,48},{64,56},{72,6... | collective-permute-start | bytes 5308424 | tf_op jit(solution)/shard_map/ppermute | solution.py:15
  90.1 150.8 %collective-permute-start.4 = (bf16[2,3,24,24,256]{4,3,2,1,0:T(8,128)(2,1)}, bf16[2,3,24,24,256]{4,3,2,1,0:T(8,128)(2,1)}, u32[]{:S(2)}, u32[]{:S(2)}) collective-permute-start(bf16[2,3,24,24,256]{4,3,2,1,0:T(8,128)(2,1)} %pad_maximum_fusion), channel_id=1, source_target_pairs={{16,0},{24,8},{32,16},{40,24},{48,32},{56,40},{64,48},{72,56},{80,... | collective-permute-start | bytes 5308424 | tf_op jit(solution)/shard_map/ppermute | solution.py:15
  118.7 123.8 %collective-permute-start.5 = (bf16[2,3,24,24,256]{4,3,2,1,0:T(8,128)(2,1)}, bf16[2,3,24,24,256]{4,3,2,1,0:T(8,128)(2,1)}, u32[]{:S(2)}, u32[]{:S(2)}) collective-permute-start(bf16[2,3,24,24,256]{4,3,2,1,0:T(8,128)(2,1)} %pad_maximum_fusion), channel_id=1, source_target_pairs={{24,0},{32,8},{40,16},{48,24},{56,32},{64,40},{72,48},{80,56},{88,... | collective-permute-start | bytes 5308424 | tf_op jit(solution)/shard_map/ppermute | solution.py:15
  142.3 75.5 %all-to-all-start = ((bf16[8,2,27648]{2,1,0:T(2,128)(2,1)}), bf16[8,2,27648]{2,1,0:T(2,128)(2,1)S(1)}, u32[]{:S(2)}, u32[]{:S(2)}) async-start(bf16[8,2,27648]{2,1,0:T(2,128)(2,1)} %reshape.171), calls=%async_computation | async-start | bytes 1769472 | tf_op jit(solution)/shard_map/all_to_all | solution.py:74
where the time goes:
time: 472 us; the launch traced here: 468 us
  local copies, waits for them, and re-layouts  175 us (37%)
  matrix products  89.3 us (19%)
  waiting for transfers between devices  88.5 us (19%)
  starting transfers between devices  42.4 us (9%)
  other arithmetic  35.9 us (8%)
  blocking collectives  18.5 us (4%)
  loops' own time  18.2 us (4%)
    unnamed x20, local copies, waits for them, and re-layouts  92.1 us
    all_to_all x1, waiting for transfers between devices, body(): lax.all_to_all(query_band, 'height', split_axis=3, concat_axis=1, tiled=T...  65.8 us
    dot_general x9, matrix products, one_tile(): jnp.einsum('hqk,hkd->hqd', weights, value_rows, preferred_element_type=jn...  48.8 us
    dot_general x9, matrix products, one_tile(): jnp.einsum('hqd,hkd->hqk', query_block, key_rows, preferred_element_type=...  40.5 us
    ppermute x6, waiting for transfers between devices, from_behind(): lax.ppermute(value, axis, [(source, source + steps) for source in range(l...  22.7 us
    convert_element_type x9, other arithmetic, one_tile(): jnp.exp(scores - largest).astype(jnp.bfloat16)  21.9 us
    ppermute x6, starting transfers between devices, from_behind(): lax.ppermute(value, axis, [(source, source + steps) for source in range(l...  21.2 us
    reshape x1, local copies, waits for them, and re-layouts, attend_plane(): window.reshape(2, key_count, local_heads, HEAD_DIM)  20.5 us
  transfers between devices with their start and end apart: 9, of which 2 were waited for; matrix products, arithmetic and copies ran while one was open for 16% of the time, Pallas kernels for 0%

commit v1 on v0

v1 whole, which is shorter than its diff:
```python
import functools

import jax
import jax.numpy as jnp
from jax import lax
from jax.experimental import pallas as pl
from jax.experimental.pallas import tpu as pltpu
from jax.sharding import Mesh, PartitionSpec as P

HEAD_DIM = 128
HEADS = 16
BLOCK = 384
HALF = 192
LOG2E = 1.4426950408889634
SCORE_SCALE = HEAD_DIM ** (-0.5) * LOG2E
LOWEST = -1e30
VMEM = 56 * 1024 * 1024
PARAMS = dict(vmem_limit_bytes=VMEM)

CHUNK = (9, 24, HEAD_DIM)


def pack_kernel(core_ref, x_ref, o_ref):
    for h in range(4):
        part = x_ref[:, :, :, h * HEAD_DIM : (h + 1) * HEAD_DIM].astype(jnp.float32)
        for c in range(3):
            for r in range(3):
                piece = jnp.concatenate([part[f, r, c * 8 : (c + 1) * 8] for f in range(3)], axis=0)
                o_ref[h, c * 3 + r] = piece.astype(jnp.bfloat16)


def pack(core, x):
    return pl.pallas_call(
        pack_kernel,
        grid_spec=pltpu.PrefetchScalarGridSpec(
            num_scalar_prefetch=1,
            grid=(4,),
            in_specs=[pl.BlockSpec((3, 3, 24, 512), lambda j, s: (0, 0, 0, (j + 2 * s[0]) % 4))],
            out_specs=pl.BlockSpec((4,) + CHUNK, lambda j, s: (j, 0, 0, 0)),
        ),
        out_shape=jax.ShapeDtypeStruct((HEADS,) + CHUNK, jnp.bfloat16),
        compiler_params=pltpu.CompilerParams(**PARAMS),
        name="pack",
    )(core, x)


def unpack_kernel(core_ref, x_ref, o_ref):
    for h in range(4):
        for r in range(3):
            parts = [x_ref[h, c * 3 + r].astype(jnp.float32) for c in range(3)]
            for f in range(3):
                piece = jnp.concatenate([p[f * 8 : (f + 1) * 8] for p in parts], axis=0)
                o_ref[f, r, :, h * HEAD_DIM : (h + 1) * HEAD_DIM] = piece.astype(jnp.bfloat16)


def unpack(core, x):
    return pl.pallas_call(
        unpack_kernel,
        grid_spec=pltpu.PrefetchScalarGridSpec(
            num_scalar_prefetch=1,
            grid=(4,),
            in_specs=[pl.BlockSpec((4,) + CHUNK, lambda j, s: (j, 0, 0, 0))],
            out_specs=pl.BlockSpec((3, 3, 24, 512), lambda j, s: (0, 0, 0, (j + 2 * s[0]) % 4)),
        ),
        out_shape=jax.ShapeDtypeStruct((3, 3, 24, HEADS * HEAD_DIM), jnp.bfloat16),
        compiler_params=pltpu.CompilerParams(**PARAMS),
        name="unpack",
    )(core, x)


def assemble_kernel(kept_ref, came_ref, o_ref):
    for b in range(3):
        halves = []
        for ref in (kept_ref, came_ref):
            for row in range(8 * b, 8 * b + 8):
                halves.append(ref[row // 3, row % 3].astype(jnp.float32))
        o_ref[0, b] = jnp.concatenate(halves, axis=0).astype(jnp.bfloat16)


def assemble(kept, came):
    spec = pl.BlockSpec((8, 3, 24, HEAD_DIM), lambda c: (0, c, 0, 0))
    return pl.pallas_call(
        assemble_kernel,
        grid=(3,),
        in_specs=[spec, spec],
        out_specs=pl.BlockSpec((1, 3, BLOCK, HEAD_DIM), lambda c: (c, 0, 0, 0)),
        out_shape=jax.ShapeDtypeStruct((3, 3, BLOCK, HEAD_DIM), jnp.bfloat16),
        compiler_params=pltpu.CompilerParams(**PARAMS),
        name="assemble",
    )(kept, came)


SUB = 128


def attend_kernel(sides, first, last, q_low, p_low, p_high, v_low, *refs):
    refs = list(refs)
    flag_ref = refs.pop(0)
    q_ref = refs.pop(0)
    pairs = [(refs.pop(0), refs.pop(0)) for _ in range(sides)]
    if not first:
        acc_in, top_in = refs.pop(0), refs.pop(0)
    if last:
        kept_ref, sent_ref = refs.pop(0), refs.pop(0)
    else:
        acc_out, top_out = refs.pop(0), refs.pop(0)
    acc_ref, top_ref = refs
    step_id = pl.program_id(0)
    col = step_id // 3 + q_low
    band = step_id % 3
    if first:
        acc_ref[...] = jnp.zeros_like(acc_ref)
        top_ref[...] = jnp.full_like(top_ref, LOWEST)
    else:
        acc_ref[...] = acc_in[0]
        top_ref[...] = top_in[0]
    lowest = jnp.maximum(col - 1, p_low)
    highest = jnp.minimum(col + 1, p_high)
    for side in range(sides):
        k_ref, v_ref = pairs[side]

        def chunk(p, bands, start, k_ref=k_ref, v_ref=v_ref):
            keys = k_ref[p, pl.ds(start, bands)].reshape(bands * BLOCK, HEAD_DIM)
            values = v_ref[p - v_low, pl.ds(start, bands)].reshape(bands * BLOCK, HEAD_DIM)
            values = jnp.concatenate([values, jnp.ones_like(values)], axis=1)
            for s in range(BLOCK // SUB):
                rows = pl.ds(s * SUB, SUB)
                scores = lax.dot_general(
                    q_ref[0, 0, rows], keys, (((1,), (1,)), ((), ())), preferred_element_type=jnp.float32
                )
                before = top_ref[rows, :1]
                top = jnp.maximum(before, jnp.max(scores, axis=1, keepdims=True) * SCORE_SCALE)
                weights = jnp.exp2(scores * SCORE_SCALE - top).astype(jnp.bfloat16)
                fade = jnp.exp2(before - top)
                acc_ref[rows, :] = acc_ref[rows, :] * fade + jnp.dot(
                    weights, values, preferred_element_type=jnp.float32
                )
                top_ref[rows, :] = jnp.broadcast_to(top, (SUB, HEAD_DIM))

        def one(p, carry, chunk=chunk):
            @pl.when(band == 1)
            def _():
                chunk(p, 3, 0)

            @pl.when(band != 1)
            def _():
                chunk(p, 2, band // 2)

            return carry

        if sides == 1:
            lax.fori_loop(lowest, highest + 1, one, 0)
        else:

            @pl.when(flag_ref[side] != 0)
            def _(one=one):
                lax.fori_loop(lowest, highest + 1, one, 0)

    if not last:
        acc_out[0] = acc_ref[...]
        top_out[0] = top_ref[...]
        return
    result = acc_ref[:, :HEAD_DIM] / acc_ref[:, HEAD_DIM:]
    for b in range(3):

        @pl.when(band == b)
        def _(b=b):
            for half, ref in enumerate((kept_ref, sent_ref)):
                for n in range(8):
                    row = 8 * b + n
                    at = half * HALF + n * 24
                    ref[row // 3, row % 3] = result[at : at + 24].astype(jnp.bfloat16)


def attend(flags, q, pairs, state=None, last=False, cols=(0, 2), part=(0, 2), v_low=0):
    first = state is None
    q_low = cols[0]
    steps = 3 * (cols[1] - cols[0] + 1)
    tile = lambda i, s: (i // 3 + q_low, i % 3, 0, 0)
    flat = lambda i, s: (i + 3 * q_low, 0, 0)
    in_specs = [pl.BlockSpec((1, 1, BLOCK, HEAD_DIM), tile)]
    operands = [q]
    for k, v in pairs:
        for a in (k, v):
            in_specs.append(pl.BlockSpec(a.shape, lambda i, s: (0, 0, 0, 0)))
            operands.append(a)
    acc_spec = pl.BlockSpec((1, BLOCK, 2 * HEAD_DIM), flat)
    top_spec = pl.BlockSpec((1, BLOCK, HEAD_DIM), flat)
    state_shape = [
        jax.ShapeDtypeStruct((9, BLOCK, 2 * HEAD_DIM), jnp.float32),
        jax.ShapeDtypeStruct((9, BLOCK, HEAD_DIM), jnp.float32),
    ]
    if not first:
        in_specs += [acc_spec, top_spec]
        operands += list(state)
    if last:
        out_specs = [pl.BlockSpec((8, 3, 24, HEAD_DIM), lambda i, s: (0, i // 3, 0, 0))] * 2
        out_shape = [jax.ShapeDtypeStruct((8, 3 * (cols[1] - cols[0] + 1), 24, HEAD_DIM), jnp.bfloat16)] * 2
    else:
        out_specs = [acc_spec, top_spec]
        out_shape = state_shape
    kernel = functools.partial(attend_kernel, len(pairs), first, last, q_low, part[0], part[1], v_low)
    return pl.pallas_call(
        kernel,
        grid_spec=pltpu.PrefetchScalarGridSpec(
            num_scalar_prefetch=1,
            grid=(steps,),
            in_specs=in_specs,
            out_specs=out_specs,
            scratch_shapes=[
                pltpu.VMEM((BLOCK, 2 * HEAD_DIM), jnp.float32),
                pltpu.VMEM((BLOCK, HEAD_DIM), jnp.float32),
            ],
        ),
        out_shape=out_shape,
        compiler_params=pltpu.CompilerParams(**PARAMS),
        name="attend",
    )(flags, *operands)


PLANE = ("ylo", "core", "z", "yhi")


def plane_groups():
    at = lambda ylo, core, n: (ylo * 2 + core) * 8 + n
    first = [at(ylo, 0, n) for ylo in (0, 1) for n in range(8)]
    second = [at(ylo, 1, n) for ylo in (1, 0) for n in range(8)]
    return [first, second]


def exchange(x):
    return lax.all_to_all(x, PLANE, 0, 0, axis_index_groups=plane_groups(), tiled=True)


def swap_cores(x):
    return lax.ppermute(x, "core", [(0, 1), (1, 0)])


def from_tile(x, steps):
    at = lambda tile: (tile % 4) * 2 + tile // 4
    return lax.ppermute(
        x, ("x", "core"), [(at(t), at(t + steps)) for t in range(8) if 0 <= t + steps < 8]
    )


def body(query_band, key_band, value_band):
    core_index = lax.axis_index("core").astype(jnp.int32)
    core = core_index.reshape(1)
    tile = core_index * 4 + lax.axis_index("x").astype(jnp.int32)
    flags = jnp.stack([tile > 0, tile < 7]).astype(jnp.int32)

    def to_tile(band):
        got = exchange(pack(core, band))
        return assemble(got, swap_cores(got[8:]))

    keys = to_tile(key_band)
    keys_near = [from_tile(keys, s) for s in (1, -1)]
    queries = to_tile(query_band)
    values = to_tile(value_band)
    values_near = [from_tile(values, s) for s in (1, -1)]
    state = attend(flags, queries, [(keys, values)])
    kept, sent = attend(flags, queries, list(zip(keys_near, values_near)), state, last=True)
    back = jnp.concatenate([kept, swap_cores(sent)], axis=0)
    return unpack(core, exchange(back))


def solution(mesh):
    split = Mesh(mesh.devices.reshape(2, 4, 2, 4, 2), ("ylo", "x", "core", "z", "yhi"))
    spec = P(("ylo", "x", "core"), ("z", "yhi"), None, None)
    return jax.shard_map(body, mesh=split, in_specs=(spec, spec, spec), out_specs=spec, check_vma=False)
```

time: 472 us -> 182 us (0.39)
  the two profiles are of different devices: /device:TPU:14 before, /device:TPU:8 now
where the time goes in v1:
time: 182 us; the launch traced here: 180 us
  Pallas kernels  73.3 us (40%)
  starting transfers between devices  49.6 us (27%)
  waiting for transfers between devices  30.9 us (17%)
  blocking collectives  23.7 us (13%)
    pallas_call x2, Pallas kernels, attend(): pl.pallas_call(kernel, grid_spec=pltpu.PrefetchScalarGridSpec(num_scalar_...  50.6 us
    all_to_all x1, blocking collectives, exchange(): lax.all_to_all(x, PLANE, 0, 0, axis_index_groups=plane_groups(), tiled=True)  23.7 us
    all_to_all x3, waiting for transfers between devices, exchange(): lax.all_to_all(x, PLANE, 0, 0, axis_index_groups=plane_groups(), tiled=True)  22.9 us
    ppermute x4, starting transfers between devices, swap_cores(): return lax.ppermute(x, 'core', [(0, 1), (1, 0)])  21.6 us
    all_to_all x3, starting transfers between devices, exchange(): lax.all_to_all(x, PLANE, 0, 0, axis_index_groups=plane_groups(), tiled=True)  18.6 us
    pallas_call x3, Pallas kernels, pack(): pl.pallas_call(pack_kernel, grid_spec=pltpu.PrefetchScalarGridSpec(num_sc...  10.2 us
    ppermute x4, starting transfers between devices, from_tile(): lax.ppermute(x, ('x', 'core'), [(at(t), at(t + steps)) for t in range(8)...  9.41 us
    pallas_call x3, Pallas kernels, assemble(): pl.pallas_call(assemble_kernel, grid=(3,), in_specs=[spec, spec], out_spe...  9.16 us
  transfers between devices with their start and end apart: 11, of which 5 were waited for; matrix products, arithmetic and copies ran while one was open for 1% of the time, Pallas kernels for 23%

profile of v1, /device:TPU:8, one launch (start us, length us, event | category | flops | bytes accessed | tf_op | source)
XLA Modules:
  0.0 180.3 jit_solution(4972175526227603994)
XLA Ops:
  0.0 3.3 %pack.4 = bf16[16,9,24,128]{3,2,1,0:T(8,128)(2,1)} custom-call(s32[1]{0:T(128)} %bitcast.core_ref, bf16[3,3,24,2048]{3,2,1,0:T(8,128)(2,1)} %x_ref.4), custom_call_target="tpu_custom_call" | custom-call | tf_op jit(solution)/shard_map/pack/pallas_call | solution.py:33
  3.3 8.4 %all-to-all-start.1 = ((bf16[16,9,24,128]{3,2,1,0:T(8,128)(2,1)}), bf16[16,9,24,128]{3,2,1,0:T(8,128)(2,1)S(1)}, u32[]{:S(2)}, u32[]{:S(2)}) async-start(bf16[16,9,24,128]{3,2,1,0:T(8,128)(2,1)} %pack.4), calls=%async_computation.1 | async-start | bytes 1769472 | tf_op jit(solution)/shard_map/all_to_all | solution.py:232
  11.8 3.4 %pack.5 = bf16[16,9,24,128]{3,2,1,0:T(8,128)(2,1)} custom-call(s32[1]{0:T(128)} %bitcast.core_ref, bf16[3,3,24,2048]{3,2,1,0:T(8,128)(2,1)} %x_ref.5), custom_call_target="tpu_custom_call" | custom-call | tf_op jit(solution)/shard_map/pack/pallas_call | solution.py:33
  15.1 9.9 %all-to-all-done.1.kept_ref = bf16[16,9,24,128]{3,2,1,0:T(8,128)(2,1)S(1)} async-done(((bf16[16,9,24,128]{3,2,1,0:T(8,128)(2,1)}), bf16[16,9,24,128]{3,2,1,0:T(8,128)(2,1)S(1)}, u32[]{:S(2)}, u32[]{:S(2)}) %all-to-all-start.1) | async-done | bytes 884768 | tf_op jit(solution)/shard_map/all_to_all | solution.py:232
  25.0 5.1 %all-to-all-start.2 = ((bf16[16,9,24,128]{3,2,1,0:T(8,128)(2,1)}), bf16[16,9,24,128]{3,2,1,0:T(8,128)(2,1)S(1)}, u32[]{:S(2)}, u32[]{:S(2)}) async-start(bf16[16,9,24,128]{3,2,1,0:T(8,128)(2,1)} %pack.5), calls=%async_computation.2 | async-start | bytes 1769472 | tf_op jit(solution)/shard_map/all_to_all | solution.py:232
  30.3 12.9 %all-to-all-done.2.kept_ref = bf16[16,9,24,128]{3,2,1,0:T(8,128)(2,1)S(1)} async-done(((bf16[16,9,24,128]{3,2,1,0:T(8,128)(2,1)}), bf16[16,9,24,128]{3,2,1,0:T(8,128)(2,1)S(1)}, u32[]{:S(2)}, u32[]{:S(2)}) %all-to-all-start.2) | async-done | bytes 884768 | tf_op jit(solution)/shard_map/all_to_all | solution.py:232
  43.4 3.5 %pack.3 = bf16[16,9,24,128]{3,2,1,0:T(8,128)(2,1)} custom-call(s32[1]{0:T(128)} %bitcast.core_ref, bf16[3,3,24,2048]{3,2,1,0:T(8,128)(2,1)} %x_ref.3), custom_call_target="tpu_custom_call" | custom-call | tf_op jit(solution)/shard_map/pack/pallas_call | solution.py:33
  46.9 5.0 %all-to-all-start = ((bf16[16,9,24,128]{3,2,1,0:T(8,128)(2,1)}), bf16[16,9,24,128]{3,2,1,0:T(8,128)(2,1)S(1)}, u32[]{:S(2)}, u32[]{:S(2)}) async-start(bf16[16,9,24,128]{3,2,1,0:T(8,128)(2,1)} %pack.3), calls=%async_computation | async-start | bytes 1769472 | tf_op jit(solution)/shard_map/all_to_all | solution.py:232
  52.0 3.0 %assemble.4.refs_2_ = bf16[3,3,384,128]{3,2,1,0:T(8,128)(2,1)} custom-call(bf16[16,9,24,128]{3,2,1,0:T(8,128)(2,1)} %copy-done.1, bf16[8,9,24,128]{3,2,1,0:T(8,128)(2,1)} %collective-permute-done.1.came_ref), custom_call_target="tpu_custom_call" | custom-call | tf_op jit(solution)/shard_map/assemble/pallas_call | solution.py:82
  55.0 3.4 %collective-permute-start.2 = (bf16[3,3,384,128]{3,2,1,0:T(8,128)(2,1)}, bf16[3,3,384,128]{3,2,1,0:T(8,128)(2,1)S(1)}, u32[]{:S(2)}, u32[]{:S(2)}) collective-permute-start(bf16[3,3,384,128]{3,2,1,0:T(8,128)(2,1)} %assemble.4.refs_2_), channel_id=1, source_target_pairs={{0,16},{16,32},{32,48},{48,8},{8,24},{24,40},{40,56},{1,17},{17,33... | collective-permute-start | bytes 2654216 | tf_op jit(solution)/shard_map/ppermute | solution.py:241
  58.5 3.1 %assemble.5.refs_3_ = bf16[3,3,384,128]{3,2,1,0:T(8,128)(2,1)} custom-call(bf16[16,9,24,128]{3,2,1,0:T(8,128)(2,1)} %copy-done.2, bf16[8,9,24,128]{3,2,1,0:T(8,128)(2,1)} %collective-permute-done.3.came_ref), custom_call_target="tpu_custom_call" | custom-call | tf_op jit(solution)/shard_map/assemble/pallas_call | solution.py:82
  61.5 3.4 %collective-permute-start.4 = (bf16[3,3,384,128]{3,2,1,0:T(8,128)(2,1)}, bf16[3,3,384,128]{3,2,1,0:T(8,128)(2,1)S(1)}, u32[]{:S(2)}, u32[]{:S(2)}) collective-permute-start(bf16[3,3,384,128]{3,2,1,0:T(8,128)(2,1)} %assemble.5.refs_3_), channel_id=1, source_target_pairs={{0,16},{16,32},{32,48},{48,8},{8,24},{24,40},{40,56},{1,17},{17,33... | collective-permute-start | bytes 2654216 | tf_op jit(solution)/shard_map/ppermute | solution.py:241
  64.9 1.3 collective-permute-start.5
  66.2 1.3 collective-permute-start.6
  68.4 3.1 %collective-permute-start = (bf16[8,9,24,128]{3,2,1,0:T(8,128)(2,1)}, bf16[8,9,24,128]{3,2,1,0:T(8,128)(2,1)}, u32[]{:S(2)}, u32[]{:S(2)}) collective-permute-start(bf16[8,9,24,128]{3,2,1,0:T(8,128)(2,1)} %slice.12), channel_id=1, source_target_pairs={{0,8},{8,0},{1,9},{9,1},{2,10},{10,2},{3,11},{11,3},{4,12},{12,4},... | collective-permute-start | bytes 1327112 | tf_op jit(solution)/shard_map/ppermute | solution.py:236
  72.1 1.2 collective-permute-done.came_ref
  73.3 3.1 %assemble.3.refs_1_ = bf16[3,3,384,128]{3,2,1,0:T(8,128)(2,1)} custom-call(bf16[16,9,24,128]{3,2,1,0:T(8,128)(2,1)} %copy-done, bf16[8,9,24,128]{3,2,1,0:T(8,128)(2,1)} %collective-permute-done.came_ref), custom_call_target="tpu_custom_call" | custom-call | tf_op jit(solution)/shard_map/assemble/pallas_call | solution.py:82
  76.4 24.7 %attend.2 = (f32[9,384,256]{2,1,0:T(8,128)}, f32[9,384,128]{2,1,0:T(8,128)}) custom-call(s32[2]{0:T(128)} %add_convert_fusion.refs_0_, bf16[3,3,384,128]{3,2,1,0:T(8,128)(2,1)} %assemble.3.refs_1_, bf16[3,3,384,128]{3,2,1,0:T(8,128)(2,1)} %assemble.4.refs_2_, bf16[3,3,384,128]{3,2,1,0:T(8,128)(2,1)} %assemble.5.refs_3_), custom_call_target="tpu_custom_call" | custom-call | tf_op jit(solution)/shard_map/attend/pallas_call | solution.py:203
  101.1 5.2 %collective-permute-done.6.refs_5_ = bf16[3,3,384,128]{3,2,1,0:T(8,128)(2,1)} collective-permute-done((bf16[3,3,384,128]{3,2,1,0:T(8,128)(2,1)}, bf16[3,3,384,128]{3,2,1,0:T(8,128)(2,1)}, u32[]{:S(2)}, u32[]{:S(2)}) %collective-permute-start.6) | collective-permute-done | bytes 884768 | tf_op jit(solution)/shard_map/ppermute | solution.py:241
  106.3 25.9 %attend.3 = (bf16[8,9,24,128]{3,2,1,0:T(8,128)(2,1)}, bf16[8,9,24,128]{3,2,1,0:T(8,128)(2,1)}) custom-call(s32[2]{0:T(128)} %add_convert_fusion.refs_0_, bf16[3,3,384,128]{3,2,1,0:T(8,128)(2,1)} %assemble.3.refs_1_, bf16[3,3,384,128]{3,2,1,0:T(8,128)(2,1)} %copy-done.3, bf16[3,3,384,128]{3,2,1,0:T(8,128)(2,1)} %copy-done.4, ...), custom_call_target="tpu_custom_call" | custom-call | tf_op jit(solution)/shard_map/attend/pallas_call | solution.py:203
  132.2 18.3 %collective-permute-start.7 = (bf16[8,9,24,128]{3,2,1,0:T(8,128)(2,1)}, bf16[8,9,24,128]{3,2,1,0:T(8,128)(2,1)S(1)}, u32[]{:S(2)}, u32[]{:S(2)}) collective-permute-start(bf16[8,9,24,128]{3,2,1,0:T(8,128)(2,1)} %get-tuple-element.12), channel_id=1, source_target_pairs={{0,8},{8,0},{1,9},{9,1},{2,10},{10,2},{3,11},{11,3},{4,12},{12,4},... | collective-permute-start | bytes 1327112 | tf_op jit(solution)/shard_map/ppermute | solution.py:236
  150.5 1.6 collective-permute-done.7
  153.2 23.7 %all_to_all.20.x_ref = bf16[16,9,24,128]{3,2,1,0:T(8,128)(2,1)} all-to-all(bf16[16,9,24,128]{3,2,1,0:T(8,128)(2,1)S(1)} %pad_maximum_fusion), channel_id=1, replica_groups={{0,1,2,3,4,5,6,7,64,65,66,67,68,69,70,71},{72,73,74,75,76,77,78,79,8,9,..., dimensions={0} | all-to-all | bytes 1769472 | tf_op jit(solution)/shard_map/all_to_all | solution.py:232
  176.9 3.3 %unpack.1 = bf16[3,3,24,2048]{3,2,1,0:T(8,128)(2,1)} custom-call(s32[1]{0:T(128)} %bitcast.core_ref, bf16[16,9,24,128]{3,2,1,0:T(8,128)(2,1)} %all_to_all.20.x_ref), custom_call_target="tpu_custom_call" | custom-call | tf_op jit(solution)/shard_map/unpack/pallas_call | solution.py:57
  (25 shorter events, 2.9 us)
Async XLA Ops:
  3.3 21.7 %all-to-all-start.1 = ((bf16[16,9,24,128]{3,2,1,0:T(8,128)(2,1)}), bf16[16,9,24,128]{3,2,1,0:T(8,128)(2,1)S(1)}, u32[]{:S(2)}, u32[]{:S(2)}) async-start(bf16[16,9,24,128]{3,2,1,0:T(8,128)(2,1)} %pack.4), calls=%async_computation.1 | async-start | bytes 1769472 | tf_op jit(solution)/shard_map/all_to_all | solution.py:232
  25.0 21.9 %copy-start.1 = (bf16[16,9,24,128]{3,2,1,0:T(8,128)(2,1)}, bf16[16,9,24,128]{3,2,1,0:T(8,128)(2,1)S(1)}, u32[]{:S(2)}) copy-start(bf16[16,9,24,128]{3,2,1,0:T(8,128)(2,1)S(1)} %all-to-all-done.1.kept_ref) | copy-start | bytes 2654212
  25.0 18.2 %all-to-all-start.2 = ((bf16[16,9,24,128]{3,2,1,0:T(8,128)(2,1)}), bf16[16,9,24,128]{3,2,1,0:T(8,128)(2,1)S(1)}, u32[]{:S(2)}, u32[]{:S(2)}) async-start(bf16[16,9,24,128]{3,2,1,0:T(8,128)(2,1)} %pack.5), calls=%async_computation.2 | async-start | bytes 1769472 | tf_op jit(solution)/shard_map/all_to_all | solution.py:232
  30.2 21.7 %collective-permute-start.1 = (bf16[8,9,24,128]{3,2,1,0:T(8,128)(2,1)S(1)}, bf16[8,9,24,128]{3,2,1,0:T(8,128)(2,1)}, u32[]{:S(2)}, u32[]{:S(2)}) collective-permute-start(bf16[8,9,24,128]{3,2,1,0:T(8,128)(2,1)S(1)} %slice.13), channel_id=1, source_target_pairs={{0,8},{8,0},{1,9},{9,1},{2,10},{10,2},{3,11},{11,3},{4,12},{12,4},... | collective-permute-start | bytes 1327112 | tf_op jit(solution)/shard_map/ppermute | solution.py:236
  43.3 15.2 %copy-start.2 = (bf16[16,9,24,128]{3,2,1,0:T(8,128)(2,1)}, bf16[16,9,24,128]{3,2,1,0:T(8,128)(2,1)S(1)}, u32[]{:S(2)}) copy-start(bf16[16,9,24,128]{3,2,1,0:T(8,128)(2,1)S(1)} %all-to-all-done.2.kept_ref) | copy-start | bytes 2654212
  43.3 15.2 %collective-permute-start.3 = (bf16[8,9,24,128]{3,2,1,0:T(8,128)(2,1)S(1)}, bf16[8,9,24,128]{3,2,1,0:T(8,128)(2,1)}, u32[]{:S(2)}, u32[]{:S(2)}) collective-permute-start(bf16[8,9,24,128]{3,2,1,0:T(8,128)(2,1)S(1)} %slice.14), channel_id=1, source_target_pairs={{0,8},{8,0},{1,9},{9,1},{2,10},{10,2},{3,11},{11,3},{4,12},{12,4},... | collective-permute-start | bytes 1327112 | tf_op jit(solution)/shard_map/ppermute | solution.py:236
  46.9 20.6 %all-to-all-start = ((bf16[16,9,24,128]{3,2,1,0:T(8,128)(2,1)}), bf16[16,9,24,128]{3,2,1,0:T(8,128)(2,1)S(1)}, u32[]{:S(2)}, u32[]{:S(2)}) async-start(bf16[16,9,24,128]{3,2,1,0:T(8,128)(2,1)} %pack.3), calls=%async_computation | async-start | bytes 1769472 | tf_op jit(solution)/shard_map/all_to_all | solution.py:232
  55.0 46.1 %collective-permute-start.2 = (bf16[3,3,384,128]{3,2,1,0:T(8,128)(2,1)}, bf16[3,3,384,128]{3,2,1,0:T(8,128)(2,1)S(1)}, u32[]{:S(2)}, u32[]{:S(2)}) collective-permute-start(bf16[3,3,384,128]{3,2,1,0:T(8,128)(2,1)} %assemble.4.refs_2_), channel_id=1, source_target_pairs={{0,16},{16,32},{32,48},{48,8},{8,24},{24,40},{40,56},{1,17},{17,33... | collective-permute-start | bytes 2654216 | tf_op jit(solution)/shard_map/ppermute | solution.py:241
  61.5 39.5 %collective-permute-start.4 = (bf16[3,3,384,128]{3,2,1,0:T(8,128)(2,1)}, bf16[3,3,384,128]{3,2,1,0:T(8,128)(2,1)S(1)}, u32[]{:S(2)}, u32[]{:S(2)}) collective-permute-start(bf16[3,3,384,128]{3,2,1,0:T(8,128)(2,1)} %assemble.5.refs_3_), channel_id=1, source_target_pairs={{0,16},{16,32},{32,48},{48,8},{8,24},{24,40},{40,56},{1,17},{17,33... | collective-permute-start | bytes 2654216 | tf_op jit(solution)/shard_map/ppermute | solution.py:241
  64.9 36.2 %collective-permute-start.5 = (bf16[3,3,384,128]{3,2,1,0:T(8,128)(2,1)}, bf16[3,3,384,128]{3,2,1,0:T(8,128)(2,1)S(1)}, u32[]{:S(2)}, u32[]{:S(2)}) collective-permute-start(bf16[3,3,384,128]{3,2,1,0:T(8,128)(2,1)} %assemble.4.refs_2_), channel_id=1, source_target_pairs={{16,0},{32,16},{48,32},{8,48},{24,8},{40,24},{56,40},{17,1},{33,17... | collective-permute-start | bytes 2654216 | tf_op jit(solution)/shard_map/ppermute | solution.py:241
  66.2 40.1 %collective-permute-start.6 = (bf16[3,3,384,128]{3,2,1,0:T(8,128)(2,1)}, bf16[3,3,384,128]{3,2,1,0:T(8,128)(2,1)}, u32[]{:S(2)}, u32[]{:S(2)}) collective-permute-start(bf16[3,3,384,128]{3,2,1,0:T(8,128)(2,1)} %assemble.5.refs_3_), channel_id=1, source_target_pairs={{16,0},{32,16},{48,32},{8,48},{24,8},{40,24},{56,40},{17,1},{33,17... | collective-permute-start | bytes 2654216 | tf_op jit(solution)/shard_map/ppermute | solution.py:241
  67.5 5.8 %copy-start = (bf16[16,9,24,128]{3,2,1,0:T(8,128)(2,1)}, bf16[16,9,24,128]{3,2,1,0:T(8,128)(2,1)S(1)}, u32[]{:S(2)}) copy-start(bf16[16,9,24,128]{3,2,1,0:T(8,128)(2,1)S(1)} %all-to-all-done.kept_ref) | copy-start | bytes 2654212
  68.4 4.9 %collective-permute-start = (bf16[8,9,24,128]{3,2,1,0:T(8,128)(2,1)}, bf16[8,9,24,128]{3,2,1,0:T(8,128)(2,1)}, u32[]{:S(2)}, u32[]{:S(2)}) collective-permute-start(bf16[8,9,24,128]{3,2,1,0:T(8,128)(2,1)} %slice.12), channel_id=1, source_target_pairs={{0,8},{8,0},{1,9},{9,1},{2,10},{10,2},{3,11},{11,3},{4,12},{12,4},... | collective-permute-start | bytes 1327112 | tf_op jit(solution)/shard_map/ppermute | solution.py:236
  101.1 5.2 %copy-start.3 = (bf16[3,3,384,128]{3,2,1,0:T(8,128)(2,1)}, bf16[3,3,384,128]{3,2,1,0:T(8,128)(2,1)S(1)}, u32[]{:S(2)}) copy-start(bf16[3,3,384,128]{3,2,1,0:T(8,128)(2,1)S(1)} %collective-permute-done.2.refs_2_) | copy-start | bytes 2654212
  101.1 5.2 %copy-start.4 = (bf16[3,3,384,128]{3,2,1,0:T(8,128)(2,1)}, bf16[3,3,384,128]{3,2,1,0:T(8,128)(2,1)S(1)}, u32[]{:S(2)}) copy-start(bf16[3,3,384,128]{3,2,1,0:T(8,128)(2,1)S(1)} %collective-permute-done.4.refs_3_) | copy-start | bytes 2654212
  101.1 5.2 %copy-start.5 = (bf16[3,3,384,128]{3,2,1,0:T(8,128)(2,1)}, bf16[3,3,384,128]{3,2,1,0:T(8,128)(2,1)S(1)}, u32[]{:S(2)}) copy-start(bf16[3,3,384,128]{3,2,1,0:T(8,128)(2,1)S(1)} %collective-permute-done.5.refs_4_) | copy-start | bytes 2654212
  132.2 19.9 %collective-permute-start.7 = (bf16[8,9,24,128]{3,2,1,0:T(8,128)(2,1)}, bf16[8,9,24,128]{3,2,1,0:T(8,128)(2,1)S(1)}, u32[]{:S(2)}, u32[]{:S(2)}) collective-permute-start(bf16[8,9,24,128]{3,2,1,0:T(8,128)(2,1)} %get-tuple-element.12), channel_id=1, source_target_pairs={{0,8},{8,0},{1,9},{9,1},{2,10},{10,2},{3,11},{11,3},{4,12},{12,4},... | collective-permute-start | bytes 1327112 | tf_op jit(solution)/shard_map/ppermute | solution.py:236

commit v2 on v0

v2 whole, which is shorter than its diff:
```python
import functools

import jax
import jax.numpy as jnp
from jax import lax
from jax.experimental import pallas as pl
from jax.experimental.pallas import tpu as pltpu
from jax.sharding import Mesh, PartitionSpec as P

HEAD_DIM = 128
HEADS = 16
BLOCK = 384
HALF = 192
SCORE_SCALE = HEAD_DIM ** (-0.5) * 1.4426950408889634
LOWEST = -1e30
OVER = 2.0**100
BF16 = jnp.bfloat16
F32 = jnp.float32
CHUNK = (9, 24, HEAD_DIM)
NT = (((1,), (1,)), ((), ()))
TN = (((0,), (0,)), ((), ()))


def params():
    return pltpu.CompilerParams(vmem_limit_bytes=56 * 1024 * 1024)


def cost(us):
    return pl.CostEstimate(flops=int(us * 1e-6 * 1.1e15), bytes_accessed=int(us * 1e-6 * 3.3e12), transcendentals=0)


def pack_kernel(*refs):
    o_ref = refs[-1]
    for n, x_ref in enumerate(refs[:-1]):
        for h in range(8):
            o_ref[h, n] = x_ref[:, :, :, h * HEAD_DIM : (h + 1) * HEAD_DIM].reshape(CHUNK)


def pack(*bands):
    count = len(bands)
    return pl.pallas_call(
        pack_kernel,
        grid=(2,),
        in_specs=[pl.BlockSpec((3, 3, 24, 1024), lambda j: (0, 0, 0, j))] * count,
        out_specs=pl.BlockSpec((8, count) + CHUNK, lambda j: (j, 0, 0, 0, 0)),
        out_shape=jax.ShapeDtypeStruct((HEADS, count) + CHUNK, BF16),
        compiler_params=params(),
        cost_estimate=cost(2 * count),
        name="pack",
    )(*bands)


def unpack_kernel(x_ref, o_ref):
    for h in range(8):
        o_ref[:, :, :, h * HEAD_DIM : (h + 1) * HEAD_DIM] = x_ref[h].reshape(3, 3, 24, HEAD_DIM)


def unpack(x):
    return pl.pallas_call(
        unpack_kernel,
        grid=(2,),
        in_specs=[pl.BlockSpec((8,) + CHUNK, lambda j: (j, 0, 0, 0))],
        out_specs=pl.BlockSpec((3, 3, 24, 1024), lambda j: (0, 0, 0, j)),
        out_shape=jax.ShapeDtypeStruct((3, 3, 24, HEADS * HEAD_DIM), BF16),
        compiler_params=params(),
        cost_estimate=cost(2),
        name="unpack",
    )(x)


def assemble_kernel(cuts, got_ref, *o_refs):
    for b in range(3):
        n = [b in cut for cut in cuts].index(True)
        for m in range(got_ref.shape[1]):
            for half in range(2):
                slabs = [
                    got_ref[half * 8 + row // 3, m, f * 3 + row % 3].astype(F32)
                    for f in range(3)
                    for row in range(8 * b, 8 * b + 8)
                ]
                for c in range(3):
                    tokens = jnp.concatenate([s[c * 8 : (c + 1) * 8] for s in slabs], axis=0)
                    o_refs[n][m, b - cuts[n][0], c, half * HALF : (half + 1) * HALF] = tokens.astype(BF16)


def assemble(got, first, count, cuts):
    shapes = [(count, len(cut), 3, BLOCK, HEAD_DIM) for cut in cuts]
    whole = lambda shape: pl.BlockSpec(shape, lambda i, n=len(shape): (0,) * n)
    return pl.pallas_call(
        functools.partial(assemble_kernel, cuts),
        grid=(1,),
        in_specs=[pl.BlockSpec((16, count) + CHUNK, lambda i: (0, first // count, 0, 0, 0))],
        out_specs=[whole(s) for s in shapes],
        out_shape=[jax.ShapeDtypeStruct(s, BF16) for s in shapes],
        compiler_params=params(),
        cost_estimate=cost(2 * count),
        name="assemble",
    )(got)


def near(n):
    return range(max(n - 1, 0), min(n + 1, 2) + 1)


def attend_kernel(plan, *refs):
    own, last, cuts, q_bands = plan
    refs = list(refs)
    sides = 1 if own else 2
    flag_ref = None if own else refs.pop(0)
    q_ref = refs.pop(0)
    kv = [{}, {}]
    for side in range(sides):
        for cut in cuts:
            ref = refs.pop(0)
            for p in cut:
                kv[side][p] = (ref, p - cut[0])
    k_bands = [p for cut in cuts for p in cut]
    if not own:
        acc_in, row_in = refs.pop(0), refs.pop(0)
    if last:
        o_ref = refs.pop(0)
    acc_out, row_out = refs

    def tile(which, side, p, c):
        ref, at = kv[side][p]
        return ref[which, at, c]

    def run(which, places, cols):
        wide = len(cols) * BLOCK
        parts = []
        for p, side in places:
            ref, at = kv[side][p]
            parts.append(ref[which, at, cols[0] : cols[-1] + 1].reshape(wide, HEAD_DIM))
        return jnp.concatenate(parts, axis=0)

    worst = jnp.zeros((1, BLOCK), F32)
    for b in range(3):
        for c in range(3):
            at = 3 * b + c
            if b not in q_bands:
                acc_out[at] = acc_in[at]
                row_out[at] = row_in[at]
                continue
            q = q_ref[0, b, c]
            places = [(p, side) for p in k_bands if p in near(b) for side in range(sides)]
            cols = list(near(c))
            wide = len(cols) * BLOCK
            scores = lax.dot_general(run(0, places, cols), q, NT, preferred_element_type=F32)
            if own:
                mine = (places.index((b, 0)) * len(cols) + cols.index(c)) * BLOCK
                top = jnp.max(scores[mine : mine + BLOCK], axis=0, keepdims=True) * SCORE_SCALE
                tops = [top]
            else:
                top = row_in[at, 1:2]
                tops = [top + (1 - flag_ref[side]).astype(F32) * 1e30 for side in range(sides)]
            weights = jnp.concatenate(
                [
                    jnp.exp2(scores[n * wide : (n + 1) * wide] * SCORE_SCALE - tops[side])
                    for n, (p, side) in enumerate(places)
                ],
                axis=0,
            )
            total = jnp.sum(weights, axis=0, keepdims=True)
            acc = lax.dot_general(run(1, places, cols), weights.astype(BF16), TN, preferred_element_type=F32)
            if not own:
                acc = acc + acc_in[at]
                total = total + row_in[at, 0:1]
            acc_out[at] = acc
            row_out[at] = jnp.concatenate([total, top, jnp.zeros((6, BLOCK), F32)], axis=0)
            worst = jnp.maximum(worst, jnp.where(total < OVER, 0.0, 1.0))

    @pl.when(jnp.max(worst) > 0.0)
    def _():
        for b in q_bands:

            def redo(c, carry, b=b):
                at = 3 * b + c
                q = q_ref[0, b, c]
                if own:
                    acc_out[at] = jnp.zeros((HEAD_DIM, BLOCK), F32)
                    row_out[at, 0:1] = jnp.zeros((1, BLOCK), F32)
                    row_out[at, 1:2] = jnp.full((1, BLOCK), LOWEST, F32)
                else:
                    acc_out[at] = acc_in[at]
                    row_out[at] = row_in[at]
                for side in range(sides):
                    for p in k_bands:
                        if p not in near(b):
                            continue

                        def some(k, carry, side=side, p=p):
                            scores = lax.dot_general(tile(0, side, p, k), q, NT, preferred_element_type=F32)
                            before = row_out[at, 1:2]
                            top = jnp.maximum(before, jnp.max(scores, axis=0, keepdims=True) * SCORE_SCALE)
                            weights = jnp.exp2(scores * SCORE_SCALE - top)
                            fade = jnp.exp2(before - top)
                            acc = lax.dot_general(
                                tile(1, side, p, k), weights.astype(BF16), TN, preferred_element_type=F32
                            )
                            acc_out[at] = acc_out[at] * fade + acc
                            row_out[at, 0:1] = row_out[at, 0:1] * fade + jnp.sum(weights, axis=0, keepdims=True)
                            row_out[at, 1:2] = top
                            return carry

                        low, high = jnp.maximum(c - 1, 0), jnp.minimum(c + 1, 2) + 1
                        if own:
                            lax.fori_loop(low, high, some, 0)
                        else:

                            @pl.when(flag_ref[side] != 0)
                            def _(some=some, low=low, high=high):
                                lax.fori_loop(low, high, some, 0)

                return carry

            lax.fori_loop(0, 3, redo, 0)

    if last:
        for b in range(3):
            tiles = [(acc_out[3 * b + c] / row_out[3 * b + c, 0:1]).T for c in range(3)]
            for half in range(2):
                for f in range(3):
                    for n in range(8):
                        row = 8 * b + n
                        at = half * HALF + f * 64 + n * 8
                        slab = jnp.concatenate([t[at : at + 8] for t in tiles], axis=0)
                        o_ref[half * 8 + row // 3, f * 3 + row % 3] = slab.astype(BF16)


ACC = (9, HEAD_DIM, BLOCK)
ROW = (9, 8, BLOCK)


def attend(queries, keys_values, cuts, flags=None, state=None, last=False, us=12):
    own = state is None
    k_bands = [p for cut in cuts for p in cut]
    q_bands = [b for b in range(3) if any(p in near(b) for p in k_bands)]
    operands = [queries] + [a for side in keys_values for a in side]
    in_specs = []
    if not own:
        operands = [flags] + operands + list(state)
        in_specs.append(pl.BlockSpec(memory_space=pltpu.SMEM))
    in_specs += [pl.BlockSpec(memory_space=pltpu.VMEM)] * (len(operands) - len(in_specs))
    state_shapes = [jax.ShapeDtypeStruct(ACC, F32), jax.ShapeDtypeStruct(ROW, F32)]
    if last:
        out_shape = [jax.ShapeDtypeStruct((16,) + CHUNK, BF16)]
        scratch = [pltpu.VMEM(s.shape, F32) for s in state_shapes]
    else:
        out_shape, scratch = state_shapes, []
    return pl.pallas_call(
        functools.partial(attend_kernel, (own, last, cuts, q_bands)),
        in_specs=in_specs,
        out_specs=[pl.BlockSpec(memory_space=pltpu.VMEM)] * len(out_shape),
        out_shape=out_shape,
        scratch_shapes=scratch,
        compiler_params=params(),
        cost_estimate=cost(us),
        name="attend",
    )(*operands)


PLANE = ("core", "z", "yhi")


def exchange(x):
    return lax.all_to_all(x, PLANE, 0, 0, tiled=True)


def from_tile(x, steps):
    return lax.ppermute(x, ("ylo", "x"), [(t, t + steps) for t in range(8) if 0 <= t + steps < 8])


CUTS = ((0, 1), (2,))


def body(query_band, key_band, value_band):
    tile = (lax.axis_index("ylo") * 4 + lax.axis_index("x")).astype(jnp.int32)
    flags = jnp.stack([tile > 0, tile < 7]).astype(jnp.int32)
    got = exchange(pack(key_band, value_band, query_band))
    here = assemble(got, 0, 2, CUTS)
    near_tiles = [[from_tile(a, s) for s in (1, -1)] for a in here]
    (queries,) = assemble(got, 2, 1, ((0, 1, 2),))
    state = attend(queries, [here], CUTS, us=12)
    for n, cut in enumerate(CUTS):
        state = attend(
            queries, [[a] for a in near_tiles[n]], (cut,), flags, state, last=n == len(CUTS) - 1, us=9 * len(cut)
        )
    return unpack(exchange(state[0]))


def solution(mesh):
    split = Mesh(mesh.devices.reshape(2, 4, 2, 4, 2), ("ylo", "x", "core", "z", "yhi"))
    spec = P(("ylo", "x", "core"), ("z", "yhi"), None, None)
    return jax.shard_map(body, mesh=split, in_specs=(spec, spec, spec), out_specs=spec, check_vma=False)
```

time: 472 us -> 133 us (0.28)
  the two profiles are of different devices: /device:TPU:14 before, /device:TPU:8 now
where the time goes in v2:
time: 133 us; the launch traced here: 131 us
  Pallas kernels  45.6 us (34%)
  waiting for transfers between devices  37.3 us (28%)
  starting transfers between devices  23 us (17%)
  blocking collectives  20.3 us (15%)
  local copies, waits for them, and re-layouts  3.56 us (3%)
    pallas_call x3, Pallas kernels, attend(): pl.pallas_call(functools.partial(attend_kernel, (own, last, cuts, q_bands...  35.3 us
    all_to_all x1, waiting for transfers between devices, exchange(): return lax.all_to_all(x, PLANE, 0, 0, tiled=True)  34.4 us
    all_to_all x1, blocking collectives, exchange(): return lax.all_to_all(x, PLANE, 0, 0, tiled=True)  20.3 us
    ppermute x4, starting transfers between devices, from_tile(): lax.ppermute(x, ('ylo', 'x'), [(t, t + steps) for t in range(8) if 0 <= t...  15.9 us
    all_to_all x1, starting transfers between devices, exchange(): return lax.all_to_all(x, PLANE, 0, 0, tiled=True)  7.15 us
    pallas_call x2, Pallas kernels, assemble(): pl.pallas_call(functools.partial(assemble_kernel, cuts), grid=(1,), in_sp...  5.27 us
    unnamed x10, local copies, waits for them, and re-layouts  3.56 us
    pallas_call x1, Pallas kernels, pack(): pl.pallas_call(pack_kernel, grid=(2,), in_specs=[pl.BlockSpec((3, 3, 24,...  3.02 us
  transfers between devices with their start and end apart: 5, of which 3 were waited for; matrix products, arithmetic and copies ran while one was open for 0% of the time, Pallas kernels for 23%

profile of v2, /device:TPU:8, one launch (start us, length us, event | category | flops | bytes accessed | tf_op | source)
XLA Modules:
  0.0 130.6 jit_solution(18442461460943781281)
XLA Ops:
  0.0 3.0 %pack.1 = bf16[16,3,9,24,128]{4,3,2,1,0:T(8,128)(2,1)} custom-call(bf16[3,3,24,2048]{3,2,1,0:T(8,128)(2,1)} %refs_0_.1, bf16[3,3,24,2048]{3,2,1,0:T(8,128)(2,1)} %refs_1_.1, bf16[3,3,24,2048]{3,2,1,0:T(8,128)(2,1)} %refs_2_.1), custom_call_target="tpu_custom_call" | custom-call | flops 6600000000 | bytes 19800000 | tf_op jit(solution)/shard_map/pack/pallas_call | solution.py:41
  3.0 7.1 %all-to-all-start = ((bf16[16,3,9,24,128]{4,3,2,1,0:T(8,128)(2,1)}), bf16[16,3,9,24,128]{4,3,2,1,0:T(8,128)(2,1)S(1)}, u32[]{:S(2)}, u32[]{:S(2)}) async-start(bf16[16,3,9,24,128]{4,3,2,1,0:T(8,128)(2,1)} %pack.1), calls=%async_computation | async-start | bytes 5308416 | tf_op jit(solution)/shard_map/all_to_all | solution.py:266
  10.2 0.6 add_convert_fusion.refs_0_
  10.8 34.4 %all-to-all-done.got_ref = bf16[16,3,9,24,128]{4,3,2,1,0:T(8,128)(2,1)S(1)} async-done(((bf16[16,3,9,24,128]{4,3,2,1,0:T(8,128)(2,1)}), bf16[16,3,9,24,128]{4,3,2,1,0:T(8,128)(2,1)S(1)}, u32[]{:S(2)}, u32[]{:S(2)}) %all-to-all-start) | async-done | bytes 2654240 | tf_op jit(solution)/shard_map/all_to_all | solution.py:266
  45.2 1.5 %copy-done = bf16[16,3,9,24,128]{4,3,2,1,0:T(8,128)(2,1)} copy-done((bf16[16,3,9,24,128]{4,3,2,1,0:T(8,128)(2,1)}, bf16[16,3,9,24,128]{4,3,2,1,0:T(8,128)(2,1)S(1)}, u32[]{:S(2)}) %copy-start) | copy-done | bytes 2654232
  46.7 3.0 %assemble.3 = (bf16[2,2,3,384,128]{4,3,2,1,0:T(8,128)(2,1)}, bf16[2,1,3,384,128]{4,3,2,1,0:T(8,128)(2,1)}) custom-call(bf16[16,3,9,24,128]{4,3,2,1,0:T(8,128)(2,1)} %copy-done), custom_call_target="tpu_custom_call" | custom-call | flops 4400000000 | bytes 13200000 | tf_op jit(solution)/shard_map/assemble/pallas_call | solution.py:89
  49.8 3.4 %collective-permute-start.2 = (bf16[2,2,3,384,128]{4,3,2,1,0:T(8,128)(2,1)}, bf16[2,2,3,384,128]{4,3,2,1,0:T(8,128)(2,1)S(1)}, u32[]{:S(2)}, u32[]{:S(2)}) collective-permute-start(bf16[2,2,3,384,128]{4,3,2,1,0:T(8,128)(2,1)} %get-tuple-element.12.refs_1_), channel_id=1, source_target_pairs={{0,16},{16,32},{32,48},{48,64},{64,80},{80,96},{96,112},{1,17},{17... | collective-permute-start | bytes 3538952 | tf_op jit(solution)/shard_map/ppermute | solution.py:270
  53.2 4.6 %collective-permute-start.3 = (bf16[2,2,3,384,128]{4,3,2,1,0:T(8,128)(2,1)}, bf16[2,2,3,384,128]{4,3,2,1,0:T(8,128)(2,1)S(1)}, u32[]{:S(2)}, u32[]{:S(2)}) collective-permute-start(bf16[2,2,3,384,128]{4,3,2,1,0:T(8,128)(2,1)} %get-tuple-element.12.refs_1_), channel_id=1, source_target_pairs={{16,0},{32,16},{48,32},{64,48},{80,64},{96,80},{112,96},{17,1},{33... | collective-permute-start | bytes 3538952 | tf_op jit(solution)/shard_map/ppermute | solution.py:270
  57.7 1.9 %collective-permute-start = (bf16[2,1,3,384,128]{4,3,2,1,0:T(8,128)(2,1)}, bf16[2,1,3,384,128]{4,3,2,1,0:T(8,128)(2,1)S(1)}, u32[]{:S(2)}, u32[]{:S(2)}) collective-permute-start(bf16[2,1,3,384,128]{4,3,2,1,0:T(8,128)(2,1)} %get-tuple-element.11.refs_2_), channel_id=1, source_target_pairs={{0,16},{16,32},{32,48},{48,64},{64,80},{80,96},{96,112},{1,17},{17... | collective-permute-start | bytes 1769480 | tf_op jit(solution)/shard_map/ppermute | solution.py:270
  59.6 6.0 %collective-permute-start.1 = (bf16[2,1,3,384,128]{4,3,2,1,0:T(8,128)(2,1)}, bf16[2,1,3,384,128]{4,3,2,1,0:T(8,128)(2,1)S(1)}, u32[]{:S(2)}, u32[]{:S(2)}) collective-permute-start(bf16[2,1,3,384,128]{4,3,2,1,0:T(8,128)(2,1)} %get-tuple-element.11.refs_2_), channel_id=1, source_target_pairs={{16,0},{32,16},{48,32},{64,48},{80,64},{96,80},{112,96},{17,1},{33... | collective-permute-start | bytes 1769480 | tf_op jit(solution)/shard_map/ppermute | solution.py:270
  65.7 2.2 %assemble.2.refs_0_.refs_1_ = bf16[1,3,3,384,128]{4,3,2,1,0:T(8,128)(2,1)} custom-call(bf16[16,3,9,24,128]{4,3,2,1,0:T(8,128)(2,1)} %copy-done), custom_call_target="tpu_custom_call" | custom-call | flops 2200000000 | bytes 6600000 | tf_op jit(solution)/shard_map/assemble/pallas_call | solution.py:89
  67.9 13.6 %attend.3 = (f32[9,128,384]{2,1,0:T(8,128)}, f32[9,8,384]{2,1,0:T(8,128)}) custom-call(bf16[1,3,3,384,128]{4,3,2,1,0:T(8,128)(2,1)} %assemble.2.refs_0_.refs_1_, bf16[2,2,3,384,128]{4,3,2,1,0:T(8,128)(2,1)} %get-tuple-element.12.refs_1_, bf16[2,1,3,384,128]{4,3,2,1,0:T(8,128)(2,1)} %get-tuple-element.11.refs_2_), custom_call_target="tpu_custom_call" | custom-call | flops 13200000000 | bytes 39600000 | tf_op jit(solution)/shard_map/attend/pallas_call | solution.py:250
  81.5 1.3 collective-permute-done.2.refs_2_
  82.8 1.6 %collective-permute-done.3.refs_3_ = bf16[2,2,3,384,128]{4,3,2,1,0:T(8,128)(2,1)S(1)} collective-permute-done((bf16[2,2,3,384,128]{4,3,2,1,0:T(8,128)(2,1)}, bf16[2,2,3,384,128]{4,3,2,1,0:T(8,128)(2,1)S(1)}, u32[]{:S(2)}, u32[]{:S(2)}) %collective-permute-start.3) | collective-permute-done | bytes 1179680 | tf_op jit(solution)/shard_map/ppermute | solution.py:270
  84.4 0.0 copy-done.1
  84.4 1.0 copy-done.2
  85.5 13.9 %attend.4 = (f32[9,128,384]{2,1,0:T(8,128)}, f32[9,8,384]{2,1,0:T(8,128)}) custom-call(s32[2]{0:T(128)} %add_convert_fusion.refs_0_, bf16[1,3,3,384,128]{4,3,2,1,0:T(8,128)(2,1)} %assemble.2.refs_0_.refs_1_, bf16[2,2,3,384,128]{4,3,2,1,0:T(8,128)(2,1)} %copy-done.1, bf16[2,2,3,384,128]{4,3,2,1,0:T(8,128)(2,1)} %copy-done.2, ...), custom_call_target="tpu_custom_call" | custom-call | flops 19800000512 | bytes 59400000 | tf_op jit(solution)/shard_map/attend/pallas_call | solution.py:250
  99.4 0.0 collective-permute-done.refs_2_
  99.4 0.0 collective-permute-done.1.refs_3_
  99.4 0.8 copy-done.3
  100.2 0.2 copy-done.4
  100.4 7.8 %attend.5 = bf16[16,9,24,128]{3,2,1,0:T(8,128)(2,1)} custom-call(s32[2]{0:T(128)} %add_convert_fusion.refs_0_, bf16[1,3,3,384,128]{4,3,2,1,0:T(8,128)(2,1)} %assemble.2.refs_0_.refs_1_, bf16[2,1,3,384,128]{4,3,2,1,0:T(8,128)(2,1)} %copy-done.3, bf16[2,1,3,384,128]{4,3,2,1,0:T(8,128)(2,1)} %copy-done.4, f32[9,128,384]{2,1,0:T(8,128)} %get-tuple-element.15.refs_4_, ...), custom_call_target="tpu_custom_call" | custom-call | flops 9900000256 | bytes 29700000 | tf_op jit(solution)/shard_map/attend/pallas_call | solution.py:250
  108.2 20.3 %all_to_all.10.x_ref = bf16[16,9,24,128]{3,2,1,0:T(8,128)(2,1)} all-to-all(bf16[16,9,24,128]{3,2,1,0:T(8,128)(2,1)} %attend.5), channel_id=1, replica_groups=mesh['ylo'=2,'x'=4,'core'=2,'z'=4,'yhi'=2] {'core','z','yhi'}, dimensions={0} | all-to-all | bytes 1769472 | tf_op jit(solution)/shard_map/all_to_all | solution.py:266
  128.5 2.0 %unpack.1 = bf16[3,3,24,2048]{3,2,1,0:T(8,128)(2,1)} custom-call(bf16[16,9,24,128]{3,2,1,0:T(8,128)(2,1)} %all_to_all.10.x_ref), custom_call_target="tpu_custom_call" | custom-call | flops 2200000000 | bytes 6600000 | tf_op jit(solution)/shard_map/unpack/pallas_call | solution.py:59
  (5 shorter events, 0.0 us)
Async XLA Ops:
  3.0 42.2 %all-to-all-start = ((bf16[16,3,9,24,128]{4,3,2,1,0:T(8,128)(2,1)}), bf16[16,3,9,24,128]{4,3,2,1,0:T(8,128)(2,1)S(1)}, u32[]{:S(2)}, u32[]{:S(2)}) async-start(bf16[16,3,9,24,128]{4,3,2,1,0:T(8,128)(2,1)} %pack.1), calls=%async_computation | async-start | bytes 5308416 | tf_op jit(solution)/shard_map/all_to_all | solution.py:266
  45.2 1.5 %copy-start = (bf16[16,3,9,24,128]{4,3,2,1,0:T(8,128)(2,1)}, bf16[16,3,9,24,128]{4,3,2,1,0:T(8,128)(2,1)S(1)}, u32[]{:S(2)}) copy-start(bf16[16,3,9,24,128]{4,3,2,1,0:T(8,128)(2,1)S(1)} %all-to-all-done.got_ref) | copy-start | bytes 7962628
  49.8 33.1 %collective-permute-start.2 = (bf16[2,2,3,384,128]{4,3,2,1,0:T(8,128)(2,1)}, bf16[2,2,3,384,128]{4,3,2,1,0:T(8,128)(2,1)S(1)}, u32[]{:S(2)}, u32[]{:S(2)}) collective-permute-start(bf16[2,2,3,384,128]{4,3,2,1,0:T(8,128)(2,1)} %get-tuple-element.12.refs_1_), channel_id=1, source_target_pairs={{0,16},{16,32},{32,48},{48,64},{64,80},{80,96},{96,112},{1,17},{17... | collective-permute-start | bytes 3538952 | tf_op jit(solution)/shard_map/ppermute | solution.py:270
  53.2 31.3 %collective-permute-start.3 = (bf16[2,2,3,384,128]{4,3,2,1,0:T(8,128)(2,1)}, bf16[2,2,3,384,128]{4,3,2,1,0:T(8,128)(2,1)S(1)}, u32[]{:S(2)}, u32[]{:S(2)}) collective-permute-start(bf16[2,2,3,384,128]{4,3,2,1,0:T(8,128)(2,1)} %get-tuple-element.12.refs_1_), channel_id=1, source_target_pairs={{16,0},{32,16},{48,32},{64,48},{80,64},{96,80},{112,96},{17,1},{33... | collective-permute-start | bytes 3538952 | tf_op jit(solution)/shard_map/ppermute | solution.py:270
  57.7 41.7 %collective-permute-start = (bf16[2,1,3,384,128]{4,3,2,1,0:T(8,128)(2,1)}, bf16[2,1,3,384,128]{4,3,2,1,0:T(8,128)(2,1)S(1)}, u32[]{:S(2)}, u32[]{:S(2)}) collective-permute-start(bf16[2,1,3,384,128]{4,3,2,1,0:T(8,128)(2,1)} %get-tuple-element.11.refs_2_), channel_id=1, source_target_pairs={{0,16},{16,32},{32,48},{48,64},{64,80},{80,96},{96,112},{1,17},{17... | collective-permute-start | bytes 1769480 | tf_op jit(solution)/shard_map/ppermute | solution.py:270
  59.6 39.7 %collective-permute-start.1 = (bf16[2,1,3,384,128]{4,3,2,1,0:T(8,128)(2,1)}, bf16[2,1,3,384,128]{4,3,2,1,0:T(8,128)(2,1)S(1)}, u32[]{:S(2)}, u32[]{:S(2)}) collective-permute-start(bf16[2,1,3,384,128]{4,3,2,1,0:T(8,128)(2,1)} %get-tuple-element.11.refs_2_), channel_id=1, source_target_pairs={{16,0},{32,16},{48,32},{64,48},{80,64},{96,80},{112,96},{17,1},{33... | collective-permute-start | bytes 1769480 | tf_op jit(solution)/shard_map/ppermute | solution.py:270
  82.8 1.6 %copy-start.1 = (bf16[2,2,3,384,128]{4,3,2,1,0:T(8,128)(2,1)}, bf16[2,2,3,384,128]{4,3,2,1,0:T(8,128)(2,1)S(1)}, u32[]{:S(2)}) copy-start(bf16[2,2,3,384,128]{4,3,2,1,0:T(8,128)(2,1)S(1)} %collective-permute-done.2.refs_2_) | copy-start | bytes 3538948
  84.4 1.1 copy-start.2
  99.4 0.8 copy-start.3
  99.4 1.0 copy-start.4

commit v3 on v2

--- a/solution.py
+++ b/solution.py
@@ -100,6 +100,14 @@
 
 def near(n):
     return range(max(n - 1, 0), min(n + 1, 2) + 1)
+
+
+def groups(q_bands, k_bands):
+    if k_bands == [0, 1, 2]:
+        return [((0, 1), (0, 1)), ((1, 2), (2,)), ((2,), (1,))]
+    if k_bands == [0, 1]:
+        return [((0, 1), (0, 1)), ((2,), (1,))]
+    return [(tuple(q_bands), tuple(k_bands))]
 
 
 def attend_kernel(plan, *refs):
@@ -135,39 +143,49 @@
 
     worst = jnp.zeros((1, BLOCK), F32)
     for b in range(3):
-        for c in range(3):
-            at = 3 * b + c
-            if b not in q_bands:
-                acc_out[at] = acc_in[at]
-                row_out[at] = row_in[at]
-                continue
-            q = q_ref[0, b, c]
-            places = [(p, side) for p in k_bands if p in near(b) for side in range(sides)]
-            cols = list(near(c))
-            wide = len(cols) * BLOCK
+        if b not in q_bands:
+            for c in range(3):
+                acc_out[3 * b + c] = acc_in[3 * b + c]
+                row_out[3 * b + c] = row_in[3 * b + c]
+    for c in range(3):
+        cols = list(near(c))
+        wide = len(cols) * BLOCK
+        accs, totals, tops = {}, {}, {}
+        if not own:
+            for b in q_bands:
+                at = 3 * b + c
+                accs[b], totals[b], tops[b] = acc_in[at], row_in[at, 0:1], row_in[at, 1:2]
+        for bands, keys in groups(q_bands, k_bands):
+            places = [(p, side) for p in keys for side in range(sides)]
+            q = jnp.concatenate([q_ref[0, b, c] for b in bands], axis=0)
             scores = lax.dot_general(run(0, places, cols), q, NT, preferred_element_type=F32)
-            if own:
-                mine = (places.index((b, 0)) * len(cols) + cols.index(c)) * BLOCK
-                top = jnp.max(scores[mine : mine + BLOCK], axis=0, keepdims=True) * SCORE_SCALE
-                tops = [top]
-            else:
-                top = row_in[at, 1:2]
-                tops = [top + (1 - flag_ref[side]).astype(F32) * 1e30 for side in range(sides)]
+            for n, b in enumerate(bands):
+                if b not in tops:
+                    mine = (places.index((b, 0)) * len(cols) + cols.index(c)) * BLOCK
+                    mine = scores[mine : mine + BLOCK, n * BLOCK : (n + 1) * BLOCK]
+                    tops[b] = jnp.max(mine, axis=0, keepdims=True) * SCORE_SCALE
+            top = jnp.concatenate([tops[b] for b in bands], axis=1)
+            shifts = [top] if own else [top + (1 - flag_ref[side]).astype(F32) * 1e30 for side in range(sides)]
             weights = jnp.concatenate(
                 [
-                    jnp.exp2(scores[n * wide : (n + 1) * wide] * SCORE_SCALE - tops[side])
+                    jnp.exp2(scores[n * wide : (n + 1) * wide] * SCORE_SCALE - shifts[side]).astype(BF16)
                     for n, (p, side) in enumerate(places)
                 ],
                 axis=0,
             )
-            total = jnp.sum(weights, axis=0, keepdims=True)
-            acc = lax.dot_general(run(1, places, cols), weights.astype(BF16), TN, preferred_element_type=F32)
-            if not own:
-                acc = acc + acc_in[at]
-                total = total + row_in[at, 0:1]
-            acc_out[at] = acc
-            row_out[at] = jnp.concatenate([total, top, jnp.zeros((6, BLOCK), F32)], axis=0)
-            worst = jnp.maximum(worst, jnp.where(total < OVER, 0.0, 1.0))
+            values = run(1, places, cols)
+            values = jnp.concatenate([values.T, jnp.ones((16, values.shape[0]), BF16)], axis=0)
+            both = jnp.dot(values, weights, preferred_element_type=F32)
+            for n, b in enumerate(bands):
+                here = both[:, n * BLOCK : (n + 1) * BLOCK]
+                acc, total = here[:HEAD_DIM], here[HEAD_DIM : HEAD_DIM + 1]
+                accs[b] = accs[b] + acc if b in accs else acc
+                totals[b] = totals[b] + total if b in totals else total
+        for b in q_bands:
+            at = 3 * b + c
+            acc_out[at] = accs[b]
+            row_out[at] = jnp.concatenate([totals[b], tops[b], jnp.zeros((6, BLOCK), F32)], axis=0)
+            worst = jnp.maximum(worst, jnp.where(totals[b] < OVER, 0.0, 1.0))
 
     @pl.when(jnp.max(worst) > 0.0)
     def _():
@@ -278,13 +296,13 @@
     flags = jnp.stack([tile > 0, tile < 7]).astype(jnp.int32)
     got = exchange(pack(key_band, value_band, query_band))
     here = assemble(got, 0, 2, CUTS)
-    near_tiles = [[from_tile(a, s) for s in (1, -1)] for a in here]
+    near_first = [from_tile(here[0], s) for s in (1, -1)]
     (queries,) = assemble(got, 2, 1, ((0, 1, 2),))
     state = attend(queries, [here], CUTS, us=12)
-    for n, cut in enumerate(CUTS):
-        state = attend(
-            queries, [[a] for a in near_tiles[n]], (cut,), flags, state, last=n == len(CUTS) - 1, us=9 * len(cut)
-        )
+    second, state = lax.optimization_barrier((here[1], state))
+    near_second = [from_tile(second, s) for s in (1, -1)]
+    state = attend(queries, [[a] for a in near_first], CUTS[:1], flags, state, us=15)
+    state = attend(queries, [[a] for a in near_second], CUTS[1:], flags, state, last=True, us=8)
     return unpack(exchange(state[0]))
 
 

time: 133 us -> 133 us (level); the launches traced: 131 us -> 132 us
  waiting for transfers between devices: 37.3 us -> 44.1 us
  Pallas kernels: 45.6 us -> 41.6 us
    ppermute x4, waiting for transfers between devices: 2.89 us -> 9.75 us  [from_tile(): lax.ppermute(x, ('ylo', 'x'), [(t, t + steps) for t in range(8) if 0 <= t...]
    pallas_call x3, Pallas kernels: 35.3 us -> 31.3 us  [attend(): pl.pallas_call(functools.partial(attend_kernel, (own, last, cuts, q_bands...]
    unnamed x10 -> x12, local copies, waits for them, and re-layouts: 3.56 us -> 3.55 us
  transfers between devices with their start and end apart: 5 -> 5, of which waited for: 3 -> 3; matrix products, arithmetic and copies ran while one was open for 0% -> 1% of each run, Pallas kernels for 23% -> 20%
where the time goes in v3:
time: 133 us; the launch traced here: 132 us
  waiting for transfers between devices  44.1 us (33%)
  Pallas kernels  41.6 us (31%)
  starting transfers between devices  21.9 us (16%)
  blocking collectives  20.5 us (15%)
  local copies, waits for them, and re-layouts  3.55 us (3%)
    all_to_all x1, waiting for transfers between devices, exchange(): return lax.all_to_all(x, PLANE, 0, 0, tiled=True)  34.4 us
    pallas_call x3, Pallas kernels, attend(): pl.pallas_call(functools.partial(attend_kernel, (own, last, cuts, q_bands...  31.3 us
    all_to_all x1, blocking collectives, exchange(): return lax.all_to_all(x, PLANE, 0, 0, tiled=True)  20.5 us
    ppermute x4, starting transfers between devices, from_tile(): lax.ppermute(x, ('ylo', 'x'), [(t, t + steps) for t in range(8) if 0 <= t...  14.8 us
    ppermute x4, waiting for transfers between devices, from_tile(): lax.ppermute(x, ('ylo', 'x'), [(t, t + steps) for t in range(8) if 0 <= t...  9.75 us
    all_to_all x1, starting transfers between devices, exchange(): return lax.all_to_all(x, PLANE, 0, 0, tiled=True)  7.15 us
    pallas_call x2, Pallas kernels, assemble(): pl.pallas_call(functools.partial(assemble_kernel, cuts), grid=(1,), in_sp...  5.24 us
    unnamed x12, local copies, waits for them, and re-layouts  3.55 us
  transfers between devices with their start and end apart: 5, of which 3 were waited for; matrix products, arithmetic and copies ran while one was open for 1% of the time, Pallas kernels for 20%

profile of v3, /device:TPU:8, one launch (start us, length us, event | category | flops | bytes accessed | tf_op | source)
XLA Modules:
  0.0 132.5 jit_solution(15517296098290879371)
XLA Ops:
  0.0 3.0 %pack.1 = bf16[16,3,9,24,128]{4,3,2,1,0:T(8,128)(2,1)} custom-call(bf16[3,3,24,2048]{3,2,1,0:T(8,128)(2,1)} %refs_0_.1, bf16[3,3,24,2048]{3,2,1,0:T(8,128)(2,1)} %refs_1_.1, bf16[3,3,24,2048]{3,2,1,0:T(8,128)(2,1)} %refs_2_.1), custom_call_target="tpu_custom_call" | custom-call | flops 6600000000 | bytes 19800000 | tf_op jit(solution)/shard_map/pack/pallas_call | solution.py:41
  3.0 7.1 %all-to-all-start = ((bf16[16,3,9,24,128]{4,3,2,1,0:T(8,128)(2,1)}), bf16[16,3,9,24,128]{4,3,2,1,0:T(8,128)(2,1)S(1)}, u32[]{:S(2)}, u32[]{:S(2)}) async-start(bf16[16,3,9,24,128]{4,3,2,1,0:T(8,128)(2,1)} %pack.1), calls=%async_computation | async-start | bytes 5308416 | tf_op jit(solution)/shard_map/all_to_all | solution.py:284
  10.2 0.7 add_convert_fusion.refs_0_
  10.8 34.4 %all-to-all-done.got_ref = bf16[16,3,9,24,128]{4,3,2,1,0:T(8,128)(2,1)S(1)} async-done(((bf16[16,3,9,24,128]{4,3,2,1,0:T(8,128)(2,1)}), bf16[16,3,9,24,128]{4,3,2,1,0:T(8,128)(2,1)S(1)}, u32[]{:S(2)}, u32[]{:S(2)}) %all-to-all-start) | async-done | bytes 2654240 | tf_op jit(solution)/shard_map/all_to_all | solution.py:284
  45.2 1.5 %copy-done = bf16[16,3,9,24,128]{4,3,2,1,0:T(8,128)(2,1)} copy-done((bf16[16,3,9,24,128]{4,3,2,1,0:T(8,128)(2,1)}, bf16[16,3,9,24,128]{4,3,2,1,0:T(8,128)(2,1)S(1)}, u32[]{:S(2)}) %copy-start) | copy-done | bytes 2654232
  46.7 3.0 %assemble.3 = (bf16[2,2,3,384,128]{4,3,2,1,0:T(8,128)(2,1)}, bf16[2,1,3,384,128]{4,3,2,1,0:T(8,128)(2,1)}) custom-call(bf16[16,3,9,24,128]{4,3,2,1,0:T(8,128)(2,1)} %copy-done), custom_call_target="tpu_custom_call" | custom-call | flops 4400000000 | bytes 13200000 | tf_op jit(solution)/shard_map/assemble/pallas_call | solution.py:89
  49.7 4.9 %collective-permute-start.3 = (bf16[2,2,3,384,128]{4,3,2,1,0:T(8,128)(2,1)}, bf16[2,2,3,384,128]{4,3,2,1,0:T(8,128)(2,1)S(1)}, u32[]{:S(2)}, u32[]{:S(2)}) collective-permute-start(bf16[2,2,3,384,128]{4,3,2,1,0:T(8,128)(2,1)} %get-tuple-element.15.refs_1_), channel_id=1, source_target_pairs={{16,0},{32,16},{48,32},{64,48},{80,64},{96,80},{112,96},{17,1},{33... | collective-permute-start | bytes 3538952 | tf_op jit(solution)/shard_map/ppermute | solution.py:288
  54.6 1.9 %collective-permute-start.2 = (bf16[2,2,3,384,128]{4,3,2,1,0:T(8,128)(2,1)}, bf16[2,2,3,384,128]{4,3,2,1,0:T(8,128)(2,1)S(1)}, u32[]{:S(2)}, u32[]{:S(2)}) collective-permute-start(bf16[2,2,3,384,128]{4,3,2,1,0:T(8,128)(2,1)} %get-tuple-element.15.refs_1_), channel_id=1, source_target_pairs={{0,16},{16,32},{32,48},{48,64},{64,80},{80,96},{96,112},{1,17},{17... | collective-permute-start | bytes 3538952 | tf_op jit(solution)/shard_map/ppermute | solution.py:288
  56.6 2.2 %assemble.2.refs_0_.refs_1_ = bf16[1,3,3,384,128]{4,3,2,1,0:T(8,128)(2,1)} custom-call(bf16[16,3,9,24,128]{4,3,2,1,0:T(8,128)(2,1)} %copy-done), custom_call_target="tpu_custom_call" | custom-call | flops 2200000000 | bytes 6600000 | tf_op jit(solution)/shard_map/assemble/pallas_call | solution.py:89
  58.8 11.2 %attend.3 = (f32[9,128,384]{2,1,0:T(8,128)}, f32[9,8,384]{2,1,0:T(8,128)}) custom-call(bf16[1,3,3,384,128]{4,3,2,1,0:T(8,128)(2,1)} %assemble.2.refs_0_.refs_1_, bf16[2,2,3,384,128]{4,3,2,1,0:T(8,128)(2,1)} %get-tuple-element.15.refs_1_, bf16[2,1,3,384,128]{4,3,2,1,0:T(8,128)(2,1)} %get-tuple-element.18.refs_2_), custom_call_target="tpu_custom_call" | custom-call | flops 13200000000 | bytes 39600000 | tf_op jit(solution)/shard_map/attend/pallas_call | solution.py:268
  70.0 0.0 copy-done.3
  70.0 6.0 %collective-permute-start.1 = (bf16[2,1,3,384,128]{4,3,2,1,0:T(8,128)(2,1)S(1)}, bf16[2,1,3,384,128]{4,3,2,1,0:T(8,128)(2,1)S(1)}, u32[]{:S(2)}, u32[]{:S(2)}) collective-permute-start(bf16[2,1,3,384,128]{4,3,2,1,0:T(8,128)(2,1)S(1)} %copy-done.3), channel_id=1, source_target_pairs={{16,0},{32,16},{48,32},{64,48},{80,64},{96,80},{112,96},{17,1},{33... | collective-permute-start | bytes 1769480 | tf_op jit(solution)/shard_map/ppermute | solution.py:288
  76.1 1.9 %collective-permute-start = (bf16[2,1,3,384,128]{4,3,2,1,0:T(8,128)(2,1)S(1)}, bf16[2,1,3,384,128]{4,3,2,1,0:T(8,128)(2,1)S(1)}, u32[]{:S(2)}, u32[]{:S(2)}) collective-permute-start(bf16[2,1,3,384,128]{4,3,2,1,0:T(8,128)(2,1)S(1)} %copy-done.3), channel_id=1, source_target_pairs={{0,16},{16,32},{32,48},{48,64},{64,80},{80,96},{96,112},{1,17},{17... | collective-permute-start | bytes 1769480 | tf_op jit(solution)/shard_map/ppermute | solution.py:288
  78.0 3.3 %collective-permute-done.3.refs_3_ = bf16[2,2,3,384,128]{4,3,2,1,0:T(8,128)(2,1)S(1)} collective-permute-done((bf16[2,2,3,384,128]{4,3,2,1,0:T(8,128)(2,1)}, bf16[2,2,3,384,128]{4,3,2,1,0:T(8,128)(2,1)S(1)}, u32[]{:S(2)}, u32[]{:S(2)}) %collective-permute-start.3) | collective-permute-done | bytes 1179680 | tf_op jit(solution)/shard_map/ppermute | solution.py:288
  81.3 6.4 %collective-permute-done.2.refs_2_ = bf16[2,2,3,384,128]{4,3,2,1,0:T(8,128)(2,1)S(1)} collective-permute-done((bf16[2,2,3,384,128]{4,3,2,1,0:T(8,128)(2,1)}, bf16[2,2,3,384,128]{4,3,2,1,0:T(8,128)(2,1)S(1)}, u32[]{:S(2)}, u32[]{:S(2)}) %collective-permute-start.2) | collective-permute-done | bytes 1179680 | tf_op jit(solution)/shard_map/ppermute | solution.py:288
  87.8 1.0 copy-done.2
  88.8 13.0 %attend.4 = (f32[9,128,384]{2,1,0:T(8,128)}, f32[9,8,384]{2,1,0:T(8,128)}) custom-call(s32[2]{0:T(128)} %add_convert_fusion.refs_0_, bf16[1,3,3,384,128]{4,3,2,1,0:T(8,128)(2,1)} %assemble.2.refs_0_.refs_1_, bf16[2,2,3,384,128]{4,3,2,1,0:T(8,128)(2,1)} %copy-done.2, bf16[2,2,3,384,128]{4,3,2,1,0:T(8,128)(2,1)} %copy-done.1, ...), custom_call_target="tpu_custom_call" | custom-call | flops 16499999744 | bytes 49500000 | tf_op jit(solution)/shard_map/attend/pallas_call | solution.py:268
  101.8 0.0 collective-permute-done.1.refs_3_
  101.8 0.0 collective-permute-done.refs_2_
  101.8 0.8 copy-done.4
  102.6 0.2 copy-done.5
  102.8 7.1 %attend.5 = bf16[16,9,24,128]{3,2,1,0:T(8,128)(2,1)} custom-call(s32[2]{0:T(128)} %add_convert_fusion.refs_0_, bf16[1,3,3,384,128]{4,3,2,1,0:T(8,128)(2,1)} %assemble.2.refs_0_.refs_1_, bf16[2,1,3,384,128]{4,3,2,1,0:T(8,128)(2,1)} %copy-done.5, bf16[2,1,3,384,128]{4,3,2,1,0:T(8,128)(2,1)} %copy-done.4, f32[9,128,384]{2,1,0:T(8,128)} %get-tuple-element.21.refs_4_, ...), custom_call_target="tpu_custom_call" | custom-call | flops 8800000000 | bytes 26400000 | tf_op jit(solution)/shard_map/attend/pallas_call | solution.py:268
  109.9 20.5 %all_to_all.10.x_ref = bf16[16,9,24,128]{3,2,1,0:T(8,128)(2,1)} all-to-all(bf16[16,9,24,128]{3,2,1,0:T(8,128)(2,1)} %attend.5), channel_id=1, replica_groups=mesh['ylo'=2,'x'=4,'core'=2,'z'=4,'yhi'=2] {'core','z','yhi'}, dimensions={0} | all-to-all | bytes 1769472 | tf_op jit(solution)/shard_map/all_to_all | solution.py:284
  130.4 2.0 %unpack.1 = bf16[3,3,24,2048]{3,2,1,0:T(8,128)(2,1)} custom-call(bf16[16,9,24,128]{3,2,1,0:T(8,128)(2,1)} %all_to_all.10.x_ref), custom_call_target="tpu_custom_call" | custom-call | flops 2200000000 | bytes 6600000 | tf_op jit(solution)/shard_map/unpack/pallas_call | solution.py:59
  (7 shorter events, 0.0 us)
Async XLA Ops:
  3.0 42.2 %all-to-all-start = ((bf16[16,3,9,24,128]{4,3,2,1,0:T(8,128)(2,1)}), bf16[16,3,9,24,128]{4,3,2,1,0:T(8,128)(2,1)S(1)}, u32[]{:S(2)}, u32[]{:S(2)}) async-start(bf16[16,3,9,24,128]{4,3,2,1,0:T(8,128)(2,1)} %pack.1), calls=%async_computation | async-start | bytes 5308416 | tf_op jit(solution)/shard_map/all_to_all | solution.py:284
  45.2 1.5 %copy-start = (bf16[16,3,9,24,128]{4,3,2,1,0:T(8,128)(2,1)}, bf16[16,3,9,24,128]{4,3,2,1,0:T(8,128)(2,1)S(1)}, u32[]{:S(2)}) copy-start(bf16[16,3,9,24,128]{4,3,2,1,0:T(8,128)(2,1)S(1)} %all-to-all-done.got_ref) | copy-start | bytes 7962628
  49.7 31.6 %collective-permute-start.3 = (bf16[2,2,3,384,128]{4,3,2,1,0:T(8,128)(2,1)}, bf16[2,2,3,384,128]{4,3,2,1,0:T(8,128)(2,1)S(1)}, u32[]{:S(2)}, u32[]{:S(2)}) collective-permute-start(bf16[2,2,3,384,128]{4,3,2,1,0:T(8,128)(2,1)} %get-tuple-element.15.refs_1_), channel_id=1, source_target_pairs={{16,0},{32,16},{48,32},{64,48},{80,64},{96,80},{112,96},{17,1},{33... | collective-permute-start | bytes 3538952 | tf_op jit(solution)/shard_map/ppermute | solution.py:288
  54.6 33.1 %collective-permute-start.2 = (bf16[2,2,3,384,128]{4,3,2,1,0:T(8,128)(2,1)}, bf16[2,2,3,384,128]{4,3,2,1,0:T(8,128)(2,1)S(1)}, u32[]{:S(2)}, u32[]{:S(2)}) collective-permute-start(bf16[2,2,3,384,128]{4,3,2,1,0:T(8,128)(2,1)} %get-tuple-element.15.refs_1_), channel_id=1, source_target_pairs={{0,16},{16,32},{32,48},{48,64},{64,80},{80,96},{96,112},{1,17},{17... | collective-permute-start | bytes 3538952 | tf_op jit(solution)/shard_map/ppermute | solution.py:288
  58.8 11.2 %copy-start.3 = (bf16[2,1,3,384,128]{4,3,2,1,0:T(8,128)(2,1)S(1)}, bf16[2,1,3,384,128]{4,3,2,1,0:T(8,128)(2,1)}, u32[]{:S(2)}) copy-start(bf16[2,1,3,384,128]{4,3,2,1,0:T(8,128)(2,1)} %get-tuple-element.18.refs_2_) | copy-start | bytes 1769476
  70.0 31.8 %collective-permute-start.1 = (bf16[2,1,3,384,128]{4,3,2,1,0:T(8,128)(2,1)S(1)}, bf16[2,1,3,384,128]{4,3,2,1,0:T(8,128)(2,1)S(1)}, u32[]{:S(2)}, u32[]{:S(2)}) collective-permute-start(bf16[2,1,3,384,128]{4,3,2,1,0:T(8,128)(2,1)S(1)} %copy-done.3), channel_id=1, source_target_pairs={{16,0},{32,16},{48,32},{64,48},{80,64},{96,80},{112,96},{17,1},{33... | collective-permute-start | bytes 1769480 | tf_op jit(solution)/shard_map/ppermute | solution.py:288
  76.1 25.7 %collective-permute-start = (bf16[2,1,3,384,128]{4,3,2,1,0:T(8,128)(2,1)S(1)}, bf16[2,1,3,384,128]{4,3,2,1,0:T(8,128)(2,1)S(1)}, u32[]{:S(2)}, u32[]{:S(2)}) collective-permute-start(bf16[2,1,3,384,128]{4,3,2,1,0:T(8,128)(2,1)S(1)} %copy-done.3), channel_id=1, source_target_pairs={{0,16},{16,32},{32,48},{48,64},{64,80},{80,96},{96,112},{1,17},{17... | collective-permute-start | bytes 1769480 | tf_op jit(solution)/shard_map/ppermute | solution.py:288
  81.3 6.4 %copy-start.1 = (bf16[2,2,3,384,128]{4,3,2,1,0:T(8,128)(2,1)}, bf16[2,2,3,384,128]{4,3,2,1,0:T(8,128)(2,1)S(1)}, u32[]{:S(2)}) copy-start(bf16[2,2,3,384,128]{4,3,2,1,0:T(8,128)(2,1)S(1)} %collective-permute-done.3.refs_3_) | copy-start | bytes 3538948
  87.8 1.0 copy-start.2
  101.8 0.8 copy-start.4
  101.8 1.0 copy-start.5

commit v4 on v3

--- a/solution.py
+++ b/solution.py
@@ -21,81 +21,109 @@
 TN = (((0,), (0,)), ((), ()))
 
 
-def params():
-    return pltpu.CompilerParams(vmem_limit_bytes=56 * 1024 * 1024)
+def params(mib):
+    return pltpu.CompilerParams(vmem_limit_bytes=mib * 1024 * 1024)
 
 
 def cost(us):
-    return pl.CostEstimate(flops=int(us * 1e-6 * 1.1e15), bytes_accessed=int(us * 1e-6 * 3.3e12), transcendentals=0)
-
-
-def pack_kernel(*refs):
+    return pl.CostEstimate(flops=int(us * 1e6), bytes_accessed=int(us * 1e4), transcendentals=0)
+
+
+def pack_first_kernel(core_ref, *refs):
     o_ref = refs[-1]
     for n, x_ref in enumerate(refs[:-1]):
         for h in range(8):
-            o_ref[h, n] = x_ref[:, :, :, h * HEAD_DIM : (h + 1) * HEAD_DIM].reshape(CHUNK)
-
-
-def pack(*bands):
-    count = len(bands)
+            o_ref[h, n] = x_ref[:, :, 0:16, h * HEAD_DIM : (h + 1) * HEAD_DIM].reshape(9, 16, HEAD_DIM)
+
+
+def pack_second_kernel(core_ref, key_ref, value_ref, query_ref, o_ref):
+    for h in range(8):
+        lanes = slice(h * HEAD_DIM, (h + 1) * HEAD_DIM)
+        for n in range(9):
+            last = [ref[n // 3, n % 3, 16:24, lanes].astype(F32) for ref in (key_ref, value_ref)]
+            o_ref[h, n, 0:16] = jnp.concatenate(last, axis=0).astype(BF16)
+            o_ref[h, n, 16:40] = query_ref[n // 3, n % 3, :, lanes]
+
+
+def pack(core, kernel, inner, *bands):
     return pl.pallas_call(
-        pack_kernel,
-        grid=(2,),
-        in_specs=[pl.BlockSpec((3, 3, 24, 1024), lambda j: (0, 0, 0, j))] * count,
-        out_specs=pl.BlockSpec((8, count) + CHUNK, lambda j: (j, 0, 0, 0, 0)),
-        out_shape=jax.ShapeDtypeStruct((HEADS, count) + CHUNK, BF16),
-        compiler_params=params(),
-        cost_estimate=cost(2 * count),
+        kernel,
+        grid_spec=pltpu.PrefetchScalarGridSpec(
+            num_scalar_prefetch=1,
+            grid=(2,),
+            in_specs=[pl.BlockSpec((3, 3, 24, 1024), lambda j, s: (0, 0, 0, (j + s[0]) % 2))] * len(bands),
+            out_specs=pl.BlockSpec((8,) + inner, lambda j, s: (j,) + (0,) * len(inner)),
+        ),
+        out_shape=jax.ShapeDtypeStruct((HEADS,) + inner, BF16),
+        compiler_params=params(56),
+        cost_estimate=cost(1.2 * len(bands)),
         name="pack",
-    )(*bands)
-
-
-def unpack_kernel(x_ref, o_ref):
+    )(core, *bands)
+
+
+FIRST = (2, 9, 16, HEAD_DIM)
+SECOND = (9, 40, HEAD_DIM)
+
+
+def unpack_kernel(core_ref, x_ref, o_ref):
     for h in range(8):
         o_ref[:, :, :, h * HEAD_DIM : (h + 1) * HEAD_DIM] = x_ref[h].reshape(3, 3, 24, HEAD_DIM)
 
 
-def unpack(x):
+def unpack(core, x):
     return pl.pallas_call(
         unpack_kernel,
-        grid=(2,),
-        in_specs=[pl.BlockSpec((8,) + CHUNK, lambda j: (j, 0, 0, 0))],
-        out_specs=pl.BlockSpec((3, 3, 24, 1024), lambda j: (0, 0, 0, j)),
+        grid_spec=pltpu.PrefetchScalarGridSpec(
+            num_scalar_prefetch=1,
+            grid=(2,),
+            in_specs=[pl.BlockSpec((8,) + CHUNK, lambda j, s: (j, 0, 0, 0))],
+            out_specs=pl.BlockSpec((3, 3, 24, 1024), lambda j, s: (0, 0, 0, (j + s[0]) % 2)),
+        ),
         out_shape=jax.ShapeDtypeStruct((3, 3, 24, HEADS * HEAD_DIM), BF16),
-        compiler_params=params(),
-        cost_estimate=cost(2),
+        compiler_params=params(12),
+        cost_estimate=cost(1),
         name="unpack",
-    )(x)
-
-
-def assemble_kernel(cuts, got_ref, *o_refs):
+    )(core, x)
+
+
+def gather(o_refs, slab):
     for b in range(3):
-        n = [b in cut for cut in cuts].index(True)
-        for m in range(got_ref.shape[1]):
-            for half in range(2):
-                slabs = [
-                    got_ref[half * 8 + row // 3, m, f * 3 + row % 3].astype(F32)
-                    for f in range(3)
-                    for row in range(8 * b, 8 * b + 8)
-                ]
-                for c in range(3):
-                    tokens = jnp.concatenate([s[c * 8 : (c + 1) * 8] for s in slabs], axis=0)
-                    o_refs[n][m, b - cuts[n][0], c, half * HALF : (half + 1) * HALF] = tokens.astype(BF16)
-
-
-def assemble(got, first, count, cuts):
-    shapes = [(count, len(cut), 3, BLOCK, HEAD_DIM) for cut in cuts]
-    whole = lambda shape: pl.BlockSpec(shape, lambda i, n=len(shape): (0,) * n)
+        for half in range(2):
+            slabs = [slab(half, row // 3, f * 3 + row % 3) for f in range(3) for row in range(8 * b, 8 * b + 8)]
+            for c, (ref, where) in enumerate(o_refs):
+                tokens = jnp.concatenate([s[c * 8 : (c + 1) * 8] for s in slabs], axis=0)
+                ref[where + (b, pl.ds(half * HALF, HALF))] = tokens.astype(BF16)
+
+
+def assemble_first_kernel(kept_ref, came_ref, kv_ref):
+    halves = (kept_ref, came_ref)
+    for m in range(2):
+        places = [(kv_ref, (m, c)) for c in range(2)]
+        gather(places, lambda half, chunk, n, m=m: halves[half][chunk, m, n].astype(F32))
+
+
+def assemble_second_kernel(kept_ref, came_ref, kv_ref):
+    halves = (kept_ref, came_ref)
+    places = [(kv_ref, (m, 0)) for m in range(2)]
+    gather(places, lambda half, chunk, n: halves[half][chunk, n, 0:16].astype(F32))
+
+
+def assemble_queries_kernel(kept_ref, came_ref, q_ref):
+    places = [(q_ref, (0, c)) for c in range(3)]
+    slab = lambda half, chunk, n: (came_ref[chunk, n] if half else kept_ref[chunk, n, 16:40]).astype(F32)
+    gather(places, slab)
+
+
+def assemble(kernel, got, came, *leads):
     return pl.pallas_call(
-        functools.partial(assemble_kernel, cuts),
-        grid=(1,),
-        in_specs=[pl.BlockSpec((16, count) + CHUNK, lambda i: (0, first // count, 0, 0, 0))],
-        out_specs=[whole(s) for s in shapes],
-        out_shape=[jax.ShapeDtypeStruct(s, BF16) for s in shapes],
-        compiler_params=params(),
-        cost_estimate=cost(2 * count),
+        kernel,
+        in_specs=[pl.BlockSpec(memory_space=pltpu.VMEM)] * 2,
+        out_specs=[pl.BlockSpec(memory_space=pltpu.VMEM)] * len(leads),
+        out_shape=[jax.ShapeDtypeStruct(lead + (3, BLOCK, HEAD_DIM), BF16) for lead in leads],
+        compiler_params=params(8),
+        cost_estimate=cost(1),
         name="assemble",
-    )(got)
+    )(got, came)
 
 
 def near(n):
@@ -126,7 +154,7 @@
     if not own:
         acc_in, row_in = refs.pop(0), refs.pop(0)
     if last:
-        o_ref = refs.pop(0)
+        o_refs = (refs.pop(0), refs.pop(0))
     acc_out, row_out = refs
 
     def tile(which, side, p, c):
@@ -235,14 +263,14 @@
 
     if last:
         for b in range(3):
-            tiles = [(acc_out[3 * b + c] / row_out[3 * b + c, 0:1]).T for c in range(3)]
+            tiles = [(acc_out[3 * c + b] / row_out[3 * c + b, 0:1]).T for c in range(3)]
             for half in range(2):
                 for f in range(3):
                     for n in range(8):
                         row = 8 * b + n
                         at = half * HALF + f * 64 + n * 8
                         slab = jnp.concatenate([t[at : at + 8] for t in tiles], axis=0)
-                        o_ref[half * 8 + row // 3, f * 3 + row % 3] = slab.astype(BF16)
+                        o_refs[half][row // 3, f * 3 + row % 3] = slab.astype(BF16)
 
 
 ACC = (9, HEAD_DIM, BLOCK)
@@ -261,7 +289,7 @@
     in_specs += [pl.BlockSpec(memory_space=pltpu.VMEM)] * (len(operands) - len(in_specs))
     state_shapes = [jax.ShapeDtypeStruct(ACC, F32), jax.ShapeDtypeStruct(ROW, F32)]
     if last:
-        out_shape = [jax.ShapeDtypeStruct((16,) + CHUNK, BF16)]
+        out_shape = [jax.ShapeDtypeStruct((8,) + CHUNK, BF16)] * 2
         scratch = [pltpu.VMEM(s.shape, F32) for s in state_shapes]
     else:
         out_shape, scratch = state_shapes, []
@@ -271,39 +299,56 @@
         out_specs=[pl.BlockSpec(memory_space=pltpu.VMEM)] * len(out_shape),
         out_shape=out_shape,
         scratch_shapes=scratch,
-        compiler_params=params(),
+        compiler_params=params(24),
         cost_estimate=cost(us),
         name="attend",
     )(*operands)
 
 
-PLANE = ("core", "z", "yhi")
+PLANE = ("ylo", "core", "z", "yhi")
+
+
+def plane_groups():
+    at = lambda ylo, core, n: (ylo * 2 + core) * 8 + n
+    return [[at(ylo, core, n) for ylo in (core, 1 - core) for n in range(8)] for core in (0, 1)]
 
 
 def exchange(x):
-    return lax.all_to_all(x, PLANE, 0, 0, tiled=True)
+    return lax.all_to_all(x, PLANE, 0, 0, axis_index_groups=plane_groups(), tiled=True)
+
+
+def swap_cores(x):
+    return lax.ppermute(x, "core", [(0, 1), (1, 0)])
 
 
 def from_tile(x, steps):
-    return lax.ppermute(x, ("ylo", "x"), [(t, t + steps) for t in range(8) if 0 <= t + steps < 8])
+    at = lambda tile: (tile % 4) * 2 + tile // 4
+    return lax.ppermute(x, ("x", "core"), [(at(t), at(t + steps)) for t in range(8) if 0 <= t + steps < 8])
 
 
 CUTS = ((0, 1), (2,))
 
 
 def body(query_band, key_band, value_band):
-    tile = (lax.axis_index("ylo") * 4 + lax.axis_index("x")).astype(jnp.int32)
+    core_index = lax.axis_index("core").astype(jnp.int32)
+    core = core_index.reshape(1)
+    tile = core_index * 4 + lax.axis_index("x").astype(jnp.int32)
     flags = jnp.stack([tile > 0, tile < 7]).astype(jnp.int32)
-    got = exchange(pack(key_band, value_band, query_band))
-    here = assemble(got, 0, 2, CUTS)
-    near_first = [from_tile(here[0], s) for s in (1, -1)]
-    (queries,) = assemble(got, 2, 1, ((0, 1, 2),))
-    state = attend(queries, [here], CUTS, us=12)
-    second, state = lax.optimization_barrier((here[1], state))
+    got = exchange(pack(core, pack_first_kernel, FIRST, key_band, value_band))
+    rest = pack(core, pack_second_kernel, SECOND, key_band, value_band, query_band)
+    rest, got = lax.optimization_barrier((rest, got))
+    came = swap_cores(got[8:])
+    got_rest = exchange(rest)
+    (first,) = assemble(assemble_first_kernel, got, came, (2, 2))
+    near_first = [from_tile(first, s) for s in (1, -1)]
+    (second,) = assemble(assemble_second_kernel, got_rest, swap_cores(got_rest[8:, :, :16]), (2, 1))
+    (queries,) = assemble(assemble_queries_kernel, got_rest, swap_cores(got_rest[8:, :, 16:]), (1, 3))
     near_second = [from_tile(second, s) for s in (1, -1)]
-    state = attend(queries, [[a] for a in near_first], CUTS[:1], flags, state, us=15)
-    state = attend(queries, [[a] for a in near_second], CUTS[1:], flags, state, last=True, us=8)
-    return unpack(exchange(state[0]))
+    state = attend(queries, [[first, second]], CUTS, us=9)
+    state = attend(queries, [[a] for a in near_first], CUTS[:1], flags, state, us=10)
+    kept, sent = attend(queries, [[a] for a in near_second], CUTS[1:], flags, state, last=True, us=5)
+    back = jnp.concatenate([kept, swap_cores(sent)], axis=0)
+    return unpack(core, exchange(back))
 
 
 def solution(mesh):

time: 133 us -> 115 us (0.86)
  waiting for transfers between devices: 44.1 us -> 31 us
  Pallas kernels: 41.6 us -> 34.2 us
  starting transfers between devices: 21.9 us -> 27.3 us
  local copies, waits for them, and re-layouts: 3.55 us -> 0.87 us
    all_to_all x1 -> x2, waiting for transfers between devices: 34.4 us -> 24.3 us  [exchange(): lax.all_to_all(x, PLANE, 0, 0, axis_index_groups=plane_groups(), tiled=True)]
    all_to_all x1 -> x2, starting transfers between devices: 7.15 us -> 15 us  [exchange(): lax.all_to_all(x, PLANE, 0, 0, axis_index_groups=plane_groups(), tiled=True)]
    pallas_call x3, Pallas kernels: 31.3 us -> 25.6 us  [attend(): pl.pallas_call(functools.partial(attend_kernel, (own, last, cuts, q_bands...]
    unnamed x12 -> x0, local copies, waits for them, and re-layouts: 3.55 us -> none
    ppermute x4 -> x8, waiting for transfers between devices: 9.75 us -> 6.68 us  [the longest x4 6.67 us: swap_cores(): return lax.ppermute(x, 'core', [(0, 1), (1, 0)])]
    ppermute x4 -> x8, starting transfers between devices: 14.8 us -> 12.3 us  [the longest x4 10.3 us: from_tile(): lax.ppermute(x, ('x', 'core'), [(at(t), at(t + steps)) for t in range(8)...]
    pallas_call x4 -> x6, Pallas kernels: 10.3 us -> 8.58 us  [the longest x2 5.04 us: pack(): pl.pallas_call(kernel, grid_spec=pltpu.PrefetchScalarGridSpec(num_scalar_...]
  transfers between devices with their start and end apart: 5 -> 10, of which waited for: 3 -> 6; matrix products, arithmetic and copies ran while one was open for 1% -> 1% of each run, Pallas kernels for 20% -> 22%
where the time goes in v4:
time: 115 us; the launch traced here: 114 us
  Pallas kernels  34.2 us (30%)
  waiting for transfers between devices  31 us (27%)
  starting transfers between devices  27.3 us (24%)
  blocking collectives  20.4 us (18%)
    pallas_call x3, Pallas kernels, attend(): pl.pallas_call(functools.partial(attend_kernel, (own, last, cuts, q_bands...  25.6 us
    all_to_all x2, waiting for transfers between devices, exchange(): lax.all_to_all(x, PLANE, 0, 0, axis_index_groups=plane_groups(), tiled=True)  24.3 us
    all_to_all x1, blocking collectives, exchange(): lax.all_to_all(x, PLANE, 0, 0, axis_index_groups=plane_groups(), tiled=True)  20.4 us
    all_to_all x2, starting transfers between devices, exchange(): lax.all_to_all(x, PLANE, 0, 0, axis_index_groups=plane_groups(), tiled=True)  15 us
    ppermute x4, starting transfers between devices, from_tile(): lax.ppermute(x, ('x', 'core'), [(at(t), at(t + steps)) for t in range(8)...  10.3 us
    ppermute x4, waiting for transfers between devices, swap_cores(): return lax.ppermute(x, 'core', [(0, 1), (1, 0)])  6.67 us
    pallas_call x2, Pallas kernels, pack(): pl.pallas_call(kernel, grid_spec=pltpu.PrefetchScalarGridSpec(num_scalar_...  5.04 us
    pallas_call x3, Pallas kernels, assemble(): pl.pallas_call(kernel, in_specs=[pl.BlockSpec(memory_space=pltpu.VMEM)] *...  2.5 us
  transfers between devices with their start and end apart: 10, of which 6 were waited for; matrix products, arithmetic and copies ran while one was open for 1% of the time, Pallas kernels for 22%

profile of v4, /device:TPU:8, one launch (start us, length us, event | category | flops | bytes accessed | tf_op | source)
XLA Modules:
  0.0 114.0 jit_solution(17367670595568875928)
XLA Ops:
  0.0 2.3 %pack.3 = bf16[16,2,9,16,128]{4,3,2,1,0:T(8,128)(2,1)} custom-call(s32[1]{0:T(128)} %bitcast.core_ref, bf16[3,3,24,2048]{3,2,1,0:T(8,128)(2,1)} %refs_0_.1, bf16[3,3,24,2048]{3,2,1,0:T(8,128)(2,1)} %refs_1_.1), custom_call_target="tpu_custom_call" | custom-call | flops 2400000 | bytes 24000 | tf_op jit(solution)/shard_map/pack/pallas_call | solution.py:49
  2.3 8.4 %all-to-all-start = ((bf16[16,2,9,16,128]{4,3,2,1,0:T(8,128)(2,1)}), bf16[16,2,9,16,128]{4,3,2,1,0:T(8,128)(2,1)S(1)}, u32[]{:S(2)}, u32[]{:S(2)}) async-start(bf16[16,2,9,16,128]{4,3,2,1,0:T(8,128)(2,1)} %pack.3), calls=%async_computation | async-start | bytes 2359296 | tf_op jit(solution)/shard_map/all_to_all | solution.py:317
  10.7 2.7 %pack.2 = bf16[16,9,40,128]{3,2,1,0:T(8,128)(2,1)} custom-call(s32[1]{0:T(128)} %bitcast.core_ref, bf16[3,3,24,2048]{3,2,1,0:T(8,128)(2,1)} %refs_0_.1, bf16[3,3,24,2048]{3,2,1,0:T(8,128)(2,1)} %refs_1_.1, bf16[3,3,24,2048]{3,2,1,0:T(8,128)(2,1)} %query_ref.1), custom_call_target="tpu_custom_call" | custom-call | flops 3599999 | bytes 36000 | tf_op jit(solution)/shard_map/pack/pallas_call | solution.py:49
  13.5 13.8 %all-to-all-done.kept_ref = bf16[16,2,9,16,128]{4,3,2,1,0:T(8,128)(2,1)S(1)} async-done(((bf16[16,2,9,16,128]{4,3,2,1,0:T(8,128)(2,1)}), bf16[16,2,9,16,128]{4,3,2,1,0:T(8,128)(2,1)S(1)}, u32[]{:S(2)}, u32[]{:S(2)}) %all-to-all-start) | async-done | bytes 1179680 | tf_op jit(solution)/shard_map/all_to_all | solution.py:317
  27.2 6.6 %all-to-all-start.1 = ((bf16[16,9,40,128]{3,2,1,0:T(8,128)(2,1)}), bf16[16,9,40,128]{3,2,1,0:T(8,128)(2,1)S(1)}, u32[]{:S(2)}, u32[]{:S(2)}) async-start(bf16[16,9,40,128]{3,2,1,0:T(8,128)(2,1)} %pack.2), calls=%async_computation.1 | async-start | bytes 2949120 | tf_op jit(solution)/shard_map/all_to_all | solution.py:317
  34.0 2.0 %collective-permute-done.4.came_ref = bf16[8,2,9,16,128]{4,3,2,1,0:T(8,128)(2,1)S(1)} collective-permute-done((bf16[8,2,9,16,128]{4,3,2,1,0:T(8,128)(2,1)S(1)}, bf16[8,2,9,16,128]{4,3,2,1,0:T(8,128)(2,1)S(1)}, u32[]{:S(2)}, u32[]{:S(2)}) %collective-permute-start.4) | collective-permute-done | bytes 589856 | tf_op jit(solution)/shard_map/ppermute | solution.py:321
  36.0 1.2 %assemble.5.refs_1_ = bf16[2,2,3,384,128]{4,3,2,1,0:T(8,128)(2,1)} custom-call(bf16[16,2,9,16,128]{4,3,2,1,0:T(8,128)(2,1)S(1)} %all-to-all-done.kept_ref, bf16[8,2,9,16,128]{4,3,2,1,0:T(8,128)(2,1)S(1)} %collective-permute-done.4.came_ref), custom_call_target="tpu_custom_call" | custom-call | flops 1000000 | bytes 10000 | tf_op jit(solution)/shard_map/assemble/pallas_call | solution.py:118
  37.2 3.5 %collective-permute-start.5 = (bf16[2,2,3,384,128]{4,3,2,1,0:T(8,128)(2,1)}, bf16[2,2,3,384,128]{4,3,2,1,0:T(8,128)(2,1)S(1)}, u32[]{:S(2)}, u32[]{:S(2)}) collective-permute-start(bf16[2,2,3,384,128]{4,3,2,1,0:T(8,128)(2,1)} %assemble.5.refs_1_), channel_id=1, source_target_pairs={{0,16},{16,32},{32,48},{48,8},{8,24},{24,40},{40,56},{1,17},{17,33... | collective-permute-start | bytes 3538952 | tf_op jit(solution)/shard_map/ppermute | solution.py:326
  40.7 1.3 %collective-permute-start.6 = (bf16[2,2,3,384,128]{4,3,2,1,0:T(8,128)(2,1)}, bf16[2,2,3,384,128]{4,3,2,1,0:T(8,128)(2,1)}, u32[]{:S(2)}, u32[]{:S(2)}) collective-permute-start(bf16[2,2,3,384,128]{4,3,2,1,0:T(8,128)(2,1)} %assemble.5.refs_1_), channel_id=1, source_target_pairs={{16,0},{32,16},{48,32},{8,48},{24,8},{40,24},{56,40},{17,1},{33,17... | collective-permute-start | bytes 3538952 | tf_op jit(solution)/shard_map/ppermute | solution.py:326
  42.0 10.5 %all-to-all-done.1.kept_ref = bf16[16,9,40,128]{3,2,1,0:T(8,128)(2,1)S(1)} async-done(((bf16[16,9,40,128]{3,2,1,0:T(8,128)(2,1)}), bf16[16,9,40,128]{3,2,1,0:T(8,128)(2,1)S(1)}, u32[]{:S(2)}, u32[]{:S(2)}) %all-to-all-start.1) | async-done | bytes 1474592 | tf_op jit(solution)/shard_map/all_to_all | solution.py:317
  52.6 1.6 %collective-permute-done.1.came_ref = bf16[8,9,16,128]{3,2,1,0:T(8,128)(2,1)S(1)} collective-permute-done((bf16[8,9,16,128]{3,2,1,0:T(8,128)(2,1)S(1)}, bf16[8,9,16,128]{3,2,1,0:T(8,128)(2,1)S(1)}, u32[]{:S(2)}, u32[]{:S(2)}) %collective-permute-start.1) | collective-permute-done | bytes 294944 | tf_op jit(solution)/shard_map/ppermute | solution.py:321
  54.3 4.2 %collective-permute-start.2 = (bf16[2,1,3,384,128]{4,3,2,1,0:T(8,128)(2,1)S(1)}, bf16[2,1,3,384,128]{4,3,2,1,0:T(8,128)(2,1)}, u32[]{:S(2)}, u32[]{:S(2)}) collective-permute-start(bf16[2,1,3,384,128]{4,3,2,1,0:T(8,128)(2,1)S(1)} %assemble.4.refs_2_), channel_id=1, source_target_pairs={{0,16},{16,32},{32,48},{48,8},{8,24},{24,40},{40,56},{1,17},{17,33... | collective-permute-start | bytes 1769480 | tf_op jit(solution)/shard_map/ppermute | solution.py:326
  58.5 1.3 %collective-permute-start.3 = (bf16[2,1,3,384,128]{4,3,2,1,0:T(8,128)(2,1)S(1)}, bf16[2,1,3,384,128]{4,3,2,1,0:T(8,128)(2,1)}, u32[]{:S(2)}, u32[]{:S(2)}) collective-permute-start(bf16[2,1,3,384,128]{4,3,2,1,0:T(8,128)(2,1)S(1)} %assemble.4.refs_2_), channel_id=1, source_target_pairs={{16,0},{32,16},{48,32},{8,48},{24,8},{40,24},{56,40},{17,1},{33,17... | collective-permute-start | bytes 1769480 | tf_op jit(solution)/shard_map/ppermute | solution.py:326
  59.8 0.8 slice.12
  60.6 1.4 %collective-permute-start = (bf16[8,9,24,128]{3,2,1,0:T(8,128)(2,1)}, bf16[8,9,24,128]{3,2,1,0:T(8,128)(2,1)}, u32[]{:S(2)}, u32[]{:S(2)}) collective-permute-start(bf16[8,9,24,128]{3,2,1,0:T(8,128)(2,1)} %slice.12), channel_id=1, source_target_pairs={{0,8},{8,0},{1,9},{9,1},{2,10},{10,2},{3,11},{11,3},{4,12},{12,4},... | collective-permute-start | bytes 1327112 | tf_op jit(solution)/shard_map/ppermute | solution.py:321
  62.1 1.7 %collective-permute-done.came_ref = bf16[8,9,24,128]{3,2,1,0:T(8,128)(2,1)} collective-permute-done((bf16[8,9,24,128]{3,2,1,0:T(8,128)(2,1)}, bf16[8,9,24,128]{3,2,1,0:T(8,128)(2,1)}, u32[]{:S(2)}, u32[]{:S(2)}) %collective-permute-start) | collective-permute-done | bytes 442400 | tf_op jit(solution)/shard_map/ppermute | solution.py:321
  63.8 1.2 %assemble.3.refs_0_.refs_1_ = bf16[1,3,3,384,128]{4,3,2,1,0:T(8,128)(2,1)S(1)} custom-call(bf16[16,9,40,128]{3,2,1,0:T(8,128)(2,1)S(1)} %all-to-all-done.1.kept_ref, bf16[8,9,24,128]{3,2,1,0:T(8,128)(2,1)} %collective-permute-done.came_ref), custom_call_target="tpu_custom_call" | custom-call | flops 1000000 | bytes 10000 | tf_op jit(solution)/shard_map/assemble/pallas_call | solution.py:118
  64.9 9.5 %attend.3 = (f32[9,128,384]{2,1,0:T(8,128)S(1)}, f32[9,8,384]{2,1,0:T(8,128)S(1)}) custom-call(bf16[1,3,3,384,128]{4,3,2,1,0:T(8,128)(2,1)S(1)} %assemble.3.refs_0_.refs_1_, bf16[2,2,3,384,128]{4,3,2,1,0:T(8,128)(2,1)} %assemble.5.refs_1_, bf16[2,1,3,384,128]{4,3,2,1,0:T(8,128)(2,1)S(1)} %assemble.4.refs_2_), custom_call_target="tpu_custom_call" | custom-call | flops 9000000 | bytes 90000 | tf_op jit(solution)/shard_map/attend/pallas_call | solution.py:296
  74.5 10.7 %attend.4 = (f32[9,128,384]{2,1,0:T(8,128)S(1)}, f32[9,8,384]{2,1,0:T(8,128)S(1)}) custom-call(s32[2]{0:T(128)S(1)} %add_convert_fusion.refs_0_, bf16[1,3,3,384,128]{4,3,2,1,0:T(8,128)(2,1)S(1)} %assemble.3.refs_0_.refs_1_, bf16[2,2,3,384,128]{4,3,2,1,0:T(8,128)(2,1)S(1)} %collective-permute-done.5.refs_2_, ...), custom_call_target="tpu_custom_call" | custom-call | flops 10000000 | bytes 100000 | tf_op jit(solution)/shard_map/attend/pallas_call | solution.py:296
  85.2 5.4 %attend.5 = (bf16[8,9,24,128]{3,2,1,0:T(8,128)(2,1)S(1)}, bf16[8,9,24,128]{3,2,1,0:T(8,128)(2,1)S(1)}) custom-call(s32[2]{0:T(128)S(1)} %add_convert_fusion.refs_0_, bf16[1,3,3,384,128]{4,3,2,1,0:T(8,128)(2,1)S(1)} %assemble.3.refs_0_.refs_1_, bf16[2,1,3,384,128]{4,3,2,1,0:T(8,128)(2,1)} %collective-permute-done.2.refs_2_, ...), custom_call_target="tpu_custom_call" | custom-call | flops 5000000 | bytes 50000 | tf_op jit(solution)/shard_map/attend/pallas_call | solution.py:296
  90.6 0.5 collective-permute-start.7
  91.1 1.4 %collective-permute-done.7 = bf16[8,9,24,128]{3,2,1,0:T(8,128)(2,1)S(1)} collective-permute-done((bf16[8,9,24,128]{3,2,1,0:T(8,128)(2,1)S(1)}, bf16[8,9,24,128]{3,2,1,0:T(8,128)(2,1)S(1)}, u32[]{:S(2)}, u32[]{:S(2)}) %collective-permute-start.7) | collective-permute-done | bytes 442400 | tf_op jit(solution)/shard_map/ppermute | solution.py:321
  92.6 20.4 %all_to_all.15.x_ref = bf16[16,9,24,128]{3,2,1,0:T(8,128)(2,1)S(1)} all-to-all(bf16[16,9,24,128]{3,2,1,0:T(8,128)(2,1)S(1)} %pad_maximum_fusion), channel_id=1, replica_groups={{0,1,2,3,4,5,6,7,64,65,66,67,68,69,70,71},{72,73,74,75,76,77,78,79,8,9,..., dimensions={0} | all-to-all | bytes 1769472 | tf_op jit(solution)/shard_map/all_to_all | solution.py:317
  112.9 1.0 unpack.1
  (11 shorter events, 0.5 us)
Async XLA Ops:
  2.3 24.9 %all-to-all-start = ((bf16[16,2,9,16,128]{4,3,2,1,0:T(8,128)(2,1)}), bf16[16,2,9,16,128]{4,3,2,1,0:T(8,128)(2,1)S(1)}, u32[]{:S(2)}, u32[]{:S(2)}) async-start(bf16[16,2,9,16,128]{4,3,2,1,0:T(8,128)(2,1)} %pack.3), calls=%async_computation | async-start | bytes 2359296 | tf_op jit(solution)/shard_map/all_to_all | solution.py:317
  27.2 25.2 %all-to-all-start.1 = ((bf16[16,9,40,128]{3,2,1,0:T(8,128)(2,1)}), bf16[16,9,40,128]{3,2,1,0:T(8,128)(2,1)S(1)}, u32[]{:S(2)}, u32[]{:S(2)}) async-start(bf16[16,9,40,128]{3,2,1,0:T(8,128)(2,1)} %pack.2), calls=%async_computation.1 | async-start | bytes 2949120 | tf_op jit(solution)/shard_map/all_to_all | solution.py:317
  33.9 2.1 %collective-permute-start.4 = (bf16[8,2,9,16,128]{4,3,2,1,0:T(8,128)(2,1)S(1)}, bf16[8,2,9,16,128]{4,3,2,1,0:T(8,128)(2,1)S(1)}, u32[]{:S(2)}, u32[]{:S(2)}) collective-permute-start(bf16[8,2,9,16,128]{4,3,2,1,0:T(8,128)(2,1)S(1)} %slice.11), channel_id=1, source_target_pairs={{0,8},{8,0},{1,9},{9,1},{2,10},{10,2},{3,11},{11,3},{4,12},{12,4},... | collective-permute-start | bytes 1769480 | tf_op jit(solution)/shard_map/ppermute | solution.py:321
  37.2 37.3 %collective-permute-start.5 = (bf16[2,2,3,384,128]{4,3,2,1,0:T(8,128)(2,1)}, bf16[2,2,3,384,128]{4,3,2,1,0:T(8,128)(2,1)S(1)}, u32[]{:S(2)}, u32[]{:S(2)}) collective-permute-start(bf16[2,2,3,384,128]{4,3,2,1,0:T(8,128)(2,1)} %assemble.5.refs_1_), channel_id=1, source_target_pairs={{0,16},{16,32},{32,48},{48,8},{8,24},{24,40},{40,56},{1,17},{17,33... | collective-permute-start | bytes 3538952 | tf_op jit(solution)/shard_map/ppermute | solution.py:326
  40.7 33.8 %collective-permute-start.6 = (bf16[2,2,3,384,128]{4,3,2,1,0:T(8,128)(2,1)}, bf16[2,2,3,384,128]{4,3,2,1,0:T(8,128)(2,1)}, u32[]{:S(2)}, u32[]{:S(2)}) collective-permute-start(bf16[2,2,3,384,128]{4,3,2,1,0:T(8,128)(2,1)} %assemble.5.refs_1_), channel_id=1, source_target_pairs={{16,0},{32,16},{48,32},{8,48},{24,8},{40,24},{56,40},{17,1},{33,17... | collective-permute-start | bytes 3538952 | tf_op jit(solution)/shard_map/ppermute | solution.py:326
  52.5 1.7 %collective-permute-start.1 = (bf16[8,9,16,128]{3,2,1,0:T(8,128)(2,1)S(1)}, bf16[8,9,16,128]{3,2,1,0:T(8,128)(2,1)S(1)}, u32[]{:S(2)}, u32[]{:S(2)}) collective-permute-start(bf16[8,9,16,128]{3,2,1,0:T(8,128)(2,1)S(1)} %slice.13), channel_id=1, source_target_pairs={{0,8},{8,0},{1,9},{9,1},{2,10},{10,2},{3,11},{11,3},{4,12},{12,4},... | collective-permute-start | bytes 884744 | tf_op jit(solution)/shard_map/ppermute | solution.py:321
  54.3 30.9 %collective-permute-start.2 = (bf16[2,1,3,384,128]{4,3,2,1,0:T(8,128)(2,1)S(1)}, bf16[2,1,3,384,128]{4,3,2,1,0:T(8,128)(2,1)}, u32[]{:S(2)}, u32[]{:S(2)}) collective-permute-start(bf16[2,1,3,384,128]{4,3,2,1,0:T(8,128)(2,1)S(1)} %assemble.4.refs_2_), channel_id=1, source_target_pairs={{0,16},{16,32},{32,48},{48,8},{8,24},{24,40},{40,56},{1,17},{17,33... | collective-permute-start | bytes 1769480 | tf_op jit(solution)/shard_map/ppermute | solution.py:326
  58.5 26.7 %collective-permute-start.3 = (bf16[2,1,3,384,128]{4,3,2,1,0:T(8,128)(2,1)S(1)}, bf16[2,1,3,384,128]{4,3,2,1,0:T(8,128)(2,1)}, u32[]{:S(2)}, u32[]{:S(2)}) collective-permute-start(bf16[2,1,3,384,128]{4,3,2,1,0:T(8,128)(2,1)S(1)} %assemble.4.refs_2_), channel_id=1, source_target_pairs={{16,0},{32,16},{48,32},{8,48},{24,8},{40,24},{56,40},{17,1},{33,17... | collective-permute-start | bytes 1769480 | tf_op jit(solution)/shard_map/ppermute | solution.py:326
  60.6 3.2 %collective-permute-start = (bf16[8,9,24,128]{3,2,1,0:T(8,128)(2,1)}, bf16[8,9,24,128]{3,2,1,0:T(8,128)(2,1)}, u32[]{:S(2)}, u32[]{:S(2)}) collective-permute-start(bf16[8,9,24,128]{3,2,1,0:T(8,128)(2,1)} %slice.12), channel_id=1, source_target_pairs={{0,8},{8,0},{1,9},{9,1},{2,10},{10,2},{3,11},{11,3},{4,12},{12,4},... | collective-permute-start | bytes 1327112 | tf_op jit(solution)/shard_map/ppermute | solution.py:321
  90.6 1.9 %collective-permute-start.7 = (bf16[8,9,24,128]{3,2,1,0:T(8,128)(2,1)S(1)}, bf16[8,9,24,128]{3,2,1,0:T(8,128)(2,1)S(1)}, u32[]{:S(2)}, u32[]{:S(2)}) collective-permute-start(bf16[8,9,24,128]{3,2,1,0:T(8,128)(2,1)S(1)} %get-tuple-element.20), channel_id=1, source_target_pairs={{0,8},{8,0},{1,9},{9,1},{2,10},{10,2},{3,11},{11,3},{4,12},{12,4},... | collective-permute-start | bytes 1327112 | tf_op jit(solution)/shard_map/ppermute | solution.py:321

commit v5 on v4

--- a/solution.py
+++ b/solution.py
@@ -33,7 +33,7 @@
     o_ref = refs[-1]
     for n, x_ref in enumerate(refs[:-1]):
         for h in range(8):
-            o_ref[h, n] = x_ref[:, :, 0:16, h * HEAD_DIM : (h + 1) * HEAD_DIM].reshape(9, 16, HEAD_DIM)
+            o_ref[h, n] = x_ref[:, :, :, h * HEAD_DIM : (h + 1) * HEAD_DIM].reshape(9, 16, HEAD_DIM)
 
 
 def pack_second_kernel(core_ref, key_ref, value_ref, query_ref, o_ref):
@@ -45,13 +45,13 @@
             o_ref[h, n, 16:40] = query_ref[n // 3, n % 3, :, lanes]
 
 
-def pack(core, kernel, inner, *bands):
+def pack(core, kernel, columns, inner, *bands):
     return pl.pallas_call(
         kernel,
         grid_spec=pltpu.PrefetchScalarGridSpec(
             num_scalar_prefetch=1,
             grid=(2,),
-            in_specs=[pl.BlockSpec((3, 3, 24, 1024), lambda j, s: (0, 0, 0, (j + s[0]) % 2))] * len(bands),
+            in_specs=[pl.BlockSpec((3, 3, columns, 1024), lambda j, s: (0, 0, 0, (j + s[0]) % 2))] * len(bands),
             out_specs=pl.BlockSpec((8,) + inner, lambda j, s: (j,) + (0,) * len(inner)),
         ),
         out_shape=jax.ShapeDtypeStruct((HEADS,) + inner, BF16),
@@ -175,45 +175,59 @@
             for c in range(3):
                 acc_out[3 * b + c] = acc_in[3 * b + c]
                 row_out[3 * b + c] = row_in[3 * b + c]
-    for c in range(3):
+    accs, totals, tops = {}, {}, {}
+    tasks = [(c, bands, keys) for c in range(3) for bands, keys in groups(q_bands, k_bands)]
+    if not own:
+        for c in range(3):
+            for b in q_bands:
+                at = 3 * b + c
+                accs[b, c], totals[b, c], tops[b, c] = acc_in[at], row_in[at, 0:1], row_in[at, 1:2]
+
+    def first_stage(c, bands, keys):
+        cols = list(near(c))
+        places = [(p, side) for p in keys for side in range(sides)]
+        q = jnp.concatenate([q_ref[0, b, c] for b in bands], axis=0)
+        scores = lax.dot_general(run(0, places, cols), q, NT, preferred_element_type=F32)
+        for n, b in enumerate(bands):
+            if (b, c) not in tops:
+                mine = (places.index((b, 0)) * len(cols) + cols.index(c)) * BLOCK
+                mine = scores[mine : mine + BLOCK, n * BLOCK : (n + 1) * BLOCK]
+                tops[b, c] = jnp.max(mine, axis=0, keepdims=True) * SCORE_SCALE
+        return scores
+
+    def second_stage(c, bands, keys, scores):
         cols = list(near(c))
         wide = len(cols) * BLOCK
-        accs, totals, tops = {}, {}, {}
-        if not own:
-            for b in q_bands:
-                at = 3 * b + c
-                accs[b], totals[b], tops[b] = acc_in[at], row_in[at, 0:1], row_in[at, 1:2]
-        for bands, keys in groups(q_bands, k_bands):
-            places = [(p, side) for p in keys for side in range(sides)]
-            q = jnp.concatenate([q_ref[0, b, c] for b in bands], axis=0)
-            scores = lax.dot_general(run(0, places, cols), q, NT, preferred_element_type=F32)
-            for n, b in enumerate(bands):
-                if b not in tops:
-                    mine = (places.index((b, 0)) * len(cols) + cols.index(c)) * BLOCK
-                    mine = scores[mine : mine + BLOCK, n * BLOCK : (n + 1) * BLOCK]
-                    tops[b] = jnp.max(mine, axis=0, keepdims=True) * SCORE_SCALE
-            top = jnp.concatenate([tops[b] for b in bands], axis=1)
-            shifts = [top] if own else [top + (1 - flag_ref[side]).astype(F32) * 1e30 for side in range(sides)]
-            weights = jnp.concatenate(
-                [
-                    jnp.exp2(scores[n * wide : (n + 1) * wide] * SCORE_SCALE - shifts[side]).astype(BF16)
-                    for n, (p, side) in enumerate(places)
-                ],
-                axis=0,
-            )
-            values = run(1, places, cols)
-            values = jnp.concatenate([values.T, jnp.ones((16, values.shape[0]), BF16)], axis=0)
-            both = jnp.dot(values, weights, preferred_element_type=F32)
-            for n, b in enumerate(bands):
-                here = both[:, n * BLOCK : (n + 1) * BLOCK]
-                acc, total = here[:HEAD_DIM], here[HEAD_DIM : HEAD_DIM + 1]
-                accs[b] = accs[b] + acc if b in accs else acc
-                totals[b] = totals[b] + total if b in totals else total
+        places = [(p, side) for p in keys for side in range(sides)]
+        top = jnp.concatenate([tops[b, c] for b in bands], axis=1)
+        shifts = [top] if own else [top + (1 - flag_ref[side]).astype(F32) * 1e30 for side in range(sides)]
+        weights = jnp.concatenate(
+            [
+                jnp.exp2(scores[n * wide : (n + 1) * wide] * SCORE_SCALE - shifts[side]).astype(BF16)
+                for n, (p, side) in enumerate(places)
+            ],
+            axis=0,
+        )
+        values = run(1, places, cols)
+        values = jnp.concatenate([values.T, jnp.ones((16, values.shape[0]), BF16)], axis=0)
+        both = jnp.dot(values, weights, preferred_element_type=F32)
+        for n, b in enumerate(bands):
+            here = both[:, n * BLOCK : (n + 1) * BLOCK]
+            acc, total = here[:HEAD_DIM], here[HEAD_DIM : HEAD_DIM + 1]
+            accs[b, c] = accs[b, c] + acc if (b, c) in accs else acc
+            totals[b, c] = totals[b, c] + total if (b, c) in totals else total
+
+    scores = first_stage(*tasks[0])
+    for n, task in enumerate(tasks):
+        ahead = first_stage(*tasks[n + 1]) if n + 1 < len(tasks) else None
+        second_stage(*task, scores)
+        scores = ahead
+    for c in range(3):
         for b in q_bands:
             at = 3 * b + c
-            acc_out[at] = accs[b]
-            row_out[at] = jnp.concatenate([totals[b], tops[b], jnp.zeros((6, BLOCK), F32)], axis=0)
-            worst = jnp.maximum(worst, jnp.where(totals[b] < OVER, 0.0, 1.0))
+            acc_out[at] = accs[b, c]
+            row_out[at] = jnp.concatenate([totals[b, c], tops[b, c], jnp.zeros((6, BLOCK), F32)], axis=0)
+            worst = jnp.maximum(worst, jnp.where(totals[b, c] < OVER, 0.0, 1.0))
 
     @pl.when(jnp.max(worst) > 0.0)
     def _():
@@ -334,15 +348,17 @@
     core = core_index.reshape(1)
     tile = core_index * 4 + lax.axis_index("x").astype(jnp.int32)
     flags = jnp.stack([tile > 0, tile < 7]).astype(jnp.int32)
-    got = exchange(pack(core, pack_first_kernel, FIRST, key_band, value_band))
-    rest = pack(core, pack_second_kernel, SECOND, key_band, value_band, query_band)
+    got = exchange(pack(core, pack_first_kernel, 16, FIRST, key_band, value_band))
+    rest = pack(core, pack_second_kernel, 24, SECOND, key_band, value_band, query_band)
     rest, got = lax.optimization_barrier((rest, got))
     came = swap_cores(got[8:])
     got_rest = exchange(rest)
     (first,) = assemble(assemble_first_kernel, got, came, (2, 2))
     near_first = [from_tile(first, s) for s in (1, -1)]
-    (second,) = assemble(assemble_second_kernel, got_rest, swap_cores(got_rest[8:, :, :16]), (2, 1))
-    (queries,) = assemble(assemble_queries_kernel, got_rest, swap_cores(got_rest[8:, :, 16:]), (1, 3))
+    came_kv, came_q = (swap_cores(got_rest[8:, :, cut]) for cut in (slice(0, 16), slice(16, 40)))
+    (second,) = assemble(assemble_second_kernel, got_rest, came_kv, (2, 1))
+    (queries,) = assemble(assemble_queries_kernel, got_rest, came_q, (1, 3))
+    second, queries = lax.optimization_barrier((second, queries))
     near_second = [from_tile(second, s) for s in (1, -1)]
     state = attend(queries, [[first, second]], CUTS, us=9)
     state = attend(queries, [[a] for a in near_first], CUTS[:1], flags, state, us=10)

time: 115 us -> 113 us (0.983)
  Pallas kernels: 34.2 us -> 32.2 us
  waiting for transfers between devices: 31 us -> 32.5 us
    ppermute x4, waiting for transfers between devices: 0.01 us -> 3.82 us  [from_tile(): lax.ppermute(x, ('x', 'core'), [(at(t), at(t + steps)) for t in range(8)...]
    ppermute x4, waiting for transfers between devices: 6.67 us -> 5.37 us  [swap_cores(): return lax.ppermute(x, 'core', [(0, 1), (1, 0)])]
    ppermute x4, starting transfers between devices: 2.03 us -> 0.83 us  [swap_cores(): return lax.ppermute(x, 'core', [(0, 1), (1, 0)])]
  transfers between devices with their start and end apart: 10 -> 10, of which waited for: 6 -> 6; matrix products, arithmetic and copies ran while one was open for 1% -> 0% of each run, Pallas kernels for 22% -> 22%
where the time goes in v5:
time: 113 us
  waiting for transfers between devices  32.5 us (29%)
  Pallas kernels  32.2 us (28%)
  starting transfers between devices  26.2 us (23%)
  blocking collectives  21.1 us (19%)
    pallas_call x3, Pallas kernels, attend(): pl.pallas_call(functools.partial(attend_kernel, (own, last, cuts, q_bands...  24.8 us
    all_to_all x2, waiting for transfers between devices, exchange(): lax.all_to_all(x, PLANE, 0, 0, axis_index_groups=plane_groups(), tiled=True)  23.3 us
    all_to_all x1, blocking collectives, exchange(): lax.all_to_all(x, PLANE, 0, 0, axis_index_groups=plane_groups(), tiled=True)  21.1 us
    all_to_all x2, starting transfers between devices, exchange(): lax.all_to_all(x, PLANE, 0, 0, axis_index_groups=plane_groups(), tiled=True)  15 us
    ppermute x4, starting transfers between devices, from_tile(): lax.ppermute(x, ('x', 'core'), [(at(t), at(t + steps)) for t in range(8)...  10.4 us
    ppermute x4, waiting for transfers between devices, swap_cores(): return lax.ppermute(x, 'core', [(0, 1), (1, 0)])  5.37 us
    pallas_call x2, Pallas kernels, pack(): pl.pallas_call(kernel, grid_spec=pltpu.PrefetchScalarGridSpec(num_scalar_...  4.93 us
    ppermute x4, waiting for transfers between devices, from_tile(): lax.ppermute(x, ('x', 'core'), [(at(t), at(t + steps)) for t in range(8)...  3.82 us
  transfers between devices with their start and end apart: 10, of which 6 were waited for; matrix products, arithmetic and copies ran while one was open for 0% of the time, Pallas kernels for 22%

profile of v5, /device:TPU:8, one launch (start us, length us, event | category | flops | bytes accessed | tf_op | source)
XLA Modules:
  0.0 112.5 jit_solution(1281081071302044427)
XLA Ops:
  0.0 2.2 %pack.3 = bf16[16,2,9,16,128]{4,3,2,1,0:T(8,128)(2,1)} custom-call(s32[1]{0:T(128)} %bitcast.core_ref, bf16[3,3,24,2048]{3,2,1,0:T(8,128)(2,1)} %refs_0_.1, bf16[3,3,24,2048]{3,2,1,0:T(8,128)(2,1)} %refs_1_.1), custom_call_target="tpu_custom_call" | custom-call | flops 2400000 | bytes 24000 | tf_op jit(solution)/shard_map/pack/pallas_call | solution.py:49
  2.2 8.4 %all-to-all-start = ((bf16[16,2,9,16,128]{4,3,2,1,0:T(8,128)(2,1)}), bf16[16,2,9,16,128]{4,3,2,1,0:T(8,128)(2,1)S(1)}, u32[]{:S(2)}, u32[]{:S(2)}) async-start(bf16[16,2,9,16,128]{4,3,2,1,0:T(8,128)(2,1)} %pack.3), calls=%async_computation | async-start | bytes 2359296 | tf_op jit(solution)/shard_map/all_to_all | solution.py:331
  10.6 2.7 %pack.2 = bf16[16,9,40,128]{3,2,1,0:T(8,128)(2,1)} custom-call(s32[1]{0:T(128)} %bitcast.core_ref, bf16[3,3,24,2048]{3,2,1,0:T(8,128)(2,1)} %refs_0_.1, bf16[3,3,24,2048]{3,2,1,0:T(8,128)(2,1)} %refs_1_.1, bf16[3,3,24,2048]{3,2,1,0:T(8,128)(2,1)} %query_ref.1), custom_call_target="tpu_custom_call" | custom-call | flops 3599999 | bytes 36000 | tf_op jit(solution)/shard_map/pack/pallas_call | solution.py:49
  13.3 13.8 %all-to-all-done.kept_ref = bf16[16,2,9,16,128]{4,3,2,1,0:T(8,128)(2,1)S(1)} async-done(((bf16[16,2,9,16,128]{4,3,2,1,0:T(8,128)(2,1)}), bf16[16,2,9,16,128]{4,3,2,1,0:T(8,128)(2,1)S(1)}, u32[]{:S(2)}, u32[]{:S(2)}) %all-to-all-start) | async-done | bytes 1179680 | tf_op jit(solution)/shard_map/all_to_all | solution.py:331
  27.1 6.6 %all-to-all-start.1 = ((bf16[16,9,40,128]{3,2,1,0:T(8,128)(2,1)}), bf16[16,9,40,128]{3,2,1,0:T(8,128)(2,1)S(1)}, u32[]{:S(2)}, u32[]{:S(2)}) async-start(bf16[16,9,40,128]{3,2,1,0:T(8,128)(2,1)} %pack.2), calls=%async_computation.1 | async-start | bytes 2949120 | tf_op jit(solution)/shard_map/all_to_all | solution.py:331
  33.7 0.1 collective-permute-start.4
  33.8 2.0 %collective-permute-done.4.came_ref = bf16[8,2,9,16,128]{4,3,2,1,0:T(8,128)(2,1)S(1)} collective-permute-done((bf16[8,2,9,16,128]{4,3,2,1,0:T(8,128)(2,1)S(1)}, bf16[8,2,9,16,128]{4,3,2,1,0:T(8,128)(2,1)S(1)}, u32[]{:S(2)}, u32[]{:S(2)}) %collective-permute-start.4) | collective-permute-done | bytes 589856 | tf_op jit(solution)/shard_map/ppermute | solution.py:335
  35.8 1.2 %assemble.5.refs_1_ = bf16[2,2,3,384,128]{4,3,2,1,0:T(8,128)(2,1)} custom-call(bf16[16,2,9,16,128]{4,3,2,1,0:T(8,128)(2,1)S(1)} %all-to-all-done.kept_ref, bf16[8,2,9,16,128]{4,3,2,1,0:T(8,128)(2,1)S(1)} %collective-permute-done.4.came_ref), custom_call_target="tpu_custom_call" | custom-call | flops 1000000 | bytes 10000 | tf_op jit(solution)/shard_map/assemble/pallas_call | solution.py:118
  37.1 4.4 %collective-permute-start.5 = (bf16[2,2,3,384,128]{4,3,2,1,0:T(8,128)(2,1)}, bf16[2,2,3,384,128]{4,3,2,1,0:T(8,128)(2,1)}, u32[]{:S(2)}, u32[]{:S(2)}) collective-permute-start(bf16[2,2,3,384,128]{4,3,2,1,0:T(8,128)(2,1)} %assemble.5.refs_1_), channel_id=1, source_target_pairs={{0,16},{16,32},{32,48},{48,8},{8,24},{24,40},{40,56},{1,17},{17,33... | collective-permute-start | bytes 3538952 | tf_op jit(solution)/shard_map/ppermute | solution.py:340
  41.5 1.3 %collective-permute-start.6 = (bf16[2,2,3,384,128]{4,3,2,1,0:T(8,128)(2,1)}, bf16[2,2,3,384,128]{4,3,2,1,0:T(8,128)(2,1)}, u32[]{:S(2)}, u32[]{:S(2)}) collective-permute-start(bf16[2,2,3,384,128]{4,3,2,1,0:T(8,128)(2,1)} %assemble.5.refs_1_), channel_id=1, source_target_pairs={{16,0},{32,16},{48,32},{8,48},{24,8},{40,24},{56,40},{17,1},{33,17... | collective-permute-start | bytes 3538952 | tf_op jit(solution)/shard_map/ppermute | solution.py:340
  42.8 9.6 %all-to-all-done.1.kept_ref = bf16[16,9,40,128]{3,2,1,0:T(8,128)(2,1)S(1)} async-done(((bf16[16,9,40,128]{3,2,1,0:T(8,128)(2,1)}), bf16[16,9,40,128]{3,2,1,0:T(8,128)(2,1)S(1)}, u32[]{:S(2)}, u32[]{:S(2)}) %all-to-all-start.1) | async-done | bytes 1474592 | tf_op jit(solution)/shard_map/all_to_all | solution.py:331
  52.5 0.6 collective-permute-start
  53.1 1.6 %collective-permute-done.came_ref = bf16[8,9,16,128]{3,2,1,0:T(8,128)(2,1)S(1)} collective-permute-done((bf16[8,9,16,128]{3,2,1,0:T(8,128)(2,1)S(1)}, bf16[8,9,16,128]{3,2,1,0:T(8,128)(2,1)S(1)}, u32[]{:S(2)}, u32[]{:S(2)}) %collective-permute-start) | collective-permute-done | bytes 294944 | tf_op jit(solution)/shard_map/ppermute | solution.py:335
  54.7 0.1 assemble.3.refs_2_
  54.8 0.2 assemble.4.refs_0_.refs_1_
  55.0 3.4 %collective-permute-start.2 = (bf16[2,1,3,384,128]{4,3,2,1,0:T(8,128)(2,1)S(1)}, bf16[2,1,3,384,128]{4,3,2,1,0:T(8,128)(2,1)S(1)}, u32[]{:S(2)}, u32[]{:S(2)}) collective-permute-start(bf16[2,1,3,384,128]{4,3,2,1,0:T(8,128)(2,1)S(1)} %assemble.3.refs_2_), channel_id=1, source_target_pairs={{0,16},{16,32},{32,48},{48,8},{8,24},{24,40},{40,56},{1,17},{17,33... | collective-permute-start | bytes 1769480 | tf_op jit(solution)/shard_map/ppermute | solution.py:340
  58.4 1.3 %collective-permute-start.3 = (bf16[2,1,3,384,128]{4,3,2,1,0:T(8,128)(2,1)S(1)}, bf16[2,1,3,384,128]{4,3,2,1,0:T(8,128)(2,1)S(1)}, u32[]{:S(2)}, u32[]{:S(2)}) collective-permute-start(bf16[2,1,3,384,128]{4,3,2,1,0:T(8,128)(2,1)S(1)} %assemble.3.refs_2_), channel_id=1, source_target_pairs={{16,0},{32,16},{48,32},{8,48},{24,8},{40,24},{56,40},{17,1},{33,17... | collective-permute-start | bytes 1769480 | tf_op jit(solution)/shard_map/ppermute | solution.py:340
  59.8 9.0 %attend.3 = (f32[9,128,384]{2,1,0:T(8,128)S(1)}, f32[9,8,384]{2,1,0:T(8,128)S(1)}) custom-call(bf16[1,3,3,384,128]{4,3,2,1,0:T(8,128)(2,1)S(1)} %assemble.4.refs_0_.refs_1_, bf16[2,2,3,384,128]{4,3,2,1,0:T(8,128)(2,1)} %assemble.5.refs_1_, bf16[2,1,3,384,128]{4,3,2,1,0:T(8,128)(2,1)S(1)} %assemble.3.refs_2_), custom_call_target="tpu_custom_call" | custom-call | flops 9000000 | bytes 90000 | tf_op jit(solution)/shard_map/attend/pallas_call | solution.py:310
  68.8 3.8 %collective-permute-done.6.refs_3_ = bf16[2,2,3,384,128]{4,3,2,1,0:T(8,128)(2,1)} collective-permute-done((bf16[2,2,3,384,128]{4,3,2,1,0:T(8,128)(2,1)}, bf16[2,2,3,384,128]{4,3,2,1,0:T(8,128)(2,1)}, u32[]{:S(2)}, u32[]{:S(2)}) %collective-permute-start.6) | collective-permute-done | bytes 1179680 | tf_op jit(solution)/shard_map/ppermute | solution.py:340
  72.6 11.1 %attend.4 = (f32[9,128,384]{2,1,0:T(8,128)S(1)}, f32[9,8,384]{2,1,0:T(8,128)S(1)}) custom-call(s32[2]{0:T(128)S(1)} %add_convert_fusion.refs_0_, bf16[1,3,3,384,128]{4,3,2,1,0:T(8,128)(2,1)S(1)} %assemble.4.refs_0_.refs_1_, bf16[2,2,3,384,128]{4,3,2,1,0:T(8,128)(2,1)} %collective-permute-done.5.refs_2_, ...), custom_call_target="tpu_custom_call" | custom-call | flops 10000000 | bytes 100000 | tf_op jit(solution)/shard_map/attend/pallas_call | solution.py:310
  83.8 4.6 %attend.5 = (bf16[8,9,24,128]{3,2,1,0:T(8,128)(2,1)S(1)}, bf16[8,9,24,128]{3,2,1,0:T(8,128)(2,1)S(1)}) custom-call(s32[2]{0:T(128)S(1)} %add_convert_fusion.refs_0_, bf16[1,3,3,384,128]{4,3,2,1,0:T(8,128)(2,1)S(1)} %assemble.4.refs_0_.refs_1_, bf16[2,1,3,384,128]{4,3,2,1,0:T(8,128)(2,1)S(1)} %collective-permute-done.2.refs_2_, ...), custom_call_target="tpu_custom_call" | custom-call | flops 5000000 | bytes 50000 | tf_op jit(solution)/shard_map/attend/pallas_call | solution.py:310
  88.5 1.8 %collective-permute-done.7 = bf16[8,9,24,128]{3,2,1,0:T(8,128)(2,1)S(1)} collective-permute-done((bf16[8,9,24,128]{3,2,1,0:T(8,128)(2,1)S(1)}, bf16[8,9,24,128]{3,2,1,0:T(8,128)(2,1)S(1)}, u32[]{:S(2)}, u32[]{:S(2)}) %collective-permute-start.7) | collective-permute-done | bytes 442400 | tf_op jit(solution)/shard_map/ppermute | solution.py:335
  90.4 21.1 %all_to_all.15.x_ref = bf16[16,9,24,128]{3,2,1,0:T(8,128)(2,1)S(1)} all-to-all(bf16[16,9,24,128]{3,2,1,0:T(8,128)(2,1)S(1)} %pad_maximum_fusion), channel_id=1, replica_groups={{0,1,2,3,4,5,6,7,64,65,66,67,68,69,70,71},{72,73,74,75,76,77,78,79,8,9,..., dimensions={0} | all-to-all | bytes 1769472 | tf_op jit(solution)/shard_map/all_to_all | solution.py:331
  111.5 1.0 unpack.1
  (11 shorter events, 0.4 us)
Async XLA Ops:
  2.2 24.9 %all-to-all-start = ((bf16[16,2,9,16,128]{4,3,2,1,0:T(8,128)(2,1)}), bf16[16,2,9,16,128]{4,3,2,1,0:T(8,128)(2,1)S(1)}, u32[]{:S(2)}, u32[]{:S(2)}) async-start(bf16[16,2,9,16,128]{4,3,2,1,0:T(8,128)(2,1)} %pack.3), calls=%async_computation | async-start | bytes 2359296 | tf_op jit(solution)/shard_map/all_to_all | solution.py:331
  27.1 25.2 %all-to-all-start.1 = ((bf16[16,9,40,128]{3,2,1,0:T(8,128)(2,1)}), bf16[16,9,40,128]{3,2,1,0:T(8,128)(2,1)S(1)}, u32[]{:S(2)}, u32[]{:S(2)}) async-start(bf16[16,9,40,128]{3,2,1,0:T(8,128)(2,1)} %pack.2), calls=%async_computation.1 | async-start | bytes 2949120 | tf_op jit(solution)/shard_map/all_to_all | solution.py:331
  33.7 2.1 %collective-permute-start.4 = (bf16[8,2,9,16,128]{4,3,2,1,0:T(8,128)(2,1)S(1)}, bf16[8,2,9,16,128]{4,3,2,1,0:T(8,128)(2,1)S(1)}, u32[]{:S(2)}, u32[]{:S(2)}) collective-permute-start(bf16[8,2,9,16,128]{4,3,2,1,0:T(8,128)(2,1)S(1)} %slice.11), channel_id=1, source_target_pairs={{0,8},{8,0},{1,9},{9,1},{2,10},{10,2},{3,11},{11,3},{4,12},{12,4},... | collective-permute-start | bytes 1769480 | tf_op jit(solution)/shard_map/ppermute | solution.py:335
  37.1 31.7 %collective-permute-start.5 = (bf16[2,2,3,384,128]{4,3,2,1,0:T(8,128)(2,1)}, bf16[2,2,3,384,128]{4,3,2,1,0:T(8,128)(2,1)}, u32[]{:S(2)}, u32[]{:S(2)}) collective-permute-start(bf16[2,2,3,384,128]{4,3,2,1,0:T(8,128)(2,1)} %assemble.5.refs_1_), channel_id=1, source_target_pairs={{0,16},{16,32},{32,48},{48,8},{8,24},{24,40},{40,56},{1,17},{17,33... | collective-permute-start | bytes 3538952 | tf_op jit(solution)/shard_map/ppermute | solution.py:340
  41.5 31.1 %collective-permute-start.6 = (bf16[2,2,3,384,128]{4,3,2,1,0:T(8,128)(2,1)}, bf16[2,2,3,384,128]{4,3,2,1,0:T(8,128)(2,1)}, u32[]{:S(2)}, u32[]{:S(2)}) collective-permute-start(bf16[2,2,3,384,128]{4,3,2,1,0:T(8,128)(2,1)} %assemble.5.refs_1_), channel_id=1, source_target_pairs={{16,0},{32,16},{48,32},{8,48},{24,8},{40,24},{56,40},{17,1},{33,17... | collective-permute-start | bytes 3538952 | tf_op jit(solution)/shard_map/ppermute | solution.py:340
  52.4 2.4 %collective-permute-start.1 = (bf16[8,9,24,128]{3,2,1,0:T(8,128)(2,1)S(1)}, bf16[8,9,24,128]{3,2,1,0:T(8,128)(2,1)S(1)}, u32[]{:S(2)}, u32[]{:S(2)}) collective-permute-start(bf16[8,9,24,128]{3,2,1,0:T(8,128)(2,1)S(1)} %slice.13), channel_id=1, source_target_pairs={{0,8},{8,0},{1,9},{9,1},{2,10},{10,2},{3,11},{11,3},{4,12},{12,4},... | collective-permute-start | bytes 1327112 | tf_op jit(solution)/shard_map/ppermute | solution.py:335
  52.5 2.2 %collective-permute-start = (bf16[8,9,16,128]{3,2,1,0:T(8,128)(2,1)S(1)}, bf16[8,9,16,128]{3,2,1,0:T(8,128)(2,1)S(1)}, u32[]{:S(2)}, u32[]{:S(2)}) collective-permute-start(bf16[8,9,16,128]{3,2,1,0:T(8,128)(2,1)S(1)} %slice.12), channel_id=1, source_target_pairs={{0,8},{8,0},{1,9},{9,1},{2,10},{10,2},{3,11},{11,3},{4,12},{12,4},... | collective-permute-start | bytes 884744 | tf_op jit(solution)/shard_map/ppermute | solution.py:335
  55.0 28.8 %collective-permute-start.2 = (bf16[2,1,3,384,128]{4,3,2,1,0:T(8,128)(2,1)S(1)}, bf16[2,1,3,384,128]{4,3,2,1,0:T(8,128)(2,1)S(1)}, u32[]{:S(2)}, u32[]{:S(2)}) collective-permute-start(bf16[2,1,3,384,128]{4,3,2,1,0:T(8,128)(2,1)S(1)} %assemble.3.refs_2_), channel_id=1, source_target_pairs={{0,16},{16,32},{32,48},{48,8},{8,24},{24,40},{40,56},{1,17},{17,33... | collective-permute-start | bytes 1769480 | tf_op jit(solution)/shard_map/ppermute | solution.py:340
  58.4 25.4 %collective-permute-start.3 = (bf16[2,1,3,384,128]{4,3,2,1,0:T(8,128)(2,1)S(1)}, bf16[2,1,3,384,128]{4,3,2,1,0:T(8,128)(2,1)S(1)}, u32[]{:S(2)}, u32[]{:S(2)}) collective-permute-start(bf16[2,1,3,384,128]{4,3,2,1,0:T(8,128)(2,1)S(1)} %assemble.3.refs_2_), channel_id=1, source_target_pairs={{16,0},{32,16},{48,32},{8,48},{24,8},{40,24},{56,40},{17,1},{33,17... | collective-permute-start | bytes 1769480 | tf_op jit(solution)/shard_map/ppermute | solution.py:340
  88.4 1.9 %collective-permute-start.7 = (bf16[8,9,24,128]{3,2,1,0:T(8,128)(2,1)S(1)}, bf16[8,9,24,128]{3,2,1,0:T(8,128)(2,1)S(1)}, u32[]{:S(2)}, u32[]{:S(2)}) collective-permute-start(bf16[8,9,24,128]{3,2,1,0:T(8,128)(2,1)S(1)} %get-tuple-element.24), channel_id=1, source_target_pairs={{0,8},{8,0},{1,9},{9,1},{2,10},{10,2},{3,11},{11,3},{4,12},{12,4},... | collective-permute-start | bytes 1327112 | tf_op jit(solution)/shard_map/ppermute | solution.py:335

commit v6 on v5

--- a/solution.py
+++ b/solution.py
@@ -132,7 +132,7 @@
 
 def groups(q_bands, k_bands):
     if k_bands == [0, 1, 2]:
-        return [((0, 1), (0, 1)), ((1, 2), (2,)), ((2,), (1,))]
+        return [((0, 1), (0,)), ((0, 1, 2), (1,)), ((1, 2), (2,))]
     if k_bands == [0, 1]:
         return [((0, 1), (0, 1)), ((2,), (1,))]
     return [(tuple(q_bands), tuple(k_bands))]
@@ -190,7 +190,7 @@
         scores = lax.dot_general(run(0, places, cols), q, NT, preferred_element_type=F32)
         for n, b in enumerate(bands):
             if (b, c) not in tops:
-                mine = (places.index((b, 0)) * len(cols) + cols.index(c)) * BLOCK
+                mine = (places.index((keys[0], 0)) * len(cols) + cols.index(c)) * BLOCK
                 mine = scores[mine : mine + BLOCK, n * BLOCK : (n + 1) * BLOCK]
                 tops[b, c] = jnp.max(mine, axis=0, keepdims=True) * SCORE_SCALE
         return scores
@@ -277,7 +277,7 @@
 
     if last:
         for b in range(3):
-            tiles = [(acc_out[3 * c + b] / row_out[3 * c + b, 0:1]).T for c in range(3)]
+            tiles = [(acc_out[3 * c + b] * (1.0 / row_out[3 * c + b, 0:1])).T for c in range(3)]
             for half in range(2):
                 for f in range(3):
                     for n in range(8):

time: 113 us -> 140 us (1.24)
  Pallas kernels: 32.2 us -> 61.8 us
  waiting for transfers between devices: 32.5 us -> 28.4 us
  starting transfers between devices: 26.2 us -> 28.4 us
    pallas_call x3, Pallas kernels: 24.8 us -> 54.3 us  [attend(): pl.pallas_call(functools.partial(attend_kernel, (own, last, cuts, q_bands...]
    ppermute x4, waiting for transfers between devices: 3.82 us -> 0.01 us  [from_tile(): lax.ppermute(x, ('x', 'core'), [(at(t), at(t + steps)) for t in range(8)...]
    ppermute x4, starting transfers between devices: 0.83 us -> 3.01 us  [swap_cores(): return lax.ppermute(x, 'core', [(0, 1), (1, 0)])]
  transfers between devices with their start and end apart: 10 -> 10, of which waited for: 6 -> 5; matrix products, arithmetic and copies ran while one was open for 0% -> 0% of each run, Pallas kernels for 22% -> 39%
where the time goes in v6:
time: 140 us; the launch traced here: 139 us
  Pallas kernels  61.8 us (44%)
  starting transfers between devices  28.4 us (20%)
  waiting for transfers between devices  28.4 us (20%)
  blocking collectives  20.4 us (15%)
    pallas_call x3, Pallas kernels, attend(): pl.pallas_call(functools.partial(attend_kernel, (own, last, cuts, q_bands...  54.3 us
    all_to_all x2, waiting for transfers between devices, exchange(): lax.all_to_all(x, PLANE, 0, 0, axis_index_groups=plane_groups(), tiled=True)  23.3 us
    all_to_all x1, blocking collectives, exchange(): lax.all_to_all(x, PLANE, 0, 0, axis_index_groups=plane_groups(), tiled=True)  20.4 us
    all_to_all x2, starting transfers between devices, exchange(): lax.all_to_all(x, PLANE, 0, 0, axis_index_groups=plane_groups(), tiled=True)  15 us
    ppermute x4, starting transfers between devices, from_tile(): lax.ppermute(x, ('x', 'core'), [(at(t), at(t + steps)) for t in range(8)...  10.4 us
    ppermute x4, waiting for transfers between devices, swap_cores(): return lax.ppermute(x, 'core', [(0, 1), (1, 0)])  5.01 us
    pallas_call x2, Pallas kernels, pack(): pl.pallas_call(kernel, grid_spec=pltpu.PrefetchScalarGridSpec(num_scalar_...  4.93 us
    ppermute x4, starting transfers between devices, swap_cores(): return lax.ppermute(x, 'core', [(0, 1), (1, 0)])  3.01 us
  transfers between devices with their start and end apart: 10, of which 5 were waited for; matrix products, arithmetic and copies ran while one was open for 0% of the time, Pallas kernels for 39%

profile of v6, /device:TPU:8, one launch (start us, length us, event | category | flops | bytes accessed | tf_op | source)
XLA Modules:
  0.0 139.3 jit_solution(9880011084928386653)
XLA Ops:
  0.0 2.2 %pack.3 = bf16[16,2,9,16,128]{4,3,2,1,0:T(8,128)(2,1)} custom-call(s32[1]{0:T(128)} %bitcast.core_ref, bf16[3,3,24,2048]{3,2,1,0:T(8,128)(2,1)} %refs_0_.1, bf16[3,3,24,2048]{3,2,1,0:T(8,128)(2,1)} %refs_1_.1), custom_call_target="tpu_custom_call" | custom-call | flops 2400000 | bytes 24000 | tf_op jit(solution)/shard_map/pack/pallas_call | solution.py:49
  2.2 8.4 %all-to-all-start = ((bf16[16,2,9,16,128]{4,3,2,1,0:T(8,128)(2,1)}), bf16[16,2,9,16,128]{4,3,2,1,0:T(8,128)(2,1)S(1)}, u32[]{:S(2)}, u32[]{:S(2)}) async-start(bf16[16,2,9,16,128]{4,3,2,1,0:T(8,128)(2,1)} %pack.3), calls=%async_computation | async-start | bytes 2359296 | tf_op jit(solution)/shard_map/all_to_all | solution.py:331
  10.6 2.7 %pack.2 = bf16[16,9,40,128]{3,2,1,0:T(8,128)(2,1)} custom-call(s32[1]{0:T(128)} %bitcast.core_ref, bf16[3,3,24,2048]{3,2,1,0:T(8,128)(2,1)} %refs_0_.1, bf16[3,3,24,2048]{3,2,1,0:T(8,128)(2,1)} %refs_1_.1, bf16[3,3,24,2048]{3,2,1,0:T(8,128)(2,1)} %query_ref.1), custom_call_target="tpu_custom_call" | custom-call | flops 3599999 | bytes 36000 | tf_op jit(solution)/shard_map/pack/pallas_call | solution.py:49
  13.3 13.8 %all-to-all-done.kept_ref = bf16[16,2,9,16,128]{4,3,2,1,0:T(8,128)(2,1)S(1)} async-done(((bf16[16,2,9,16,128]{4,3,2,1,0:T(8,128)(2,1)}), bf16[16,2,9,16,128]{4,3,2,1,0:T(8,128)(2,1)S(1)}, u32[]{:S(2)}, u32[]{:S(2)}) %all-to-all-start) | async-done | bytes 1179680 | tf_op jit(solution)/shard_map/all_to_all | solution.py:331
  27.1 6.6 %all-to-all-start.1 = ((bf16[16,9,40,128]{3,2,1,0:T(8,128)(2,1)}), bf16[16,9,40,128]{3,2,1,0:T(8,128)(2,1)S(1)}, u32[]{:S(2)}, u32[]{:S(2)}) async-start(bf16[16,9,40,128]{3,2,1,0:T(8,128)(2,1)} %pack.2), calls=%async_computation.1 | async-start | bytes 2949120 | tf_op jit(solution)/shard_map/all_to_all | solution.py:331
  33.7 0.1 collective-permute-start.4
  33.8 2.0 %collective-permute-done.4.came_ref = bf16[8,2,9,16,128]{4,3,2,1,0:T(8,128)(2,1)S(1)} collective-permute-done((bf16[8,2,9,16,128]{4,3,2,1,0:T(8,128)(2,1)S(1)}, bf16[8,2,9,16,128]{4,3,2,1,0:T(8,128)(2,1)S(1)}, u32[]{:S(2)}, u32[]{:S(2)}) %collective-permute-start.4) | collective-permute-done | bytes 589856 | tf_op jit(solution)/shard_map/ppermute | solution.py:335
  35.8 1.2 assemble.5.refs_1_
  37.1 4.4 %collective-permute-start.5 = (bf16[2,2,3,384,128]{4,3,2,1,0:T(8,128)(2,1)}, bf16[2,2,3,384,128]{4,3,2,1,0:T(8,128)(2,1)}, u32[]{:S(2)}, u32[]{:S(2)}) collective-permute-start(bf16[2,2,3,384,128]{4,3,2,1,0:T(8,128)(2,1)} %assemble.5.refs_1_), channel_id=1, source_target_pairs={{0,16},{16,32},{32,48},{48,8},{8,24},{24,40},{40,56},{1,17},{17,33... | collective-permute-start | bytes 3538952 | tf_op jit(solution)/shard_map/ppermute | solution.py:340
  41.5 1.3 collective-permute-start.6
  42.8 9.6 %all-to-all-done.1.kept_ref = bf16[16,9,40,128]{3,2,1,0:T(8,128)(2,1)S(1)} async-done(((bf16[16,9,40,128]{3,2,1,0:T(8,128)(2,1)}), bf16[16,9,40,128]{3,2,1,0:T(8,128)(2,1)S(1)}, u32[]{:S(2)}, u32[]{:S(2)}) %all-to-all-start.1) | async-done | bytes 1474592 | tf_op jit(solution)/shard_map/all_to_all | solution.py:331
  52.5 0.6 collective-permute-start
  53.1 1.6 %collective-permute-done.came_ref = bf16[8,9,16,128]{3,2,1,0:T(8,128)(2,1)S(1)} collective-permute-done((bf16[8,9,16,128]{3,2,1,0:T(8,128)(2,1)S(1)}, bf16[8,9,16,128]{3,2,1,0:T(8,128)(2,1)S(1)}, u32[]{:S(2)}, u32[]{:S(2)}) %collective-permute-start) | collective-permute-done | bytes 294944 | tf_op jit(solution)/shard_map/ppermute | solution.py:335
  54.7 0.1 assemble.3.refs_2_
  54.8 0.2 assemble.4.refs_0_.refs_1_
  55.0 3.4 %collective-permute-start.2 = (bf16[2,1,3,384,128]{4,3,2,1,0:T(8,128)(2,1)S(1)}, bf16[2,1,3,384,128]{4,3,2,1,0:T(8,128)(2,1)S(1)}, u32[]{:S(2)}, u32[]{:S(2)}) collective-permute-start(bf16[2,1,3,384,128]{4,3,2,1,0:T(8,128)(2,1)S(1)} %assemble.3.refs_2_), channel_id=1, source_target_pairs={{0,16},{16,32},{32,48},{48,8},{8,24},{24,40},{40,56},{1,17},{17,33... | collective-permute-start | bytes 1769480 | tf_op jit(solution)/shard_map/ppermute | solution.py:340
  58.4 1.3 collective-permute-start.3
  59.8 38.5 %attend.3 = (f32[9,128,384]{2,1,0:T(8,128)S(1)}, f32[9,8,384]{2,1,0:T(8,128)S(1)}) custom-call(bf16[1,3,3,384,128]{4,3,2,1,0:T(8,128)(2,1)S(1)} %assemble.4.refs_0_.refs_1_, bf16[2,2,3,384,128]{4,3,2,1,0:T(8,128)(2,1)} %assemble.5.refs_1_, bf16[2,1,3,384,128]{4,3,2,1,0:T(8,128)(2,1)S(1)} %assemble.3.refs_2_), custom_call_target="tpu_custom_call" | custom-call | flops 9000000 | bytes 90000 | tf_op jit(solution)/shard_map/attend/pallas_call | solution.py:310
  98.3 11.1 %attend.4 = (f32[9,128,384]{2,1,0:T(8,128)S(1)}, f32[9,8,384]{2,1,0:T(8,128)S(1)}) custom-call(s32[2]{0:T(128)S(1)} %add_convert_fusion.refs_0_, bf16[1,3,3,384,128]{4,3,2,1,0:T(8,128)(2,1)S(1)} %assemble.4.refs_0_.refs_1_, bf16[2,2,3,384,128]{4,3,2,1,0:T(8,128)(2,1)} %collective-permute-done.5.refs_2_, ...), custom_call_target="tpu_custom_call" | custom-call | flops 10000000 | bytes 100000 | tf_op jit(solution)/shard_map/attend/pallas_call | solution.py:310
  109.5 4.6 %attend.5 = (bf16[8,9,24,128]{3,2,1,0:T(8,128)(2,1)S(1)}, bf16[8,9,24,128]{3,2,1,0:T(8,128)(2,1)S(1)}) custom-call(s32[2]{0:T(128)S(1)} %add_convert_fusion.refs_0_, bf16[1,3,3,384,128]{4,3,2,1,0:T(8,128)(2,1)S(1)} %assemble.4.refs_0_.refs_1_, bf16[2,1,3,384,128]{4,3,2,1,0:T(8,128)(2,1)S(1)} %collective-permute-done.2.refs_2_, ...), custom_call_target="tpu_custom_call" | custom-call | flops 5000000 | bytes 50000 | tf_op jit(solution)/shard_map/attend/pallas_call | solution.py:310
  114.2 2.3 %collective-permute-start.7 = (bf16[8,9,24,128]{3,2,1,0:T(8,128)(2,1)S(1)}, bf16[8,9,24,128]{3,2,1,0:T(8,128)(2,1)S(1)}, u32[]{:S(2)}, u32[]{:S(2)}) collective-permute-start(bf16[8,9,24,128]{3,2,1,0:T(8,128)(2,1)S(1)} %get-tuple-element.24), channel_id=1, source_target_pairs={{0,8},{8,0},{1,9},{9,1},{2,10},{10,2},{3,11},{11,3},{4,12},{12,4},... | collective-permute-start | bytes 1327112 | tf_op jit(solution)/shard_map/ppermute | solution.py:335
  116.4 1.4 %collective-permute-done.7 = bf16[8,9,24,128]{3,2,1,0:T(8,128)(2,1)S(1)} collective-permute-done((bf16[8,9,24,128]{3,2,1,0:T(8,128)(2,1)S(1)}, bf16[8,9,24,128]{3,2,1,0:T(8,128)(2,1)S(1)}, u32[]{:S(2)}, u32[]{:S(2)}) %collective-permute-start.7) | collective-permute-done | bytes 442400 | tf_op jit(solution)/shard_map/ppermute | solution.py:335
  117.9 20.4 %all_to_all.15.x_ref = bf16[16,9,24,128]{3,2,1,0:T(8,128)(2,1)S(1)} all-to-all(bf16[16,9,24,128]{3,2,1,0:T(8,128)(2,1)S(1)} %pad_maximum_fusion), channel_id=1, replica_groups={{0,1,2,3,4,5,6,7,64,65,66,67,68,69,70,71},{72,73,74,75,76,77,78,79,8,9,..., dimensions={0} | all-to-all | bytes 1769472 | tf_op jit(solution)/shard_map/all_to_all | solution.py:331
  138.3 1.0 unpack.1
  (11 shorter events, 0.4 us)
Async XLA Ops:
  2.2 24.9 %all-to-all-start = ((bf16[16,2,9,16,128]{4,3,2,1,0:T(8,128)(2,1)}), bf16[16,2,9,16,128]{4,3,2,1,0:T(8,128)(2,1)S(1)}, u32[]{:S(2)}, u32[]{:S(2)}) async-start(bf16[16,2,9,16,128]{4,3,2,1,0:T(8,128)(2,1)} %pack.3), calls=%async_computation | async-start | bytes 2359296 | tf_op jit(solution)/shard_map/all_to_all | solution.py:331
  27.1 25.2 %all-to-all-start.1 = ((bf16[16,9,40,128]{3,2,1,0:T(8,128)(2,1)}), bf16[16,9,40,128]{3,2,1,0:T(8,128)(2,1)S(1)}, u32[]{:S(2)}, u32[]{:S(2)}) async-start(bf16[16,9,40,128]{3,2,1,0:T(8,128)(2,1)} %pack.2), calls=%async_computation.1 | async-start | bytes 2949120 | tf_op jit(solution)/shard_map/all_to_all | solution.py:331
  33.7 2.1 %collective-permute-start.4 = (bf16[8,2,9,16,128]{4,3,2,1,0:T(8,128)(2,1)S(1)}, bf16[8,2,9,16,128]{4,3,2,1,0:T(8,128)(2,1)S(1)}, u32[]{:S(2)}, u32[]{:S(2)}) collective-permute-start(bf16[8,2,9,16,128]{4,3,2,1,0:T(8,128)(2,1)S(1)} %slice.11), channel_id=1, source_target_pairs={{0,8},{8,0},{1,9},{9,1},{2,10},{10,2},{3,11},{11,3},{4,12},{12,4},... | collective-permute-start | bytes 1769480 | tf_op jit(solution)/shard_map/ppermute | solution.py:335
  37.1 61.3 %collective-permute-start.5 = (bf16[2,2,3,384,128]{4,3,2,1,0:T(8,128)(2,1)}, bf16[2,2,3,384,128]{4,3,2,1,0:T(8,128)(2,1)}, u32[]{:S(2)}, u32[]{:S(2)}) collective-permute-start(bf16[2,2,3,384,128]{4,3,2,1,0:T(8,128)(2,1)} %assemble.5.refs_1_), channel_id=1, source_target_pairs={{0,16},{16,32},{32,48},{48,8},{8,24},{24,40},{40,56},{1,17},{17,33... | collective-permute-start | bytes 3538952 | tf_op jit(solution)/shard_map/ppermute | solution.py:340
  41.5 56.8 %collective-permute-start.6 = (bf16[2,2,3,384,128]{4,3,2,1,0:T(8,128)(2,1)}, bf16[2,2,3,384,128]{4,3,2,1,0:T(8,128)(2,1)}, u32[]{:S(2)}, u32[]{:S(2)}) collective-permute-start(bf16[2,2,3,384,128]{4,3,2,1,0:T(8,128)(2,1)} %assemble.5.refs_1_), channel_id=1, source_target_pairs={{16,0},{32,16},{48,32},{8,48},{24,8},{40,24},{56,40},{17,1},{33,17... | collective-permute-start | bytes 3538952 | tf_op jit(solution)/shard_map/ppermute | solution.py:340
  52.4 2.4 %collective-permute-start.1 = (bf16[8,9,24,128]{3,2,1,0:T(8,128)(2,1)S(1)}, bf16[8,9,24,128]{3,2,1,0:T(8,128)(2,1)S(1)}, u32[]{:S(2)}, u32[]{:S(2)}) collective-permute-start(bf16[8,9,24,128]{3,2,1,0:T(8,128)(2,1)S(1)} %slice.13), channel_id=1, source_target_pairs={{0,8},{8,0},{1,9},{9,1},{2,10},{10,2},{3,11},{11,3},{4,12},{12,4},... | collective-permute-start | bytes 1327112 | tf_op jit(solution)/shard_map/ppermute | solution.py:335
  52.5 2.2 %collective-permute-start = (bf16[8,9,16,128]{3,2,1,0:T(8,128)(2,1)S(1)}, bf16[8,9,16,128]{3,2,1,0:T(8,128)(2,1)S(1)}, u32[]{:S(2)}, u32[]{:S(2)}) collective-permute-start(bf16[8,9,16,128]{3,2,1,0:T(8,128)(2,1)S(1)} %slice.12), channel_id=1, source_target_pairs={{0,8},{8,0},{1,9},{9,1},{2,10},{10,2},{3,11},{11,3},{4,12},{12,4},... | collective-permute-start | bytes 884744 | tf_op jit(solution)/shard_map/ppermute | solution.py:335
  55.0 54.5 %collective-permute-start.2 = (bf16[2,1,3,384,128]{4,3,2,1,0:T(8,128)(2,1)S(1)}, bf16[2,1,3,384,128]{4,3,2,1,0:T(8,128)(2,1)S(1)}, u32[]{:S(2)}, u32[]{:S(2)}) collective-permute-start(bf16[2,1,3,384,128]{4,3,2,1,0:T(8,128)(2,1)S(1)} %assemble.3.refs_2_), channel_id=1, source_target_pairs={{0,16},{16,32},{32,48},{48,8},{8,24},{24,40},{40,56},{1,17},{17,33... | collective-permute-start | bytes 1769480 | tf_op jit(solution)/shard_map/ppermute | solution.py:340
  58.4 51.1 %collective-permute-start.3 = (bf16[2,1,3,384,128]{4,3,2,1,0:T(8,128)(2,1)S(1)}, bf16[2,1,3,384,128]{4,3,2,1,0:T(8,128)(2,1)S(1)}, u32[]{:S(2)}, u32[]{:S(2)}) collective-permute-start(bf16[2,1,3,384,128]{4,3,2,1,0:T(8,128)(2,1)S(1)} %assemble.3.refs_2_), channel_id=1, source_target_pairs={{16,0},{32,16},{48,32},{8,48},{24,8},{40,24},{56,40},{17,1},{33,17... | collective-permute-start | bytes 1769480 | tf_op jit(solution)/shard_map/ppermute | solution.py:340
  114.2 3.7 %collective-permute-start.7 = (bf16[8,9,24,128]{3,2,1,0:T(8,128)(2,1)S(1)}, bf16[8,9,24,128]{3,2,1,0:T(8,128)(2,1)S(1)}, u32[]{:S(2)}, u32[]{:S(2)}) collective-permute-start(bf16[8,9,24,128]{3,2,1,0:T(8,128)(2,1)S(1)} %get-tuple-element.24), channel_id=1, source_target_pairs={{0,8},{8,0},{1,9},{9,1},{2,10},{10,2},{3,11},{11,3},{4,12},{12,4},... | collective-permute-start | bytes 1327112 | tf_op jit(solution)/shard_map/ppermute | solution.py:335

commit v7 on v5

--- a/solution.py
+++ b/solution.py
@@ -121,7 +121,7 @@
         out_specs=[pl.BlockSpec(memory_space=pltpu.VMEM)] * len(leads),
         out_shape=[jax.ShapeDtypeStruct(lead + (3, BLOCK, HEAD_DIM), BF16) for lead in leads],
         compiler_params=params(8),
-        cost_estimate=cost(1),
+        cost_estimate=cost(16000) if kernel is assemble_first_kernel else cost(1),
         name="assemble",
     )(got, came)
 
@@ -277,7 +277,7 @@
 
     if last:
         for b in range(3):
-            tiles = [(acc_out[3 * c + b] / row_out[3 * c + b, 0:1]).T for c in range(3)]
+            tiles = [(acc_out[3 * c + b] * (1.0 / row_out[3 * c + b, 0:1])).T for c in range(3)]
             for half in range(2):
                 for f in range(3):
                     for n in range(8):

time: 113 us -> 114 us (level)
  starting transfers between devices: 26.2 us -> 28.3 us
  waiting for transfers between devices: 32.5 us -> 30.6 us
    all_to_all x2, waiting for transfers between devices: 23.3 us -> 27.5 us  [exchange(): lax.all_to_all(x, PLANE, 0, 0, axis_index_groups=plane_groups(), tiled=True)]
    ppermute x4, waiting for transfers between devices: 3.82 us -> 0.01 us  [from_tile(): lax.ppermute(x, ('x', 'core'), [(at(t), at(t + steps)) for t in range(8)...]
    ppermute x4, waiting for transfers between devices: 5.37 us -> 3.03 us  [swap_cores(): return lax.ppermute(x, 'core', [(0, 1), (1, 0)])]
    ppermute x4, starting transfers between devices: 0.83 us -> 2.92 us  [swap_cores(): return lax.ppermute(x, 'core', [(0, 1), (1, 0)])]
  transfers between devices with their start and end apart: 10 -> 10, of which waited for: 6 -> 4; matrix products, arithmetic and copies ran while one was open for 0% -> 0% of each run, Pallas kernels for 22% -> 22%
where the time goes in v7:
time: 114 us; the launch traced here: 113 us
  Pallas kernels  32.2 us (28%)
  waiting for transfers between devices  30.6 us (27%)
  starting transfers between devices  28.3 us (25%)
  blocking collectives  20.5 us (18%)
    all_to_all x2, waiting for transfers between devices, exchange(): lax.all_to_all(x, PLANE, 0, 0, axis_index_groups=plane_groups(), tiled=True)  27.5 us
    pallas_call x3, Pallas kernels, attend(): pl.pallas_call(functools.partial(attend_kernel, (own, last, cuts, q_bands...  24.8 us
    all_to_all x1, blocking collectives, exchange(): lax.all_to_all(x, PLANE, 0, 0, axis_index_groups=plane_groups(), tiled=True)  20.5 us
    all_to_all x2, starting transfers between devices, exchange(): lax.all_to_all(x, PLANE, 0, 0, axis_index_groups=plane_groups(), tiled=True)  15 us
    ppermute x4, starting transfers between devices, from_tile(): lax.ppermute(x, ('x', 'core'), [(at(t), at(t + steps)) for t in range(8)...  10.4 us
    pallas_call x2, Pallas kernels, pack(): pl.pallas_call(kernel, grid_spec=pltpu.PrefetchScalarGridSpec(num_scalar_...  4.93 us
    ppermute x4, waiting for transfers between devices, swap_cores(): return lax.ppermute(x, 'core', [(0, 1), (1, 0)])  3.03 us
    ppermute x4, starting transfers between devices, swap_cores(): return lax.ppermute(x, 'core', [(0, 1), (1, 0)])  2.92 us
  transfers between devices with their start and end apart: 10, of which 4 were waited for; matrix products, arithmetic and copies ran while one was open for 0% of the time, Pallas kernels for 22%

profile of v7, /device:TPU:8, one launch (start us, length us, event | category | flops | bytes accessed | tf_op | source)
XLA Modules:
  0.0 112.9 jit_solution(9498207030027749372)
XLA Ops:
  0.0 2.2 %pack.3 = bf16[16,2,9,16,128]{4,3,2,1,0:T(8,128)(2,1)} custom-call(s32[1]{0:T(128)} %bitcast.core_ref, bf16[3,3,24,2048]{3,2,1,0:T(8,128)(2,1)} %refs_0_.1, bf16[3,3,24,2048]{3,2,1,0:T(8,128)(2,1)} %refs_1_.1), custom_call_target="tpu_custom_call" | custom-call | flops 2400000 | bytes 24000 | tf_op jit(solution)/shard_map/pack/pallas_call | solution.py:49
  2.2 8.4 %all-to-all-start = ((bf16[16,2,9,16,128]{4,3,2,1,0:T(8,128)(2,1)}), bf16[16,2,9,16,128]{4,3,2,1,0:T(8,128)(2,1)S(1)}, u32[]{:S(2)}, u32[]{:S(2)}) async-start(bf16[16,2,9,16,128]{4,3,2,1,0:T(8,128)(2,1)} %pack.3), calls=%async_computation | async-start | bytes 2359296 | tf_op jit(solution)/shard_map/all_to_all | solution.py:331
  10.6 2.7 %pack.2 = bf16[16,9,40,128]{3,2,1,0:T(8,128)(2,1)} custom-call(s32[1]{0:T(128)} %bitcast.core_ref, bf16[3,3,24,2048]{3,2,1,0:T(8,128)(2,1)} %refs_0_.1, bf16[3,3,24,2048]{3,2,1,0:T(8,128)(2,1)} %refs_1_.1, bf16[3,3,24,2048]{3,2,1,0:T(8,128)(2,1)} %query_ref.1), custom_call_target="tpu_custom_call" | custom-call | flops 3599999 | bytes 36000 | tf_op jit(solution)/shard_map/pack/pallas_call | solution.py:49
  13.3 13.8 %all-to-all-done.kept_ref = bf16[16,2,9,16,128]{4,3,2,1,0:T(8,128)(2,1)S(1)} async-done(((bf16[16,2,9,16,128]{4,3,2,1,0:T(8,128)(2,1)}), bf16[16,2,9,16,128]{4,3,2,1,0:T(8,128)(2,1)S(1)}, u32[]{:S(2)}, u32[]{:S(2)}) %all-to-all-start) | async-done | bytes 1179680 | tf_op jit(solution)/shard_map/all_to_all | solution.py:331
  27.1 0.9 slice.11
  28.0 6.6 %all-to-all-start.1 = ((bf16[16,9,40,128]{3,2,1,0:T(8,128)(2,1)}), bf16[16,9,40,128]{3,2,1,0:T(8,128)(2,1)S(1)}, u32[]{:S(2)}, u32[]{:S(2)}) async-start(bf16[16,9,40,128]{3,2,1,0:T(8,128)(2,1)} %pack.2), calls=%async_computation.1 | async-start | bytes 2949120 | tf_op jit(solution)/shard_map/all_to_all | solution.py:331
  34.6 1.2 %assemble.5.refs_1_ = bf16[2,2,3,384,128]{4,3,2,1,0:T(8,128)(2,1)} custom-call(bf16[16,2,9,16,128]{4,3,2,1,0:T(8,128)(2,1)S(1)} %all-to-all-done.kept_ref, bf16[8,2,9,16,128]{4,3,2,1,0:T(8,128)(2,1)S(1)} %collective-permute-done.4.came_ref), custom_call_target="tpu_custom_call" | custom-call | flops 16000000000 | bytes 160000000 | tf_op jit(solution)/shard_map/assemble/pallas_call | solution.py:118
  35.8 4.4 %collective-permute-start.5 = (bf16[2,2,3,384,128]{4,3,2,1,0:T(8,128)(2,1)}, bf16[2,2,3,384,128]{4,3,2,1,0:T(8,128)(2,1)}, u32[]{:S(2)}, u32[]{:S(2)}) collective-permute-start(bf16[2,2,3,384,128]{4,3,2,1,0:T(8,128)(2,1)} %assemble.5.refs_1_), channel_id=1, source_target_pairs={{0,16},{16,32},{32,48},{48,8},{8,24},{24,40},{40,56},{1,17},{17,33... | collective-permute-start | bytes 3538952 | tf_op jit(solution)/shard_map/ppermute | solution.py:340
  40.2 1.3 %collective-permute-start.6 = (bf16[2,2,3,384,128]{4,3,2,1,0:T(8,128)(2,1)}, bf16[2,2,3,384,128]{4,3,2,1,0:T(8,128)(2,1)}, u32[]{:S(2)}, u32[]{:S(2)}) collective-permute-start(bf16[2,2,3,384,128]{4,3,2,1,0:T(8,128)(2,1)} %assemble.5.refs_1_), channel_id=1, source_target_pairs={{16,0},{32,16},{48,32},{8,48},{24,8},{40,24},{56,40},{17,1},{33,17... | collective-permute-start | bytes 3538952 | tf_op jit(solution)/shard_map/ppermute | solution.py:340
  41.5 13.8 %all-to-all-done.1.kept_ref = bf16[16,9,40,128]{3,2,1,0:T(8,128)(2,1)S(1)} async-done(((bf16[16,9,40,128]{3,2,1,0:T(8,128)(2,1)}), bf16[16,9,40,128]{3,2,1,0:T(8,128)(2,1)S(1)}, u32[]{:S(2)}, u32[]{:S(2)}) %all-to-all-start.1) | async-done | bytes 1474592 | tf_op jit(solution)/shard_map/all_to_all | solution.py:331
  55.3 0.1 collective-permute-start.1
  55.5 0.6 collective-permute-start
  56.0 1.6 %collective-permute-done.came_ref = bf16[8,9,16,128]{3,2,1,0:T(8,128)(2,1)S(1)} collective-permute-done((bf16[8,9,16,128]{3,2,1,0:T(8,128)(2,1)S(1)}, bf16[8,9,16,128]{3,2,1,0:T(8,128)(2,1)S(1)}, u32[]{:S(2)}, u32[]{:S(2)}) %collective-permute-start) | collective-permute-done | bytes 294944 | tf_op jit(solution)/shard_map/ppermute | solution.py:335
  57.6 0.1 assemble.3.refs_2_
  57.7 0.2 assemble.4.refs_0_.refs_1_
  57.9 3.4 %collective-permute-start.2 = (bf16[2,1,3,384,128]{4,3,2,1,0:T(8,128)(2,1)S(1)}, bf16[2,1,3,384,128]{4,3,2,1,0:T(8,128)(2,1)S(1)}, u32[]{:S(2)}, u32[]{:S(2)}) collective-permute-start(bf16[2,1,3,384,128]{4,3,2,1,0:T(8,128)(2,1)S(1)} %assemble.3.refs_2_), channel_id=1, source_target_pairs={{0,16},{16,32},{32,48},{48,8},{8,24},{24,40},{40,56},{1,17},{17,33... | collective-permute-start | bytes 1769480 | tf_op jit(solution)/shard_map/ppermute | solution.py:340
  61.3 1.3 %collective-permute-start.3 = (bf16[2,1,3,384,128]{4,3,2,1,0:T(8,128)(2,1)S(1)}, bf16[2,1,3,384,128]{4,3,2,1,0:T(8,128)(2,1)S(1)}, u32[]{:S(2)}, u32[]{:S(2)}) collective-permute-start(bf16[2,1,3,384,128]{4,3,2,1,0:T(8,128)(2,1)S(1)} %assemble.3.refs_2_), channel_id=1, source_target_pairs={{16,0},{32,16},{48,32},{8,48},{24,8},{40,24},{56,40},{17,1},{33,17... | collective-permute-start | bytes 1769480 | tf_op jit(solution)/shard_map/ppermute | solution.py:340
  62.7 9.0 %attend.3 = (f32[9,128,384]{2,1,0:T(8,128)S(1)}, f32[9,8,384]{2,1,0:T(8,128)S(1)}) custom-call(bf16[1,3,3,384,128]{4,3,2,1,0:T(8,128)(2,1)S(1)} %assemble.4.refs_0_.refs_1_, bf16[2,2,3,384,128]{4,3,2,1,0:T(8,128)(2,1)} %assemble.5.refs_1_, bf16[2,1,3,384,128]{4,3,2,1,0:T(8,128)(2,1)S(1)} %assemble.3.refs_2_), custom_call_target="tpu_custom_call" | custom-call | flops 9000000 | bytes 90000 | tf_op jit(solution)/shard_map/attend/pallas_call | solution.py:310
  71.8 11.1 %attend.4 = (f32[9,128,384]{2,1,0:T(8,128)S(1)}, f32[9,8,384]{2,1,0:T(8,128)S(1)}) custom-call(s32[2]{0:T(128)S(1)} %add_convert_fusion.refs_0_, bf16[1,3,3,384,128]{4,3,2,1,0:T(8,128)(2,1)S(1)} %assemble.4.refs_0_.refs_1_, bf16[2,2,3,384,128]{4,3,2,1,0:T(8,128)(2,1)} %collective-permute-done.5.refs_2_, ...), custom_call_target="tpu_custom_call" | custom-call | flops 10000000 | bytes 100000 | tf_op jit(solution)/shard_map/attend/pallas_call | solution.py:310
  82.9 4.6 %attend.5 = (bf16[8,9,24,128]{3,2,1,0:T(8,128)(2,1)S(1)}, bf16[8,9,24,128]{3,2,1,0:T(8,128)(2,1)S(1)}) custom-call(s32[2]{0:T(128)S(1)} %add_convert_fusion.refs_0_, bf16[1,3,3,384,128]{4,3,2,1,0:T(8,128)(2,1)S(1)} %assemble.4.refs_0_.refs_1_, bf16[2,1,3,384,128]{4,3,2,1,0:T(8,128)(2,1)S(1)} %collective-permute-done.2.refs_2_, ...), custom_call_target="tpu_custom_call" | custom-call | flops 5000000 | bytes 50000 | tf_op jit(solution)/shard_map/attend/pallas_call | solution.py:310
  87.6 2.3 %collective-permute-start.7 = (bf16[8,9,24,128]{3,2,1,0:T(8,128)(2,1)S(1)}, bf16[8,9,24,128]{3,2,1,0:T(8,128)(2,1)S(1)}, u32[]{:S(2)}, u32[]{:S(2)}) collective-permute-start(bf16[8,9,24,128]{3,2,1,0:T(8,128)(2,1)S(1)} %get-tuple-element.24), channel_id=1, source_target_pairs={{0,8},{8,0},{1,9},{9,1},{2,10},{10,2},{3,11},{11,3},{4,12},{12,4},... | collective-permute-start | bytes 1327112 | tf_op jit(solution)/shard_map/ppermute | solution.py:335
  89.8 1.4 %collective-permute-done.7 = bf16[8,9,24,128]{3,2,1,0:T(8,128)(2,1)S(1)} collective-permute-done((bf16[8,9,24,128]{3,2,1,0:T(8,128)(2,1)S(1)}, bf16[8,9,24,128]{3,2,1,0:T(8,128)(2,1)S(1)}, u32[]{:S(2)}, u32[]{:S(2)}) %collective-permute-start.7) | collective-permute-done | bytes 442400 | tf_op jit(solution)/shard_map/ppermute | solution.py:335
  91.3 20.5 %all_to_all.15.x_ref = bf16[16,9,24,128]{3,2,1,0:T(8,128)(2,1)S(1)} all-to-all(bf16[16,9,24,128]{3,2,1,0:T(8,128)(2,1)S(1)} %pad_maximum_fusion), channel_id=1, replica_groups={{0,1,2,3,4,5,6,7,64,65,66,67,68,69,70,71},{72,73,74,75,76,77,78,79,8,9,..., dimensions={0} | all-to-all | bytes 1769472 | tf_op jit(solution)/shard_map/all_to_all | solution.py:331
  111.8 1.0 unpack.1
  (11 shorter events, 0.2 us)
Async XLA Ops:
  2.2 24.9 %all-to-all-start = ((bf16[16,2,9,16,128]{4,3,2,1,0:T(8,128)(2,1)}), bf16[16,2,9,16,128]{4,3,2,1,0:T(8,128)(2,1)S(1)}, u32[]{:S(2)}, u32[]{:S(2)}) async-start(bf16[16,2,9,16,128]{4,3,2,1,0:T(8,128)(2,1)} %pack.3), calls=%async_computation | async-start | bytes 2359296 | tf_op jit(solution)/shard_map/all_to_all | solution.py:331
  28.0 6.6 %collective-permute-start.4 = (bf16[8,2,9,16,128]{4,3,2,1,0:T(8,128)(2,1)}, bf16[8,2,9,16,128]{4,3,2,1,0:T(8,128)(2,1)S(1)}, u32[]{:S(2)}, u32[]{:S(2)}) collective-permute-start(bf16[8,2,9,16,128]{4,3,2,1,0:T(8,128)(2,1)} %slice.11), channel_id=1, source_target_pairs={{0,8},{8,0},{1,9},{9,1},{2,10},{10,2},{3,11},{11,3},{4,12},{12,4},... | collective-permute-start | bytes 1769480 | tf_op jit(solution)/shard_map/ppermute | solution.py:335
  28.0 27.3 %all-to-all-start.1 = ((bf16[16,9,40,128]{3,2,1,0:T(8,128)(2,1)}), bf16[16,9,40,128]{3,2,1,0:T(8,128)(2,1)S(1)}, u32[]{:S(2)}, u32[]{:S(2)}) async-start(bf16[16,9,40,128]{3,2,1,0:T(8,128)(2,1)} %pack.2), calls=%async_computation.1 | async-start | bytes 2949120 | tf_op jit(solution)/shard_map/all_to_all | solution.py:331
  35.8 35.9 %collective-permute-start.5 = (bf16[2,2,3,384,128]{4,3,2,1,0:T(8,128)(2,1)}, bf16[2,2,3,384,128]{4,3,2,1,0:T(8,128)(2,1)}, u32[]{:S(2)}, u32[]{:S(2)}) collective-permute-start(bf16[2,2,3,384,128]{4,3,2,1,0:T(8,128)(2,1)} %assemble.5.refs_1_), channel_id=1, source_target_pairs={{0,16},{16,32},{32,48},{48,8},{8,24},{24,40},{40,56},{1,17},{17,33... | collective-permute-start | bytes 3538952 | tf_op jit(solution)/shard_map/ppermute | solution.py:340
  40.2 31.5 %collective-permute-start.6 = (bf16[2,2,3,384,128]{4,3,2,1,0:T(8,128)(2,1)}, bf16[2,2,3,384,128]{4,3,2,1,0:T(8,128)(2,1)}, u32[]{:S(2)}, u32[]{:S(2)}) collective-permute-start(bf16[2,2,3,384,128]{4,3,2,1,0:T(8,128)(2,1)} %assemble.5.refs_1_), channel_id=1, source_target_pairs={{16,0},{32,16},{48,32},{8,48},{24,8},{40,24},{56,40},{17,1},{33,17... | collective-permute-start | bytes 3538952 | tf_op jit(solution)/shard_map/ppermute | solution.py:340
  55.3 2.4 %collective-permute-start.1 = (bf16[8,9,24,128]{3,2,1,0:T(8,128)(2,1)S(1)}, bf16[8,9,24,128]{3,2,1,0:T(8,128)(2,1)S(1)}, u32[]{:S(2)}, u32[]{:S(2)}) collective-permute-start(bf16[8,9,24,128]{3,2,1,0:T(8,128)(2,1)S(1)} %slice.13), channel_id=1, source_target_pairs={{0,8},{8,0},{1,9},{9,1},{2,10},{10,2},{3,11},{11,3},{4,12},{12,4},... | collective-permute-start | bytes 1327112 | tf_op jit(solution)/shard_map/ppermute | solution.py:335
  55.5 2.2 %collective-permute-start = (bf16[8,9,16,128]{3,2,1,0:T(8,128)(2,1)S(1)}, bf16[8,9,16,128]{3,2,1,0:T(8,128)(2,1)S(1)}, u32[]{:S(2)}, u32[]{:S(2)}) collective-permute-start(bf16[8,9,16,128]{3,2,1,0:T(8,128)(2,1)S(1)} %slice.12), channel_id=1, source_target_pairs={{0,8},{8,0},{1,9},{9,1},{2,10},{10,2},{3,11},{11,3},{4,12},{12,4},... | collective-permute-start | bytes 884744 | tf_op jit(solution)/shard_map/ppermute | solution.py:335
  57.9 25.0 %collective-permute-start.2 = (bf16[2,1,3,384,128]{4,3,2,1,0:T(8,128)(2,1)S(1)}, bf16[2,1,3,384,128]{4,3,2,1,0:T(8,128)(2,1)S(1)}, u32[]{:S(2)}, u32[]{:S(2)}) collective-permute-start(bf16[2,1,3,384,128]{4,3,2,1,0:T(8,128)(2,1)S(1)} %assemble.3.refs_2_), channel_id=1, source_target_pairs={{0,16},{16,32},{32,48},{48,8},{8,24},{24,40},{40,56},{1,17},{17,33... | collective-permute-start | bytes 1769480 | tf_op jit(solution)/shard_map/ppermute | solution.py:340
  61.3 21.6 %collective-permute-start.3 = (bf16[2,1,3,384,128]{4,3,2,1,0:T(8,128)(2,1)S(1)}, bf16[2,1,3,384,128]{4,3,2,1,0:T(8,128)(2,1)S(1)}, u32[]{:S(2)}, u32[]{:S(2)}) collective-permute-start(bf16[2,1,3,384,128]{4,3,2,1,0:T(8,128)(2,1)S(1)} %assemble.3.refs_2_), channel_id=1, source_target_pairs={{16,0},{32,16},{48,32},{8,48},{24,8},{40,24},{56,40},{17,1},{33,17... | collective-permute-start | bytes 1769480 | tf_op jit(solution)/shard_map/ppermute | solution.py:340
  87.6 3.7 %collective-permute-start.7 = (bf16[8,9,24,128]{3,2,1,0:T(8,128)(2,1)S(1)}, bf16[8,9,24,128]{3,2,1,0:T(8,128)(2,1)S(1)}, u32[]{:S(2)}, u32[]{:S(2)}) collective-permute-start(bf16[8,9,24,128]{3,2,1,0:T(8,128)(2,1)S(1)} %get-tuple-element.24), channel_id=1, source_target_pairs={{0,8},{8,0},{1,9},{9,1},{2,10},{10,2},{3,11},{11,3},{4,12},{12,4},... | collective-permute-start | bytes 1327112 | tf_op jit(solution)/shard_map/ppermute | solution.py:335
